TPU v7x, 512 devices: a whole 4x8x8 slice. The times are simulated.
512 devices in a mesh: lat: 16 (over z, core), lon: 32 (over x, y).
Axes of the slice: x: 4, y: 8, z: 8, core: 2. Of those that a mesh axis runs over, the one named last changes fastest.
Arguments:
- rhs: float32 [2, 16, 32, 2048], P(None, 'lat', 'lon'), may hold values from -45 to 45
- cond: float32 [16, 32, 2048], P('lat', 'lon'), may hold values from 0.2 to 5
- blk_diag: float32 [16, 32, 16, 128, 128], P('lat', 'lon'), may hold values from -0.3 to 8, as said below
- blk_off: float32 [16, 32, 15, 128, 128], P('lat', 'lon'), may hold values from -0.3 to 0.3
- iface_idx: int32 [16, 32, 4, 256], P('lat', 'lon'), may hold values from 0 to 2047
- iface_cnt: int32 [16, 32, 4], P('lat', 'lon'), may hold values from 32 to 256, as said below
- iface_coup: float32 [16, 32, 4, 256], P('lat', 'lon'), may hold values from -4 to 4
- edge_nodes: int32 [16, 32, 2, 2048], P('lat', 'lon'), may hold values from 0 to 1279, as said below
Outputs:
- solution: float32 [2, 16, 32, 2048], P(None, 'lat', 'lon')
- residual: float32 [2, 16, 32, 2048], P(None, 'lat', 'lon')
- res_history: float32 [2], replicated
Inputs may be any that keep to these rules, and one draw needn't show every extreme that they name: `blk_diag`: symmetric within each block, diagonal entries 4 to 8, off-diagonal entries of magnitude at most 0.3. `iface_cnt`: some partition has 256 live slots in every direction. `edge_nodes`: heads are always nodes of the partition itself; a tail differs from its edge's head and never names a partition beyond the first or last latitude sector; every node of every partition is the head of some edge.
All inputs are finite; a program needn't handle non-finite values.
Results may differ from a plain program's by a relative error of at most 0.0033.
Values sent between devices are 32-bit elements; how exact they have to be, the bound alone decides.
No kernel may reach another device: no remote copies, remote signals or barrier semaphores. Data moves between devices by JAX's collectives and lax.ppermute only.
A program may use at most 64 MiB of HBM per device.

v0:
```python
import jax
import jax.numpy as jnp
from jax import lax
from jax.sharding import PartitionSpec as P

ITERS = 2
ND = 256


OMEGA = 0.8
HIGH = lax.Precision.HIGHEST


def extended(shard, sides, width, wrap):
    for axis, dim in sides:
        count, length = (lax.axis_size(axis), shard.shape[dim])
        up = [(i, (i + 1) % count) for i in range(count if wrap else count - 1)]
        down = [(j, i) for i, j in up]
        last = lax.slice_in_dim(shard, length - width, length, axis=dim)
        first = lax.slice_in_dim(shard, 0, width, axis=dim)
        before = lax.ppermute(last, axis, up)
        after = lax.ppermute(first, axis, down)
        shard = jnp.concatenate([before, shard, after], axis=dim)
    return shard


def complex_times(left, right):
    return jnp.stack(
        [left[0] * right[0] - left[1] * right[1], left[0] * right[1] + left[1] * right[0]]
    )


def complex_inverse(value):
    scale = value[0] * value[0] + value[1] * value[1]
    return jnp.stack([value[0] / scale, -value[1] / scale])


def local_apply(field, blk_diag, blk_off, cond):
    width = blk_diag.shape[-1]
    blocks = field.shape[1] // width
    shaped = field.reshape(2, blocks, width)
    result = jnp.einsum("bij,cbj->cbi", blk_diag, shaped, precision=HIGH)
    upper = jnp.einsum("bij,cbj->cbi", blk_off, shaped[:, 1:], precision=HIGH)
    lower = jnp.einsum("bji,cbj->cbi", blk_off, shaped[:, :-1], precision=HIGH)
    result = (
        result + jnp.pad(upper, ((0, 0), (0, 1), (0, 0))) + jnp.pad(lower, ((0, 0), (1, 0), (0, 0)))
    )
    result = result.reshape(2, -1)
    return jnp.stack([result[0] - cond * field[1], result[1] + cond * field[0]])


def interface_terms(field, edge_list, coefs):
    sent = field[:, edge_list]
    from_lat = extended(sent[:, 0:2], (("lat", 1),), 1, False)
    from_lon = extended(sent[:, 2:4], (("lon", 1),), 1, True)
    arrived = jnp.stack([from_lat[:, 0], from_lat[:, 3], from_lon[:, 0], from_lon[:, 3]], 1)
    terms = (arrived * coefs[None]).reshape(2, -1)
    return jnp.zeros_like(field).at[:, edge_list.reshape(-1)].add(terms)


def to_owner(ext):
    rows = ext.shape[0]
    lat_part = extended(ext[:, ND : 3 * ND].reshape(rows, 2, ND), (("lat", 1),), 1, False)
    lon_part = extended(ext[:, 3 * ND :].reshape(rows, 2, ND), (("lon", 1),), 1, True)
    return ext[:, :ND] + lat_part[:, 0] + lat_part[:, 3] + lon_part[:, 0] + lon_part[:, 3]


def spread(own):
    lat_part = extended(own[:, None], (("lat", 1),), 1, False)
    lon_part = extended(own[:, None], (("lon", 1),), 1, True)
    return jnp.concatenate([own, lat_part[:, 0], lat_part[:, 2], lon_part[:, 0], lon_part[:, 2]], 1)


def on_device(rhs, cond, blk_diag, blk_off, iface_idx, iface_cnt, iface_coup, edge_nodes):
    right = rhs[:, 0, 0]
    cond = cond[0, 0]
    blk_diag = blk_diag[0, 0]
    blk_off = blk_off[0, 0]
    edge_list = iface_idx[0, 0]
    counts = iface_cnt[0, 0]
    coup = iface_coup[0, 0]
    tails = edge_nodes[0, 0, 0]
    heads = edge_nodes[0, 0, 1]
    slots = lax.broadcasted_iota(jnp.int32, coup.shape, 1)
    coefs = jnp.where(slots < counts[:, None], coup, 0.0)

    def operator(field):
        return local_apply(field, blk_diag, blk_off, cond) + interface_terms(
            field, edge_list, coefs
        )

    def nodal_partial(values, sign):
        ext = jnp.zeros((2, 5 * ND), jnp.float32)
        return ext.at[:, heads].add(values).at[:, tails].add(sign * values)

    edge_diag = jnp.diagonal(blk_diag, axis1=1, axis2=2).reshape(-1)
    edge_value = jnp.stack([edge_diag, cond])
    edge_inv = complex_inverse(edge_value)
    diag_ext = nodal_partial(edge_value, 1.0)
    node_inv = complex_inverse(to_owner(diag_ext))
    solution = jnp.zeros_like(right)
    residual = right
    start = lax.psum(jnp.sum(right * right), ("lat", "lon"))
    history = []
    for step in range(ITERS):
        first = OMEGA * complex_times(edge_inv, residual)
        second = first + OMEGA * complex_times(edge_inv, residual - operator(first))
        remain = nodal_partial(residual - operator(second), -1.0)
        correction = spread(complex_times(node_inv, to_owner(remain)))
        direction = second + correction[:, heads] - correction[:, tails]
        image = operator(direction)
        c_re = jnp.sum(image[0] * residual[0] + image[1] * residual[1])
        c_im = jnp.sum(image[0] * residual[1] - image[1] * residual[0])
        ww = jnp.sum(image * image)
        c_re, c_im, ww = lax.psum((c_re, c_im, ww), ("lat", "lon"))
        alpha = jnp.stack([c_re / ww, c_im / ww])[:, None]
        solution = solution + complex_times(alpha, direction)
        residual = residual - complex_times(alpha, image)
        fresh = lax.psum(jnp.sum(residual * residual), ("lat", "lon"))
        history.append(fresh / start)
    return (solution[:, None, None], residual[:, None, None], jnp.stack(history))


def solution(mesh):
    placed = (
        P(None, "lat", "lon", None),
        P("lat", "lon", None),
        P("lat", "lon", None, None, None),
        P("lat", "lon", None, None, None),
        P("lat", "lon", None, None),
        P("lat", "lon", None),
        P("lat", "lon", None, None),
        P("lat", "lon", None, None),
    )
    return jax.shard_map(
        on_device,
        mesh=mesh,
        in_specs=placed,
        out_specs=(P(None, "lat", "lon", None), P(None, "lat", "lon", None), P()),
        check_vma=False,
    )
```

profile of v0, /device:TPU:1, one launch (start us, length us, event | category | flops | bytes accessed | tf_op | source)
XLA Modules:
  0.0 741.0 jit_solution(9230207026560262623)
XLA Ops:
  27.8 6.7 collective-permute-start.3
  35.9 12.0 %scatter_custom_fusion.1 = f32[2,1280]{0,1:T(8,128)S(1)} fusion(s32[2048]{0:T(1024)S(1)} %bitcast.539, f32[2048,2]{1,0:T(8,128)} %copy.400, f32[]{:T(128)} %constant.7.clone.1), kind=kCustom, calls=%fused_computation.77 | custom fusion | flops 4096 | bytes 10752 | tf_op jit(solution)/shard_map/scatter-add | solution.py:94
  47.9 12.1 %scatter_fusion.1 = f32[2,1280]{0,1:T(8,128)S(1)} fusion(f32[2,1280]{0,1:T(8,128)S(1)} %scatter_custom_fusion.1, s32[2048]{0:T(1024)S(1)} %bitcast.510, f32[2048,2]{1,0:T(8,128)} %copy.400), kind=kCustom, calls=%fused_computation.13 | custom fusion | flops 4096 | bytes 57344 | tf_op jit(solution)/shard_map/scatter-add | solution.py:94
  75.1 7.0 scatter_fusion
  119.8 6.8 scatter_fusion.2
  128.9 12.0 %scatter_custom_fusion.4 = f32[2,1280]{0,1:T(8,128)S(1)} fusion(s32[2048]{0:T(1024)} %bitcast.540, f32[2048,2]{1,0:T(8,128)} %copy.415, f32[]{:T(128)} %constant.7.clone.1), kind=kCustom, calls=%fused_computation.75 | custom fusion | flops 4096 | bytes 10752 | tf_op jit(solution)/shard_map/scatter-add | solution.py:94
  142.3 12.1 %scatter_fusion.3 = f32[2,1280]{0,1:T(8,128)S(1)} fusion(f32[2,1280]{0,1:T(8,128)S(1)} %scatter_custom_fusion.4, s32[2048]{0:T(1024)S(1)} %bitcast.511, f32[2048,2]{1,0:T(8,128)} %copy.416), kind=kCustom, calls=%fused_computation.16 | custom fusion | flops 4096 | bytes 57344 | tf_op jit(solution)/shard_map/scatter-add | solution.py:94
  179.7 7.6 %collective-permute-start.19 = (f32[2,1,256]{2,0,1:T(2,128)S(1)}, f32[2,1,256]{2,0,1:T(2,128)S(1)}, u32[]{:S(2)}, u32[]{:S(2)}) collective-permute-start(f32[2,1,256]{2,0,1:T(2,128)S(1)} %get-tuple-element.112), channel_id=1, source_target_pairs={{1,0},{2,1},{3,2},{4,3},{5,4},{6,5},{7,6},{8,7},{9,8},{10,9},{11,1... | collective-permute-start | bytes 6152 | tf_op jit(solution)/shard_map/ppermute | solution.py:22
  187.9 7.6 %gather_fusion.3 = f32[2048,2]{1,0:T(8,128)} fusion(f32[2,1280]{0,1:T(8,128)S(1)} %copy.424, s32[2048]{0:T(1024)S(1)} %get-tuple-element.115), kind=kCustom, calls=%fused_computation.3 | custom fusion | bytes 40960 | tf_op jit(solution)/shard_map/gather | solution.py:110
  197.1 7.6 %gather_fusion.4 = f32[2048,2]{1,0:T(8,128)} fusion(f32[2,1280]{0,1:T(8,128)S(1)} %copy.424, s32[2048]{0:T(1024)S(1)} %get-tuple-element.114), kind=kCustom, calls=%fused_computation.4 | custom fusion | bytes 40960 | tf_op jit(solution)/shard_map/gather | solution.py:110
  222.9 7.2 collective-permute-start.23
  233.4 6.8 scatter_fusion.4
  246.6 104.4 %all-reduce.14 = (f32[]{:T(128)}, f32[]{:T(128)}, f32[]{:T(128)}) all-reduce(f32[]{:T(128)} %get-tuple-element.6, f32[]{:T(128)} %multiply_reduce_fusion.1, f32[]{:T(128)} %get-tuple-element.5), channel_id=1, replica_groups=mesh['lat'=16,'lon'=32] {'lat','lon'}, use_global_device_ids=true, to_apply=%region_12.13 | all-reduce | flops 3 | bytes 24 | tf_op jit(solution)/shard_map/psum | solution.py:115
  378.3 6.8 scatter_fusion.5
  411.6 6.8 scatter_fusion.6
  420.1 12.2 %scatter_custom_fusion.9 = f32[2,1280]{0,1:T(8,128)S(1)} fusion(s32[2048]{0:T(1024)} %bitcast.542, f32[2048,2]{1,0:T(8,128)} %copy.453, f32[]{:T(128)} %constant.7.clone.1), kind=kCustom, calls=%fused_computation.73 | custom fusion | flops 4096 | bytes 10752 | tf_op jit(solution)/shard_map/scatter-add | solution.py:94
  433.7 12.1 %scatter_fusion.7 = f32[2,1280]{0,1:T(8,128)S(1)} fusion(f32[2,1280]{0,1:T(8,128)S(1)} %scatter_custom_fusion.9, s32[2048]{0:T(1024)S(1)} %bitcast.513, f32[2048,2]{1,0:T(8,128)} %copy.454), kind=kCustom, calls=%fused_computation.21 | custom fusion | flops 4096 | bytes 57344 | tf_op jit(solution)/shard_map/scatter-add | solution.py:94
  454.2 6.7 collective-permute-start.35
  470.3 7.2 collective-permute-start.39
  478.6 7.6 %gather_fusion.8 = f32[2048,2]{1,0:T(8,128)} fusion(f32[2,1280]{0,1:T(8,128)S(1)} %copy.462, s32[2048]{0:T(1024)S(1)} %get-tuple-element.115), kind=kCustom, calls=%fused_computation.8 | custom fusion | bytes 40960 | tf_op jit(solution)/shard_map/gather | solution.py:110
  486.2 7.6 %gather_fusion.9 = f32[2048,2]{1,0:T(8,128)} fusion(f32[2,1280]{0,1:T(8,128)S(1)} %copy.462, s32[2048]{0:T(1024)S(1)} %get-tuple-element.114), kind=kCustom, calls=%fused_computation.9 | custom fusion | bytes 40960 | tf_op jit(solution)/shard_map/gather | solution.py:110
  513.5 7.2 collective-permute-start.43
  534.5 103.6 %all-reduce.13 = (f32[]{:T(128)}, f32[]{:T(128)}, f32[]{:T(128)}) all-reduce(f32[]{:T(128)} %get-tuple-element.4, f32[]{:T(128)} %multiply_reduce_fusion, f32[]{:T(128)} %get-tuple-element.3), channel_id=1, replica_groups=mesh['lat'=16,'lon'=32] {'lat','lon'}, use_global_device_ids=true, to_apply=%region_23.24 | all-reduce | flops 3 | bytes 24 | tf_op jit(solution)/shard_map/psum | solution.py:115
  641.5 94.6 %all-reduce.12 = (f32[]{:T(128)}, f32[]{:T(128)}, f32[]{:T(128)}) all-reduce(f32[]{:T(128)} %get-tuple-element.8, f32[]{:T(128)} %get-tuple-element.71, f32[]{:T(128)} %get-tuple-element.7), channel_id=1, replica_groups=mesh['lat'=16,'lon'=32] {'lat','lon'}, use_global_device_ids=true, to_apply=%region_29.30 | all-reduce | flops 3 | bytes 24 | tf_op jit(solution)/shard_map/psum | solution.py:119
  (321 shorter events, 247.9 us)
Async XLA Ops:
  15.2 58.0 %collective-permute-start = (f32[2,1,256]{2,1,0:T(1,128)}, f32[2,1,256]{2,1,0:T(1,128)}, u32[]{:S(2)}, u32[]{:S(2)}) collective-permute-start(f32[2,1,256]{2,1,0:T(1,128)} %get-tuple-element.104), channel_id=1, source_target_pairs={{0,32},{32,64},{64,96},{96,128},{128,160},{160,192},{192,224},{224... | collective-permute-start | bytes 6152 | tf_op jit(solution)/shard_map/ppermute | solution.py:21
  20.6 52.6 %collective-permute-start.1 = (f32[2,1,256]{2,1,0:T(1,128)}, f32[2,1,256]{2,1,0:T(1,128)}, u32[]{:S(2)}, u32[]{:S(2)}) collective-permute-start(f32[2,1,256]{2,1,0:T(1,128)} %get-tuple-element.106), channel_id=1, source_target_pairs={{32,0},{64,32},{96,64},{128,96},{160,128},{192,160},{224,192},{256... | collective-permute-start | bytes 6152 | tf_op jit(solution)/shard_map/ppermute | solution.py:22
  25.9 47.4 %collective-permute-start.2 = (f32[2,1,256]{2,1,0:T(1,128)}, f32[2,1,256]{2,1,0:T(1,128)}, u32[]{:S(2)}, u32[]{:S(2)}) collective-permute-start(f32[2,1,256]{2,1,0:T(1,128)} %get-tuple-element.105), channel_id=1, source_target_pairs={{0,1},{1,2},{2,3},{3,4},{4,5},{5,6},{6,7},{7,8},{8,9},{9,10},{10,1... | collective-permute-start | bytes 6152 | tf_op jit(solution)/shard_map/ppermute | solution.py:21
  27.8 45.5 %collective-permute-start.3 = (f32[2,1,256]{2,1,0:T(1,128)}, f32[2,1,256]{2,1,0:T(1,128)}, u32[]{:S(2)}, u32[]{:S(2)}) collective-permute-start(f32[2,1,256]{2,1,0:T(1,128)} %get-tuple-element.107), channel_id=1, source_target_pairs={{1,0},{2,1},{3,2},{4,3},{5,4},{6,5},{7,6},{8,7},{9,8},{10,9},{11,1... | collective-permute-start | bytes 6152 | tf_op jit(solution)/shard_map/ppermute | solution.py:22
  60.8 98.2 %collective-permute-start.4 = (f32[2,1,256]{2,0,1:T(2,128)}, f32[2,1,256]{2,0,1:T(2,128)}, u32[]{:S(2)}, u32[]{:S(2)}) collective-permute-start(f32[2,1,256]{2,0,1:T(2,128)} %copy.501), channel_id=1, source_target_pairs={{0,32},{32,64},{64,96},{96,128},{128,160},{160,192},{192,224},{224... | collective-permute-start | bytes 6152 | tf_op jit(solution)/shard_map/ppermute | solution.py:21
  91.8 15.6 %collective-permute-start.10 = (f32[2,1,256]{2,1,0:T(1,128)S(1)}, f32[2,1,256]{2,1,0:T(1,128)S(1)}, u32[]{:S(2)}, u32[]{:S(2)}) collective-permute-start(f32[2,1,256]{2,1,0:T(1,128)S(1)} %get-tuple-element.101), channel_id=1, source_target_pairs={{0,1},{1,2},{2,3},{3,4},{4,5},{5,6},{6,7},{7,8},{8,9},{9,10},{10,1... | collective-permute-start | bytes 6152 | tf_op jit(solution)/shard_map/ppermute | solution.py:21
  93.7 15.6 %collective-permute-start.11 = (f32[2,1,256]{2,1,0:T(1,128)S(1)}, f32[2,1,256]{2,1,0:T(1,128)S(1)}, u32[]{:S(2)}, u32[]{:S(2)}) collective-permute-start(f32[2,1,256]{2,1,0:T(1,128)S(1)} %get-tuple-element.103), channel_id=1, source_target_pairs={{1,0},{2,1},{3,2},{4,3},{5,4},{6,5},{7,6},{8,7},{9,8},{10,9},{11,1... | collective-permute-start | bytes 6152 | tf_op jit(solution)/shard_map/ppermute | solution.py:22
  102.7 15.4 %collective-permute-start.9 = (f32[2,1,256]{2,1,0:T(1,128)S(1)}, f32[2,1,256]{2,1,0:T(1,128)S(1)}, u32[]{:S(2)}, u32[]{:S(2)}) collective-permute-start(f32[2,1,256]{2,1,0:T(1,128)S(1)} %get-tuple-element.102), channel_id=1, source_target_pairs={{32,0},{64,32},{96,64},{128,96},{160,128},{192,160},{224,192},{256... | collective-permute-start | bytes 6152 | tf_op jit(solution)/shard_map/ppermute | solution.py:22
  107.5 53.5 %collective-permute-start.5 = (f32[2,1,256]{2,0,1:T(2,128)}, f32[2,1,256]{2,0,1:T(2,128)S(1)}, u32[]{:S(2)}, u32[]{:S(2)}) collective-permute-start(f32[2,1,256]{2,0,1:T(2,128)} %copy.502), channel_id=1, source_target_pairs={{32,0},{64,32},{96,64},{128,96},{160,128},{192,160},{224,192},{256... | collective-permute-start | bytes 6152 | tf_op jit(solution)/shard_map/ppermute | solution.py:22
  109.4 53.5 %collective-permute-start.6 = (f32[2,1,256]{2,0,1:T(2,128)}, f32[2,1,256]{2,0,1:T(2,128)S(1)}, u32[]{:S(2)}, u32[]{:S(2)}) collective-permute-start(f32[2,1,256]{2,0,1:T(2,128)} %copy.503), channel_id=1, source_target_pairs={{0,1},{1,2},{2,3},{3,4},{4,5},{5,6},{6,7},{7,8},{8,9},{9,10},{10,1... | collective-permute-start | bytes 6152 | tf_op jit(solution)/shard_map/ppermute | solution.py:21
  111.3 58.2 %collective-permute-start.7 = (f32[2,1,256]{2,0,1:T(2,128)}, f32[2,1,256]{2,0,1:T(2,128)S(1)}, u32[]{:S(2)}, u32[]{:S(2)}) collective-permute-start(f32[2,1,256]{2,0,1:T(2,128)} %copy.504), channel_id=1, source_target_pairs={{1,0},{2,1},{3,2},{4,3},{5,4},{6,5},{7,6},{8,7},{9,8},{10,9},{11,1... | collective-permute-start | bytes 6152 | tf_op jit(solution)/shard_map/ppermute | solution.py:22
  154.5 15.9 %collective-permute-start.12 = (f32[2,1,256]{2,0,1:T(2,128)S(1)}, f32[2,1,256]{2,0,1:T(2,128)S(1)}, u32[]{:S(2)}, u32[]{:S(2)}) collective-permute-start(f32[2,1,256]{2,0,1:T(2,128)S(1)} %copy.506), channel_id=1, source_target_pairs={{0,32},{32,64},{64,96},{96,128},{128,160},{160,192},{192,224},{224... | collective-permute-start | bytes 6152 | tf_op jit(solution)/shard_map/ppermute | solution.py:21
  170.5 16.8 %collective-permute-start.16 = (f32[2,1,256]{2,0,1:T(2,128)S(1)}, f32[2,1,256]{2,0,1:T(2,128)S(1)}, u32[]{:S(2)}, u32[]{:S(2)}) collective-permute-start(f32[2,1,256]{2,0,1:T(2,128)S(1)} %get-tuple-element.112), channel_id=1, source_target_pairs={{0,32},{32,64},{64,96},{96,128},{128,160},{160,192},{192,224},{224... | collective-permute-start | bytes 6152 | tf_op jit(solution)/shard_map/ppermute | solution.py:21
  175.8 11.5 %collective-permute-start.17 = (f32[2,1,256]{2,0,1:T(2,128)S(1)}, f32[2,1,256]{2,0,1:T(2,128)S(1)}, u32[]{:S(2)}, u32[]{:S(2)}) collective-permute-start(f32[2,1,256]{2,0,1:T(2,128)S(1)} %get-tuple-element.112), channel_id=1, source_target_pairs={{32,0},{64,32},{96,64},{128,96},{160,128},{192,160},{224,192},{256... | collective-permute-start | bytes 6152 | tf_op jit(solution)/shard_map/ppermute | solution.py:22
  214.5 17.8 %collective-permute-start.20 = (f32[2,1,256]{2,1,0:T(1,128)S(1)}, f32[2,1,256]{2,1,0:T(1,128)S(1)}, u32[]{:S(2)}, u32[]{:S(2)}) collective-permute-start(f32[2,1,256]{2,1,0:T(1,128)S(1)} %get-tuple-element.96), channel_id=1, source_target_pairs={{0,32},{32,64},{64,96},{96,128},{128,160},{160,192},{192,224},{224... | collective-permute-start | bytes 6152 | tf_op jit(solution)/shard_map/ppermute | solution.py:21
  219.0 13.3 %collective-permute-start.21 = (f32[2,1,256]{2,1,0:T(1,128)S(1)}, f32[2,1,256]{2,1,0:T(1,128)S(1)}, u32[]{:S(2)}, u32[]{:S(2)}) collective-permute-start(f32[2,1,256]{2,1,0:T(1,128)S(1)} %get-tuple-element.98), channel_id=1, source_target_pairs={{32,0},{64,32},{96,64},{128,96},{160,128},{192,160},{224,192},{256... | collective-permute-start | bytes 6152 | tf_op jit(solution)/shard_map/ppermute | solution.py:22
  361.8 15.3 %collective-permute-start.24 = (f32[2,1,256]{2,1,0:T(1,128)S(1)}, f32[2,1,256]{2,1,0:T(1,128)S(1)}, u32[]{:S(2)}, u32[]{:S(2)}) collective-permute-start(f32[2,1,256]{2,1,0:T(1,128)S(1)} %get-tuple-element.92), channel_id=1, source_target_pairs={{0,32},{32,64},{64,96},{96,128},{128,160},{160,192},{192,224},{224... | collective-permute-start | bytes 6152 | tf_op jit(solution)/shard_map/ppermute | solution.py:21
  364.0 13.1 %collective-permute-start.25 = (f32[2,1,256]{2,1,0:T(1,128)S(1)}, f32[2,1,256]{2,1,0:T(1,128)S(1)}, u32[]{:S(2)}, u32[]{:S(2)}) collective-permute-start(f32[2,1,256]{2,1,0:T(1,128)S(1)} %get-tuple-element.94), channel_id=1, source_target_pairs={{32,0},{64,32},{96,64},{128,96},{160,128},{192,160},{224,192},{256... | collective-permute-start | bytes 6152 | tf_op jit(solution)/shard_map/ppermute | solution.py:22
  393.7 16.7 %collective-permute-start.28 = (f32[2,1,256]{2,1,0:T(1,128)S(1)}, f32[2,1,256]{2,1,0:T(1,128)S(1)}, u32[]{:S(2)}, u32[]{:S(2)}) collective-permute-start(f32[2,1,256]{2,1,0:T(1,128)S(1)} %get-tuple-element.88), channel_id=1, source_target_pairs={{0,32},{32,64},{64,96},{96,128},{128,160},{160,192},{192,224},{224... | collective-permute-start | bytes 6152 | tf_op jit(solution)/shard_map/ppermute | solution.py:21
  397.7 12.7 %collective-permute-start.29 = (f32[2,1,256]{2,1,0:T(1,128)S(1)}, f32[2,1,256]{2,1,0:T(1,128)S(1)}, u32[]{:S(2)}, u32[]{:S(2)}) collective-permute-start(f32[2,1,256]{2,1,0:T(1,128)S(1)} %get-tuple-element.90), channel_id=1, source_target_pairs={{32,0},{64,32},{96,64},{128,96},{160,128},{192,160},{224,192},{256... | collective-permute-start | bytes 6152 | tf_op jit(solution)/shard_map/ppermute | solution.py:22
  445.9 15.1 %collective-permute-start.32 = (f32[2,1,256]{2,0,1:T(2,128)S(1)}, f32[2,1,256]{2,0,1:T(2,128)S(1)}, u32[]{:S(2)}, u32[]{:S(2)}) collective-permute-start(f32[2,1,256]{2,0,1:T(2,128)S(1)} %copy.513), channel_id=1, source_target_pairs={{0,32},{32,64},{64,96},{96,128},{128,160},{160,192},{192,224},{224... | collective-permute-start | bytes 6152 | tf_op jit(solution)/shard_map/ppermute | solution.py:21
  461.7 15.9 %collective-permute-start.36 = (f32[2,1,256]{2,0,1:T(2,128)S(1)}, f32[2,1,256]{2,0,1:T(2,128)S(1)}, u32[]{:S(2)}, u32[]{:S(2)}) collective-permute-start(f32[2,1,256]{2,0,1:T(2,128)S(1)} %get-tuple-element.110), channel_id=1, source_target_pairs={{0,32},{32,64},{64,96},{96,128},{128,160},{160,192},{192,224},{224... | collective-permute-start | bytes 6152 | tf_op jit(solution)/shard_map/ppermute | solution.py:21
  505.2 17.8 %collective-permute-start.40 = (f32[2,1,256]{2,1,0:T(1,128)S(1)}, f32[2,1,256]{2,1,0:T(1,128)S(1)}, u32[]{:S(2)}, u32[]{:S(2)}) collective-permute-start(f32[2,1,256]{2,1,0:T(1,128)S(1)} %get-tuple-element.84), channel_id=1, source_target_pairs={{0,32},{32,64},{64,96},{96,128},{128,160},{160,192},{192,224},{224... | collective-permute-start | bytes 6152 | tf_op jit(solution)/shard_map/ppermute | solution.py:21
  509.7 13.3 %collective-permute-start.41 = (f32[2,1,256]{2,1,0:T(1,128)S(1)}, f32[2,1,256]{2,1,0:T(1,128)S(1)}, u32[]{:S(2)}, u32[]{:S(2)}) collective-permute-start(f32[2,1,256]{2,1,0:T(1,128)S(1)} %get-tuple-element.86), channel_id=1, source_target_pairs={{32,0},{64,32},{96,64},{128,96},{160,128},{192,160},{224,192},{256... | collective-permute-start | bytes 6152 | tf_op jit(solution)/shard_map/ppermute | solution.py:22
  (41 other events, 1374.4 us)
where the time goes:
time: 752 us; the launch traced here: 741 us
  blocking collectives  303 us (40%)
  starting transfers between devices  165 us (22%)
  other arithmetic  125 us (17%)
  local copies, waits for them, and re-layouts  111 us (15%)
  matrix products  25.7 us (3%)
  between operations  10.6 us (1%)
    psum x2, blocking collectives, on_device(): c_re, c_im, ww = lax.psum((c_re, c_im, ww), ('lat', 'lon'))  208 us
    ppermute x22, starting transfers between devices, extended(): after = lax.ppermute(first, axis, down)  100 us
    psum x1, blocking collectives, on_device(): fresh = lax.psum(jnp.sum(residual * residual), ('lat', 'lon'))  94.6 us
    scatter-add x6, other arithmetic, nodal_partial(): return ext.at[:, heads].add(values).at[:, tails].add(sign * values)  72.4 us
    ppermute x22, starting transfers between devices, extended(): before = lax.ppermute(last, axis, up)  65.2 us
    scatter-add x6, other arithmetic, interface_terms(): return jnp.zeros_like(field).at[:, edge_list.reshape(-1)].add(terms)  40.7 us
    gather x8, local copies, waits for them, and re-layouts, on_device(): direction = second + correction[:, heads] - correction[:, tails]  36.6 us
    gather x12, local copies, waits for them, and re-layouts, interface_terms(): sent = field[:, edge_list]  31.8 us
  transfers between devices with their start and end apart: 44, of which 3 were waited for; matrix products, arithmetic and copies ran while one was open for 14% of the time, Pallas kernels for 0%

commit v1 on v0

v1 whole, which is shorter than its diff:
```python
import jax
import jax.numpy as jnp
from jax import lax
from jax.experimental import pallas as pl
from jax.experimental.pallas import tpu as pltpu
from jax.sharding import PartitionSpec as P

ITERS = 2
EB = 16
BS = 128
E = EB * BS
ND = 256
IFC = 256
OMEGA = 0.8
F32 = jnp.float32
BF16 = jnp.bfloat16
LIMIT = 20 * 1024 * 1024
NT = (((1,), (1,)), ((), ()))


def complex_times(a, b):
    return a[0] * b[0] - a[1] * b[1], a[0] * b[1] + a[1] * b[0]


def complex_inverse(a):
    scale = a[0] * a[0] + a[1] * a[1]
    return a[0] / scale, -a[1] / scale


def pieces(x):
    first = x.astype(BF16).astype(F32)
    rest = x - first
    second = rest.astype(BF16).astype(F32)
    return first, second, rest - second


def lanes(x, count):
    return jnp.concatenate([x[k : k + 1] for k in range(count)], axis=1)


def to_blocks(row, ref):
    for k in range(EB):
        ref[k : k + 1] = row[:, k * BS : (k + 1) * BS]
    return ref[...]


def block_mask(blocks, rows):
    return lax.broadcasted_iota(jnp.int32, (rows, blocks.shape[1]), 0) == blocks


def lane_onehot(index):
    spot = lax.broadcasted_iota(jnp.int32, (BS, index.shape[1]), 0)
    return jnp.where(spot == index % BS, 1.0, 0.0).astype(BF16)


def take(field, onehot, mask):
    parts = [pieces(part) for part in field]
    stack = jnp.concatenate([parts[c][p] for p in range(3) for c in range(2)], axis=0)
    got = jnp.dot(stack.astype(BF16), onehot[...], preferred_element_type=F32)
    got = got[:32] + got[32:64] + got[64:]
    return [
        jnp.sum(jnp.where(mask, got[16 * c : 16 * c + 16], 0.0), axis=0, keepdims=True)
        for c in range(2)
    ]


def put(rows, onehot, mask):
    parts = [pieces(part) for part in rows]
    stack = jnp.concatenate(
        [jnp.where(mask, parts[c][p], 0.0) for p in range(3) for c in range(2)], axis=0
    )
    got = lax.dot_general(stack.astype(BF16), onehot[...], NT, preferred_element_type=F32)
    got = got[:32] + got[32:64] + got[64:]
    return got[:16], got[16:]


def put_heads(rows, onehot, block):
    spot = lax.broadcasted_iota(jnp.int32, (8, block.shape[1]), 0)
    right = [pieces(part) for part in rows]
    match = (spot % 2 == block) & (spot < 4)
    stack = jnp.concatenate(
        [
            jnp.where(match, jnp.where(spot < 2, right[0][p], right[1][p]), 0.0)
            for p in range(3)
        ],
        axis=0,
    )
    got = lax.dot_general(stack.astype(BF16), onehot[...], NT, preferred_element_type=F32)
    return got[:8] + got[8:16] + got[16:]


def take_heads(own, onehot, block):
    stack = jnp.concatenate(pieces(own), axis=0)
    got = jnp.dot(stack.astype(BF16), onehot[...], preferred_element_type=F32)
    got = got[:8] + got[8:16] + got[16:]
    low = block == 0
    return [jnp.where(low, got[2 * c : 2 * c + 1], got[2 * c + 1 : 2 * c + 2]) for c in range(2)]


def parities():
    return lax.axis_index("lat") % 2 == 0, lax.axis_index("lon") % 2 == 0


def hand_out(refs, towards, at=0):
    even_lat, even_lon = parities()
    refs[0][at : at + 4] = jnp.where(even_lat, towards[1], towards[0])
    refs[1][at : at + 4] = jnp.where(even_lat, towards[0], towards[1])
    refs[2][at : at + 4] = jnp.where(even_lon, towards[3], towards[2])
    refs[3][at : at + 4] = jnp.where(even_lon, towards[2], towards[3])


def collect(refs, at=0):
    even_lat, even_lon = parities()
    core, far, near, wide = [ref[at : at + 4] for ref in refs]
    return (
        jnp.where(even_lat, far, core),
        jnp.where(even_lat, core, far),
        jnp.where(even_lon, wide, near),
        jnp.where(even_lon, near, wide),
    )


def index_rows(idx_ref):
    idx = idx_ref[0, 0]
    return jnp.concatenate([idx[d : d + 1] for d in range(4)], axis=1)


def interface_messages(field, onehot, index):
    got = take(field, onehot, block_mask(index // BS, EB))
    return [
        jnp.concatenate(
            [
                got[c][:, d * IFC + h * BS : d * IFC + (h + 1) * BS]
                for c in range(2)
                for h in range(2)
            ],
            axis=0,
        )
        for d in range(4)
    ]


def interface_sum(arrived, coefs, onehot, index):
    rows = [
        jnp.concatenate(
            [arrived[d][2 * c + h : 2 * c + h + 1] for d in range(4) for h in range(2)], axis=1
        )
        * coefs
        for c in range(2)
    ]
    return put(rows, onehot, block_mask(index // BS, EB))


def pair(ref):
    return ref[0:EB], ref[EB : 2 * EB]


def keep(ref, value):
    ref[0:EB] = value[0]
    ref[EB : 2 * EB] = value[1]


def nodal(rows, onehot_head, onehot_tail, nodes_ref, sign, out_refs, own_ref, at):
    tails = nodes_ref[0, 0, 0:1]
    heads = nodes_ref[0, 0, 1:2]
    own = put_heads(rows, onehot_head, heads // BS)
    ext = put(rows, onehot_tail, block_mask(tails // BS, EB))
    ext = [sign * ext[0], sign * ext[1]]
    own_ref[...] = own
    for c in range(2):
        own_ref[2 * c : 2 * c + 2] += ext[c][0:2]
    towards = [
        jnp.concatenate([ext[0][2 * d : 2 * d + 2], ext[1][2 * d : 2 * d + 2]], axis=0)
        for d in range(1, 5)
    ]
    hand_out(out_refs, towards, at)


def begin_kernel(
    rhs_ref, cond_ref, diag_ref, idx_ref, cnt_ref, coup_ref, nodes_ref,
    m0, m1, m2, m3, ohi_ref, oht_ref, ohh_ref, coef_ref, value_ref, scale_ref, right_ref, first_ref, own_ref,
    blocks,
):
    messages = (m0, m1, m2, m3)
    index = index_rows(idx_ref)
    ohi_ref[...] = lane_onehot(index)
    oht_ref[...] = lane_onehot(nodes_ref[0, 0, 0:1])
    ohh_ref[...] = lane_onehot(nodes_ref[0, 0, 1:2])
    slot = lax.broadcasted_iota(jnp.int32, (1, IFC), 1)
    coef_ref[...] = jnp.concatenate(
        [jnp.where(slot < cnt_ref[0, 0, d], coup_ref[0, 0, d : d + 1], 0.0) for d in range(4)], axis=1
    )
    eye = lax.broadcasted_iota(jnp.int32, (BS, BS), 0) == lax.broadcasted_iota(jnp.int32, (BS, BS), 1)
    for b in range(EB):
        value_ref[b : b + 1] = jnp.sum(jnp.where(eye, diag_ref[0, 0, b], 0.0), axis=0, keepdims=True)
    value_ref[EB : 2 * EB] = to_blocks(cond_ref[0], blocks)
    value = pair(value_ref)
    inverse = complex_inverse(value)
    scale = (OMEGA * inverse[0], OMEGA * inverse[1])
    keep(scale_ref, scale)
    for c in range(2):
        right_ref[EB * c : EB * c + EB] = to_blocks(rhs_ref[c, 0], blocks)
    first = complex_times(scale, pair(right_ref))
    keep(first_ref, first)
    hand_out(messages, interface_messages(first, ohi_ref, index), 0)
    rows = [lanes(value[c], EB) for c in range(2)]
    nodal(rows, ohh_ref, oht_ref, nodes_ref, 1.0, messages, own_ref, 4)


def weight_kernel(diag_ref, off_ref, w_ref):
    eye = lax.broadcasted_iota(jnp.int32, (BS, BS), 0) == lax.broadcasted_iota(jnp.int32, (BS, BS), 1)

    def store(b, at, block):
        high = block.astype(BF16)
        w_ref[b, at : at + BS, 0:BS] = high
        w_ref[b, at : at + BS, BS:] = (block - high.astype(F32)).astype(BF16)

    zero = jnp.zeros((BS, 2 * BS), BF16)
    w_ref[0, 0:BS] = zero
    w_ref[EB - 1, 2 * BS :] = zero
    for b in range(EB):
        store(b, BS, jnp.where(eye, 0.0, diag_ref[0, 0, b]))
        if b < EB - 1:
            off = off_ref[0, 0, b]
            store(b + 1, 0, off)
            store(b, 2 * BS, off.T)


def stiffness(field, value, w_ref, wide, out):
    wide[0:8] = jnp.zeros((8, BS), F32)
    wide[8 * (EB + 1) :] = jnp.zeros((8, BS), F32)
    for c in range(2):
        for p, piece in enumerate(pieces(field[c])):
            wide[pl.ds(8 + 2 * p + c, EB, stride=8)] = piece
    for k in (6, 7):
        wide[pl.ds(8 + k, EB, stride=8)] = jnp.zeros((EB, BS), F32)
    for b in range(EB):
        around = jnp.concatenate([wide[8 * (b + k) : 8 * (b + k) + 8] for k in range(3)], axis=1)
        got = jnp.dot(around.astype(BF16), w_ref[b], preferred_element_type=F32)
        out[8 * b : 8 * b + 8] = got[:, :BS] + got[:, BS:]
    sums = [
        out[pl.ds(c, EB, stride=8)] + out[pl.ds(2 + c, EB, stride=8)] + out[pl.ds(4 + c, EB, stride=8)]
        for c in range(2)
    ]
    turned = complex_times(value, field)
    return sums[0] + turned[0], sums[1] + turned[1]


def local_kernel(field_ref, value_ref, w_ref, out_ref, wide, out):
    keep(out_ref, stiffness(pair(field_ref), pair(value_ref), w_ref, wide, out))


def smooth(arrived, ohi_ref, coef_ref, idx_ref, first_ref, local_ref, scale_ref, right_ref, m, second_ref):
    index = index_rows(idx_ref)
    extra = interface_sum(arrived, coef_ref[...], ohi_ref, index)
    first, local, right = pair(first_ref), pair(local_ref), pair(right_ref)
    change = complex_times(pair(scale_ref), [right[c] - local[c] - extra[c] for c in range(2)])
    second = (first[0] + change[0], first[1] + change[1])
    keep(second_ref, second)
    hand_out(m, interface_messages(second, ohi_ref, index))


def smooth_first_kernel(
    a0, a1, a2, a3, own_ref, ohi_ref, coef_ref, idx_ref, first_ref, local_ref, scale_ref, right_ref,
    m0, m1, m2, m3, second_ref, ninv_ref,
):
    arrived = collect((a0, a1, a2, a3))
    smooth(arrived, ohi_ref, coef_ref, idx_ref, first_ref, local_ref, scale_ref, right_ref, (m0, m1, m2, m3), second_ref)
    sums = own_ref[0:4]
    for part in collect((a0, a1, a2, a3), 4):
        sums = sums + part
    inverse = complex_inverse((sums[0:2], sums[2:4]))
    ninv_ref[0:2] = inverse[0]
    ninv_ref[2:4] = inverse[1]


def smooth_kernel(
    a0, a1, a2, a3, ohi_ref, coef_ref, idx_ref, first_ref, local_ref, scale_ref, right_ref,
    m0, m1, m2, m3, second_ref,
):
    arrived = collect((a0, a1, a2, a3))
    smooth(arrived, ohi_ref, coef_ref, idx_ref, first_ref, local_ref, scale_ref, right_ref, (m0, m1, m2, m3), second_ref)


def restrict_kernel(
    a0, a1, a2, a3, ohi_ref, oht_ref, ohh_ref, coef_ref, idx_ref, nodes_ref, local_ref, right_ref,
    m0, m1, m2, m3, own_ref,
):
    index = index_rows(idx_ref)
    extra = interface_sum(collect((a0, a1, a2, a3)), coef_ref[...], ohi_ref, index)
    local, right = pair(local_ref), pair(right_ref)
    rows = [lanes(right[c] - local[c] - extra[c], EB) for c in range(2)]
    nodal(rows, ohh_ref, oht_ref, nodes_ref, -1.0, (m0, m1, m2, m3), own_ref, 0)


def node_kernel(a0, a1, a2, a3, own_ref, ninv_ref, y_ref):
    sums = own_ref[0:4]
    for part in collect((a0, a1, a2, a3)):
        sums = sums + part
    result = complex_times((ninv_ref[0:2], ninv_ref[2:4]), (sums[0:2], sums[2:4]))
    y_ref[0:2] = result[0]
    y_ref[2:4] = result[1]


def prolong_kernel(
    a0, a1, a2, a3, y_ref, ohi_ref, oht_ref, ohh_ref, idx_ref, nodes_ref, second_ref,
    m0, m1, m2, m3, direction_ref,
    blocks, wide,
):
    tails = nodes_ref[0, 0, 0:1]
    heads = nodes_ref[0, 0, 1:2]
    wide[...] = jnp.zeros((2 * EB, BS), F32)
    nodes = (y_ref[...],) + collect((a0, a1, a2, a3))
    for d in range(5):
        for c in range(2):
            wide[EB * c + 2 * d : EB * c + 2 * d + 2] = nodes[d][2 * c : 2 * c + 2]
    low = take(pair(wide), oht_ref, block_mask(tails // BS, EB))
    own = jnp.concatenate([nodes[0], nodes[0]], axis=0)
    high = take_heads(own, ohh_ref, heads // BS)
    second = pair(second_ref)
    direction = [second[c] + to_blocks(high[c] - low[c], blocks) for c in range(2)]
    keep(direction_ref, direction)
    hand_out((m0, m1, m2, m3), interface_messages(direction, ohi_ref, index_rows(idx_ref)))


def image_kernel(
    a0, a1, a2, a3, ohi_ref, coef_ref, idx_ref, local_ref, scale_ref,
    m0, m1, m2, m3, image_ref, first_ref,
):
    index = index_rows(idx_ref)
    extra = interface_sum(collect((a0, a1, a2, a3)), coef_ref[...], ohi_ref, index)
    local = pair(local_ref)
    image = (local[0] + extra[0], local[1] + extra[1])
    keep(image_ref, image)
    first = complex_times(pair(scale_ref), image)
    keep(first_ref, first)
    hand_out((m0, m1, m2, m3), interface_messages(first, ohi_ref, index))


def total(x):
    return jnp.sum(jnp.sum(x, axis=0, keepdims=True), axis=1, keepdims=True)


def inner(a, b):
    return total(a[0] * b[0] + a[1] * b[1]), total(a[0] * b[1] - a[1] * b[0])


def sums_kernel(
    a0, a1, a2, a3, ohi_ref, coef_ref, idx_ref, local_ref, right_ref, image_ref,
    image2_ref, sums_ref,
):
    index = index_rows(idx_ref)
    extra = interface_sum(collect((a0, a1, a2, a3)), coef_ref[...], ohi_ref, index)
    local, right, image = pair(local_ref), pair(right_ref), pair(image_ref)
    image2 = (local[0] + extra[0], local[1] + extra[1])
    keep(image2_ref, image2)
    rest = (right[0] - image[0], right[1] - image[1])
    turn = (image[0] - image2[0], image[1] - image2[1])
    found = [inner(right, right)[0], inner(image, image)[0], inner(rest, rest)[0], inner(turn, turn)[0]]
    found += [*inner(image, rest), *inner(turn, rest), *inner(turn, image)]
    lane = lax.broadcasted_iota(jnp.int32, (1, BS), 1)
    row = jnp.zeros((1, BS), F32)
    for k, value in enumerate(found):
        row = jnp.where(lane == k, value, row)
    sums_ref[...] = jnp.broadcast_to(row[None], sums_ref.shape)


def finish_kernel(
    sums_ref, right_ref, image_ref, image2_ref, direction_ref, direction2_ref,
    solution_ref, residual_ref, history_ref,
):
    row = jnp.sum(sums_ref[...], axis=0)
    lane = lax.broadcasted_iota(jnp.int32, (1, BS), 1)
    found = [jnp.sum(jnp.where(lane == k, row, 0.0), axis=1, keepdims=True) for k in range(10)]
    start, ww, rr, tt = found[:4]
    wr, tr, tw = found[4:6], found[6:8], found[8:10]
    extra = (wr[0] / ww, wr[1] / ww)
    alpha = (1.0 + extra[0], extra[1])
    fresh = rr - (wr[0] * extra[0] + wr[1] * extra[1])
    moved = complex_times(extra, tw)
    c2 = complex_times((alpha[0], -alpha[1]), (tr[0] - moved[0], tr[1] - moved[1]))
    cross = complex_times(complex_times((extra[0], -extra[1]), alpha), (tw[0], -tw[1]))
    ww2 = (alpha[0] * alpha[0] + alpha[1] * alpha[1]) * tt
    ww2 = ww2 + (extra[0] * extra[0] + extra[1] * extra[1]) * ww - 2.0 * cross[0]
    alpha2 = (c2[0] / ww2, c2[1] / ww2)
    fresh2 = fresh - (c2[0] * alpha2[0] + c2[1] * alpha2[1])
    history_ref[...] = jnp.where(lane == 0, fresh / start, fresh2 / start)
    right, image, image2 = pair(right_ref), pair(image_ref), pair(image2_ref)
    direction, direction2 = pair(direction_ref), pair(direction2_ref)
    step = complex_times(alpha, direction)
    other = complex_times(alpha, direction2)
    step2 = complex_times(alpha2, (direction[0] - other[0], direction[1] - other[1]))
    away = complex_times(extra, image)
    other = complex_times(alpha, image2)
    away2 = complex_times(alpha2, (image[0] - other[0], image[1] - other[1]))
    for c in range(2):
        solution_ref[c, 0] = lanes(step[c] + step2[c], EB)
        residual_ref[c, 0] = lanes(right[c] - image[c] - away[c] - away2[c], EB)


def shape(*dims, dtype=F32):
    return jax.ShapeDtypeStruct(dims, dtype)


FIELD = shape(2 * EB, BS)
MESSAGES = [shape(4, BS)] * 4


def call(body, outs, args, name, scratch=(), smem=(), flops=0):
    specs = [pl.BlockSpec(memory_space=pltpu.SMEM if k in smem else pltpu.VMEM) for k in range(len(args))]
    moved = sum(a.size * a.dtype.itemsize for a in args)
    return pl.pallas_call(
        body,
        out_shape=outs,
        in_specs=specs,
        out_specs=[pl.BlockSpec(memory_space=pltpu.VMEM)] * len(outs),
        scratch_shapes=scratch,
        compiler_params=pltpu.CompilerParams(vmem_limit_bytes=LIMIT),
        cost_estimate=pl.CostEstimate(flops=flops, bytes_accessed=moved, transcendentals=0),
        name=name,
    )(*args)


def swap(pairs):
    return [(a, b) for a, b in pairs] + [(b, a) for a, b in pairs]


def exchange(messages):
    lat, lon = lax.axis_size("lat"), lax.axis_size("lon")
    core = swap([(k, k + 1) for k in range(0, lat, 2)])
    far = swap([(k, k + 1) for k in range(1, lat - 1, 2)])
    near = swap([(k, k + 1) for k in range(0, lon, 2)])
    wide = swap([(k, (k + 1) % lon) for k in range(1, lon, 2)])
    return [
        lax.ppermute(messages[0], "lat", core),
        lax.ppermute(messages[1], "lat", far),
        lax.ppermute(messages[2], "lon", near),
        lax.ppermute(messages[3], "lon", wide),
    ]


def everywhere(row, axis):
    return lax.all_to_all(row, axis, 0, 0)


def on_device(rhs, cond, blk_diag, blk_off, idx, cnt, coup, nodes):
    blocks = pltpu.VMEM((EB, BS), F32)
    wide = pltpu.VMEM((8 * (EB + 2), BS), F32)
    out = pltpu.VMEM((8 * EB, BS), F32)
    *sent, ohi, oht, ohh, coef, value, scale, right, first, own = call(
        begin_kernel,
        [shape(8, BS)] * 4
        + [shape(BS, 4 * IFC, dtype=BF16), shape(BS, E, dtype=BF16), shape(BS, E, dtype=BF16), shape(1, 4 * IFC)]
        + [FIELD] * 4
        + [shape(8, BS)],
        (rhs, cond, blk_diag, idx, cnt, coup, nodes),
        "begin",
        scratch=[blocks],
        smem=(4,),
    )
    arrived = exchange(sent)
    (weights,) = call(
        weight_kernel, [shape(EB, 3 * BS, 2 * BS, dtype=BF16)], (blk_diag, blk_off), "weights", flops=10**7
    )

    def local(field):
        return call(
            local_kernel, [FIELD], (field, value, weights), "local", scratch=[wide, out], flops=2 * 8 * EB * 3 * BS * 2 * BS
        )[0]

    images, directions = [], []
    for step in range(ITERS):
        stiff = local(first)
        if step == 0:
            *sent, second, ninv = call(
                smooth_first_kernel,
                MESSAGES + [FIELD, shape(4, BS)],
                (*arrived, own, ohi, coef, idx, first, stiff, scale, right),
                "smooth_first",
            )
            source = right
        else:
            *sent, second = call(
                smooth_kernel,
                MESSAGES + [FIELD],
                (*arrived, ohi, coef, idx, first, stiff, scale, source),
                "smooth",
            )
        arrived = exchange(sent)
        stiff = local(second)
        *sent, own = call(
            restrict_kernel,
            MESSAGES + [shape(8, BS)],
            (*arrived, ohi, oht, ohh, coef, idx, nodes, stiff, source),
            "restrict",
        )
        arrived = exchange(sent)
        (y,) = call(node_kernel, [shape(4, BS)], (*arrived, own, ninv), "node")
        arrived = exchange([y] * 4)
        *sent, direction = call(
            prolong_kernel,
            MESSAGES + [FIELD],
            (*arrived, y, ohi, oht, ohh, idx, nodes, second),
            "prolong",
            scratch=[blocks, pltpu.VMEM((2 * EB, BS), F32)],
        )
        directions.append(direction)
        arrived = exchange(sent)
        stiff = local(direction)
        if step == 0:
            *sent, image, first = call(
                image_kernel,
                MESSAGES + [FIELD, FIELD],
                (*arrived, ohi, coef, idx, stiff, scale),
                "image",
            )
            source = image
            arrived = exchange(sent)
    image2, sums = call(
        sums_kernel,
        [FIELD, shape(lax.axis_size("lat"), 1, BS)],
        (*arrived, ohi, coef, idx, stiff, right, image),
        "sums",
    )
    sums = jnp.sum(everywhere(sums, "lat"), axis=0, keepdims=True)
    sums = everywhere(jnp.broadcast_to(sums, (lax.axis_size("lon"), 1, BS)), "lon")
    solution, residual, history = call(
        finish_kernel,
        [shape(2, 1, 1, E), shape(2, 1, 1, E), shape(1, BS)],
        (sums, right, image, image2, directions[0], directions[1]),
        "finish",
    )
    return solution, residual, history[0, :ITERS]


def solution(mesh):
    placed = (
        P(None, "lat", "lon", None),
        P("lat", "lon", None),
        P("lat", "lon", None, None, None),
        P("lat", "lon", None, None, None),
        P("lat", "lon", None, None),
        P("lat", "lon", None),
        P("lat", "lon", None, None),
        P("lat", "lon", None, None),
    )
    return jax.shard_map(
        on_device,
        mesh=mesh,
        in_specs=placed,
        out_specs=(P(None, "lat", "lon", None), P(None, "lat", "lon", None), P()),
        check_vma=False,
    )
```

time: 752 us -> 204 us (0.27); the launches traced: 741 us -> 203 us
  blocking collectives: 303 us -> 28.1 us
  other arithmetic: 125 us -> 0.03 us
  local copies, waits for them, and re-layouts: 111 us -> 8.33 us
  starting transfers between devices: 165 us -> 132 us
  matrix products: 25.7 us -> 0 us
  waiting for transfers between devices: 1.59 us -> 22.8 us
  Pallas kernels: 0 us -> 10 us
  between operations: 10.6 us -> 1.3 us
    psum x3 -> x0, blocking collectives: 303 us -> none  [the longest x2 208 us: on_device(): c_re, c_im, ww = lax.psum((c_re, c_im, ww), ('lat', 'lon'))]
    scatter-add x12 -> x0, other arithmetic: 113 us -> none  [the longest x6 72.4 us: nodal_partial(): return ext.at[:, heads].add(values).at[:, tails].add(sign * values)]
    gather x22 -> x0, local copies, waits for them, and re-layouts: 70.2 us -> none  [the longest x8 36.6 us: on_device(): direction = second + correction[:, heads] - correction[:, tails]]
    ppermute x44 -> x40, starting transfers between devices: 165 us -> 132 us  [the longest x10 43.4 us: exchange(): lax.ppermute(messages[3], 'lon', wide)]
    all_to_all x0 -> x2, blocking collectives: none -> 28.1 us  [everywhere(): return lax.all_to_all(row, axis, 0, 0)]
    dot_general x18 -> x0, matrix products: 25.7 us -> none  [the longest x6 10.4 us: local_apply(): result = jnp.einsum('bij,cbj->cbi', blk_diag, shaped, precision=HIGH)]
    ppermute x44 -> x40, waiting for transfers between devices: 1.59 us -> 22.8 us  [the longest x10 20.5 us: exchange(): lax.ppermute(messages[3], 'lon', wide)]
    pallas_call x0 -> x19, Pallas kernels: none -> 10 us  [call(): pl.pallas_call(body, out_shape=outs, in_specs=specs, out_specs=[pl.BlockS...]
  transfers between devices with their start and end apart: 44 -> 40, of which waited for: 3 -> 9; matrix products, arithmetic and copies ran while one was open for 14% -> 0% of each run, Pallas kernels for 0% -> 2%
where the time goes in v1:
time: 204 us; the launch traced here: 203 us
  starting transfers between devices  132 us (65%)
  blocking collectives  28.1 us (14%)
  waiting for transfers between devices  22.8 us (11%)
  Pallas kernels  10 us (5%)
  local copies, waits for them, and re-layouts  8.33 us (4%)
    ppermute x10, starting transfers between devices, exchange(): lax.ppermute(messages[3], 'lon', wide)  43.4 us
    ppermute x10, starting transfers between devices, exchange(): lax.ppermute(messages[1], 'lat', far)  39.6 us
    all_to_all x2, blocking collectives, everywhere(): return lax.all_to_all(row, axis, 0, 0)  28.1 us
    ppermute x10, starting transfers between devices, exchange(): lax.ppermute(messages[0], 'lat', core)  26.4 us
    ppermute x10, starting transfers between devices, exchange(): lax.ppermute(messages[2], 'lon', near)  22.7 us
    ppermute x10, waiting for transfers between devices, exchange(): lax.ppermute(messages[3], 'lon', wide)  20.5 us
    pallas_call x19, Pallas kernels, call(): pl.pallas_call(body, out_shape=outs, in_specs=specs, out_specs=[pl.BlockS...  10 us
    unnamed x22, local copies, waits for them, and re-layouts  7.81 us
  transfers between devices with their start and end apart: 40, of which 9 were waited for; matrix products, arithmetic and copies ran while one was open for 0% of the time, Pallas kernels for 2%

profile of v1, /device:TPU:1, one launch (start us, length us, event | category | flops | bytes accessed | tf_op | source)
XLA Modules:
  0.0 202.7 jit_solution(13786151601997805019)
XLA Ops:
  7.4 8.8 %collective-permute-start = (f32[8,128]{1,0:T(8,128)S(1)}, f32[8,128]{1,0:T(8,128)S(1)}, u32[]{:S(2)}, u32[]{:S(2)}) collective-permute-start(f32[8,128]{1,0:T(8,128)S(1)} %get-tuple-element.58), channel_id=1, source_target_pairs={{0,32},{64,96},{128,160},{192,224},{256,288},{320,352},{384,416},{... | collective-permute-start | bytes 12296 | tf_op jit(solution)/shard_map/ppermute | solution.py:435
  20.1 5.0 %collective-permute-start.3 = (f32[8,128]{1,0:T(8,128)S(1)}, f32[8,128]{1,0:T(8,128)S(1)}, u32[]{:S(2)}, u32[]{:S(2)}) collective-permute-start(f32[8,128]{1,0:T(8,128)S(1)} %get-tuple-element.61), channel_id=1, source_target_pairs={{1,2},{3,4},{5,6},{7,8},{9,10},{11,12},{13,14},{15,16},{17,18},{19... | collective-permute-start | bytes 12296 | tf_op jit(solution)/shard_map/ppermute | solution.py:438
  31.0 4.4 %collective-permute-start.5 = (f32[4,128]{1,0:T(4,128)S(1)}, f32[4,128]{1,0:T(4,128)S(1)}, u32[]{:S(2)}, u32[]{:S(2)}) collective-permute-start(f32[4,128]{1,0:T(4,128)S(1)} %get-tuple-element.70), channel_id=1, source_target_pairs={{32,64},{96,128},{160,192},{224,256},{288,320},{352,384},{416,448}... | collective-permute-start | bytes 6152 | tf_op jit(solution)/shard_map/ppermute | solution.py:436
  37.3 4.1 %collective-permute-start.7 = (f32[4,128]{1,0:T(4,128)S(1)}, f32[4,128]{1,0:T(4,128)S(1)}, u32[]{:S(2)}, u32[]{:S(2)}) collective-permute-start(f32[4,128]{1,0:T(4,128)S(1)} %get-tuple-element.72), channel_id=1, source_target_pairs={{1,2},{3,4},{5,6},{7,8},{9,10},{11,12},{13,14},{15,16},{17,18},{19... | collective-permute-start | bytes 6152 | tf_op jit(solution)/shard_map/ppermute | solution.py:438
  47.6 4.4 %collective-permute-start.9 = (f32[4,128]{1,0:T(4,128)S(1)}, f32[4,128]{1,0:T(4,128)S(1)}, u32[]{:S(2)}, u32[]{:S(2)}) collective-permute-start(f32[4,128]{1,0:T(4,128)S(1)} %get-tuple-element.77), channel_id=1, source_target_pairs={{32,64},{96,128},{160,192},{224,256},{288,320},{352,384},{416,448}... | collective-permute-start | bytes 6152 | tf_op jit(solution)/shard_map/ppermute | solution.py:436
  53.9 4.1 %collective-permute-start.11 = (f32[4,128]{1,0:T(4,128)S(1)}, f32[4,128]{1,0:T(4,128)S(1)}, u32[]{:S(2)}, u32[]{:S(2)}) collective-permute-start(f32[4,128]{1,0:T(4,128)S(1)} %get-tuple-element.79), channel_id=1, source_target_pairs={{1,2},{3,4},{5,6},{7,8},{9,10},{11,12},{13,14},{15,16},{17,18},{19... | collective-permute-start | bytes 6152 | tf_op jit(solution)/shard_map/ppermute | solution.py:438
  58.1 3.5 %collective-permute-done.11.a3 = f32[4,128]{1,0:T(4,128)S(1)} collective-permute-done((f32[4,128]{1,0:T(4,128)S(1)}, f32[4,128]{1,0:T(4,128)S(1)}, u32[]{:S(2)}, u32[]{:S(2)}) %collective-permute-start.11) | collective-permute-done | bytes 2080 | tf_op jit(solution)/shard_map/ppermute | solution.py:438
  61.6 4.1 %collective-permute-start.15 = (f32[4,128]{1,0:T(4,128)S(1)}, f32[4,128]{1,0:T(4,128)S(1)}, u32[]{:S(2)}, u32[]{:S(2)}) collective-permute-start(f32[4,128]{1,0:T(4,128)S(1)} %node.2.y_ref), channel_id=1, source_target_pairs={{1,2},{3,4},{5,6},{7,8},{9,10},{11,12},{13,14},{15,16},{17,18},{19... | collective-permute-start | bytes 6152 | tf_op jit(solution)/shard_map/ppermute | solution.py:438
  76.6 5.4 %collective-permute-start.17 = (f32[4,128]{1,0:T(4,128)S(1)}, f32[4,128]{1,0:T(4,128)S(1)}, u32[]{:S(2)}, u32[]{:S(2)}) collective-permute-start(f32[4,128]{1,0:T(4,128)S(1)} %get-tuple-element.83), channel_id=1, source_target_pairs={{32,64},{96,128},{160,192},{224,256},{288,320},{352,384},{416,448}... | collective-permute-start | bytes 6152 | tf_op jit(solution)/shard_map/ppermute | solution.py:436
  82.1 3.6 %collective-permute-start.18 = (f32[4,128]{1,0:T(4,128)S(1)}, f32[4,128]{1,0:T(4,128)S(1)}, u32[]{:S(2)}, u32[]{:S(2)}) collective-permute-start(f32[4,128]{1,0:T(4,128)S(1)} %get-tuple-element.84), channel_id=1, source_target_pairs={{0,1},{2,3},{4,5},{6,7},{8,9},{10,11},{12,13},{14,15},{16,17},{18,... | collective-permute-start | bytes 6152 | tf_op jit(solution)/shard_map/ppermute | solution.py:437
  85.7 4.5 %collective-permute-start.19 = (f32[4,128]{1,0:T(4,128)S(1)}, f32[4,128]{1,0:T(4,128)S(1)}, u32[]{:S(2)}, u32[]{:S(2)}) collective-permute-start(f32[4,128]{1,0:T(4,128)S(1)} %get-tuple-element.85), channel_id=1, source_target_pairs={{1,2},{3,4},{5,6},{7,8},{9,10},{11,12},{13,14},{15,16},{17,18},{19... | collective-permute-start | bytes 6152 | tf_op jit(solution)/shard_map/ppermute | solution.py:438
  95.8 3.6 %collective-permute-start.21 = (f32[4,128]{1,0:T(4,128)S(1)}, f32[4,128]{1,0:T(4,128)S(1)}, u32[]{:S(2)}, u32[]{:S(2)}) collective-permute-start(f32[4,128]{1,0:T(4,128)S(1)} %get-tuple-element.88), channel_id=1, source_target_pairs={{32,64},{96,128},{160,192},{224,256},{288,320},{352,384},{416,448}... | collective-permute-start | bytes 6152 | tf_op jit(solution)/shard_map/ppermute | solution.py:436
  101.3 4.5 %collective-permute-start.23 = (f32[4,128]{1,0:T(4,128)S(1)}, f32[4,128]{1,0:T(4,128)S(1)}, u32[]{:S(2)}, u32[]{:S(2)}) collective-permute-start(f32[4,128]{1,0:T(4,128)S(1)} %get-tuple-element.90), channel_id=1, source_target_pairs={{1,2},{3,4},{5,6},{7,8},{9,10},{11,12},{13,14},{15,16},{17,18},{19... | collective-permute-start | bytes 6152 | tf_op jit(solution)/shard_map/ppermute | solution.py:438
  111.4 5.0 %collective-permute-start.25 = (f32[4,128]{1,0:T(4,128)S(1)}, f32[4,128]{1,0:T(4,128)S(1)}, u32[]{:S(2)}, u32[]{:S(2)}) collective-permute-start(f32[4,128]{1,0:T(4,128)S(1)} %get-tuple-element.94), channel_id=1, source_target_pairs={{32,64},{96,128},{160,192},{224,256},{288,320},{352,384},{416,448}... | collective-permute-start | bytes 6152 | tf_op jit(solution)/shard_map/ppermute | solution.py:436
  118.3 4.3 %collective-permute-start.27 = (f32[4,128]{1,0:T(4,128)S(1)}, f32[4,128]{1,0:T(4,128)S(1)}, u32[]{:S(2)}, u32[]{:S(2)}) collective-permute-start(f32[4,128]{1,0:T(4,128)S(1)} %get-tuple-element.96), channel_id=1, source_target_pairs={{1,2},{3,4},{5,6},{7,8},{9,10},{11,12},{13,14},{15,16},{17,18},{19... | collective-permute-start | bytes 6152 | tf_op jit(solution)/shard_map/ppermute | solution.py:438
  128.6 3.6 %collective-permute-start.29 = (f32[4,128]{1,0:T(4,128)S(1)}, f32[4,128]{1,0:T(4,128)S(1)}, u32[]{:S(2)}, u32[]{:S(2)}) collective-permute-start(f32[4,128]{1,0:T(4,128)S(1)} %get-tuple-element.99), channel_id=1, source_target_pairs={{32,64},{96,128},{160,192},{224,256},{288,320},{352,384},{416,448}... | collective-permute-start | bytes 6152 | tf_op jit(solution)/shard_map/ppermute | solution.py:436
  134.1 4.3 %collective-permute-start.31 = (f32[4,128]{1,0:T(4,128)S(1)}, f32[4,128]{1,0:T(4,128)S(1)}, u32[]{:S(2)}, u32[]{:S(2)}) collective-permute-start(f32[4,128]{1,0:T(4,128)S(1)} %get-tuple-element.101), channel_id=1, source_target_pairs={{1,2},{3,4},{5,6},{7,8},{9,10},{11,12},{13,14},{15,16},{17,18},{19... | collective-permute-start | bytes 6152 | tf_op jit(solution)/shard_map/ppermute | solution.py:438
  141.8 4.3 %collective-permute-start.35 = (f32[4,128]{1,0:T(4,128)S(1)}, f32[4,128]{1,0:T(4,128)S(1)}, u32[]{:S(2)}, u32[]{:S(2)}) collective-permute-start(f32[4,128]{1,0:T(4,128)S(1)} %node.3.y_ref), channel_id=1, source_target_pairs={{1,2},{3,4},{5,6},{7,8},{9,10},{11,12},{13,14},{15,16},{17,18},{19... | collective-permute-start | bytes 6152 | tf_op jit(solution)/shard_map/ppermute | solution.py:438
  148.0 3.4 %collective-permute-start.33 = (f32[4,128]{1,0:T(4,128)S(1)}, f32[4,128]{1,0:T(4,128)S(1)}, u32[]{:S(2)}, u32[]{:S(2)}) collective-permute-start(f32[4,128]{1,0:T(4,128)S(1)} %node.3.y_ref), channel_id=1, source_target_pairs={{32,64},{96,128},{160,192},{224,256},{288,320},{352,384},{416,448}... | collective-permute-start | bytes 6152 | tf_op jit(solution)/shard_map/ppermute | solution.py:436
  157.1 4.6 %collective-permute-start.37 = (f32[4,128]{1,0:T(4,128)S(1)}, f32[4,128]{1,0:T(4,128)S(1)}, u32[]{:S(2)}, u32[]{:S(2)}) collective-permute-start(f32[4,128]{1,0:T(4,128)S(1)} %get-tuple-element.104), channel_id=1, source_target_pairs={{32,64},{96,128},{160,192},{224,256},{288,320},{352,384},{416,448}... | collective-permute-start | bytes 6152 | tf_op jit(solution)/shard_map/ppermute | solution.py:436
  161.6 3.6 %collective-permute-start.38 = (f32[4,128]{1,0:T(4,128)S(1)}, f32[4,128]{1,0:T(4,128)S(1)}, u32[]{:S(2)}, u32[]{:S(2)}) collective-permute-start(f32[4,128]{1,0:T(4,128)S(1)} %get-tuple-element.105), channel_id=1, source_target_pairs={{0,1},{2,3},{4,5},{6,7},{8,9},{10,11},{12,13},{14,15},{16,17},{18,... | collective-permute-start | bytes 6152 | tf_op jit(solution)/shard_map/ppermute | solution.py:437
  165.3 4.3 %collective-permute-start.39 = (f32[4,128]{1,0:T(4,128)S(1)}, f32[4,128]{1,0:T(4,128)S(1)}, u32[]{:S(2)}, u32[]{:S(2)}) collective-permute-start(f32[4,128]{1,0:T(4,128)S(1)} %get-tuple-element.106), channel_id=1, source_target_pairs={{1,2},{3,4},{5,6},{7,8},{9,10},{11,12},{13,14},{15,16},{17,18},{19... | collective-permute-start | bytes 6152 | tf_op jit(solution)/shard_map/ppermute | solution.py:438
  173.3 15.6 %all_to_all.10 = f32[16,1,128]{2,1,0:T(1,128)S(1)} all-to-all(f32[16,1,128]{2,1,0:T(1,128)S(1)} %get-tuple-element.108), channel_id=1, replica_groups=mesh['lat'=16,'lon'=32] {'lat'}, dimensions={0} | all-to-all | bytes 16384 | tf_op jit(solution)/shard_map/all_to_all | solution.py:443
  188.9 12.5 %all_to_all.11.sums_ref = f32[32,1,128]{2,1,0:T(1,128)S(1)} all-to-all(f32[32,1,128]{2,1,0:T(1,128)S(1)} %broadcast_in_dim.2), channel_id=1, replica_groups=mesh['lat'=16,'lon'=32] {'lon'}, dimensions={0} | all-to-all | bytes 32768 | tf_op jit(solution)/shard_map/all_to_all | solution.py:443
  (102 shorter events, 75.9 us)
Async XLA Ops:
  7.4 21.1 %collective-permute-start = (f32[8,128]{1,0:T(8,128)S(1)}, f32[8,128]{1,0:T(8,128)S(1)}, u32[]{:S(2)}, u32[]{:S(2)}) collective-permute-start(f32[8,128]{1,0:T(8,128)S(1)} %get-tuple-element.58), channel_id=1, source_target_pairs={{0,32},{64,96},{128,160},{192,224},{256,288},{320,352},{384,416},{... | collective-permute-start | bytes 12296 | tf_op jit(solution)/shard_map/ppermute | solution.py:435
  16.2 12.3 %collective-permute-start.1 = (f32[8,128]{1,0:T(8,128)S(1)}, f32[8,128]{1,0:T(8,128)S(1)}, u32[]{:S(2)}, u32[]{:S(2)}) collective-permute-start(f32[8,128]{1,0:T(8,128)S(1)} %get-tuple-element.59), channel_id=1, source_target_pairs={{32,64},{96,128},{160,192},{224,256},{288,320},{352,384},{416,448}... | collective-permute-start | bytes 12296 | tf_op jit(solution)/shard_map/ppermute | solution.py:436
  18.1 10.4 %collective-permute-start.2 = (f32[8,128]{1,0:T(8,128)S(1)}, f32[8,128]{1,0:T(8,128)S(1)}, u32[]{:S(2)}, u32[]{:S(2)}) collective-permute-start(f32[8,128]{1,0:T(8,128)S(1)} %get-tuple-element.60), channel_id=1, source_target_pairs={{0,1},{2,3},{4,5},{6,7},{8,9},{10,11},{12,13},{14,15},{16,17},{18,... | collective-permute-start | bytes 12296 | tf_op jit(solution)/shard_map/ppermute | solution.py:437
  20.1 8.5 %collective-permute-start.3 = (f32[8,128]{1,0:T(8,128)S(1)}, f32[8,128]{1,0:T(8,128)S(1)}, u32[]{:S(2)}, u32[]{:S(2)}) collective-permute-start(f32[8,128]{1,0:T(8,128)S(1)} %get-tuple-element.61), channel_id=1, source_target_pairs={{1,2},{3,4},{5,6},{7,8},{9,10},{11,12},{13,14},{15,16},{17,18},{19... | collective-permute-start | bytes 12296 | tf_op jit(solution)/shard_map/ppermute | solution.py:438
  29.1 12.9 %collective-permute-start.4 = (f32[4,128]{1,0:T(4,128)S(1)}, f32[4,128]{1,0:T(4,128)S(1)}, u32[]{:S(2)}, u32[]{:S(2)}) collective-permute-start(f32[4,128]{1,0:T(4,128)S(1)} %get-tuple-element.69), channel_id=1, source_target_pairs={{0,32},{64,96},{128,160},{192,224},{256,288},{320,352},{384,416},{... | collective-permute-start | bytes 6152 | tf_op jit(solution)/shard_map/ppermute | solution.py:435
  31.0 11.0 %collective-permute-start.5 = (f32[4,128]{1,0:T(4,128)S(1)}, f32[4,128]{1,0:T(4,128)S(1)}, u32[]{:S(2)}, u32[]{:S(2)}) collective-permute-start(f32[4,128]{1,0:T(4,128)S(1)} %get-tuple-element.70), channel_id=1, source_target_pairs={{32,64},{96,128},{160,192},{224,256},{288,320},{352,384},{416,448}... | collective-permute-start | bytes 6152 | tf_op jit(solution)/shard_map/ppermute | solution.py:436
  37.3 7.6 %collective-permute-start.7 = (f32[4,128]{1,0:T(4,128)S(1)}, f32[4,128]{1,0:T(4,128)S(1)}, u32[]{:S(2)}, u32[]{:S(2)}) collective-permute-start(f32[4,128]{1,0:T(4,128)S(1)} %get-tuple-element.72), channel_id=1, source_target_pairs={{1,2},{3,4},{5,6},{7,8},{9,10},{11,12},{13,14},{15,16},{17,18},{19... | collective-permute-start | bytes 6152 | tf_op jit(solution)/shard_map/ppermute | solution.py:438
  45.6 12.4 %collective-permute-start.8 = (f32[4,128]{1,0:T(4,128)S(1)}, f32[4,128]{1,0:T(4,128)S(1)}, u32[]{:S(2)}, u32[]{:S(2)}) collective-permute-start(f32[4,128]{1,0:T(4,128)S(1)} %get-tuple-element.76), channel_id=1, source_target_pairs={{0,32},{64,96},{128,160},{192,224},{256,288},{320,352},{384,416},{... | collective-permute-start | bytes 6152 | tf_op jit(solution)/shard_map/ppermute | solution.py:435
  47.6 10.5 %collective-permute-start.9 = (f32[4,128]{1,0:T(4,128)S(1)}, f32[4,128]{1,0:T(4,128)S(1)}, u32[]{:S(2)}, u32[]{:S(2)}) collective-permute-start(f32[4,128]{1,0:T(4,128)S(1)} %get-tuple-element.77), channel_id=1, source_target_pairs={{32,64},{96,128},{160,192},{224,256},{288,320},{352,384},{416,448}... | collective-permute-start | bytes 6152 | tf_op jit(solution)/shard_map/ppermute | solution.py:436
  53.9 7.6 %collective-permute-start.11 = (f32[4,128]{1,0:T(4,128)S(1)}, f32[4,128]{1,0:T(4,128)S(1)}, u32[]{:S(2)}, u32[]{:S(2)}) collective-permute-start(f32[4,128]{1,0:T(4,128)S(1)} %get-tuple-element.79), channel_id=1, source_target_pairs={{1,2},{3,4},{5,6},{7,8},{9,10},{11,12},{13,14},{15,16},{17,18},{19... | collective-permute-start | bytes 6152 | tf_op jit(solution)/shard_map/ppermute | solution.py:438
  61.6 11.3 %collective-permute-start.15 = (f32[4,128]{1,0:T(4,128)S(1)}, f32[4,128]{1,0:T(4,128)S(1)}, u32[]{:S(2)}, u32[]{:S(2)}) collective-permute-start(f32[4,128]{1,0:T(4,128)S(1)} %node.2.y_ref), channel_id=1, source_target_pairs={{1,2},{3,4},{5,6},{7,8},{9,10},{11,12},{13,14},{15,16},{17,18},{19... | collective-permute-start | bytes 6152 | tf_op jit(solution)/shard_map/ppermute | solution.py:438
  74.6 16.2 %collective-permute-start.16 = (f32[4,128]{1,0:T(4,128)S(1)}, f32[4,128]{1,0:T(4,128)S(1)}, u32[]{:S(2)}, u32[]{:S(2)}) collective-permute-start(f32[4,128]{1,0:T(4,128)S(1)} %get-tuple-element.82), channel_id=1, source_target_pairs={{0,32},{64,96},{128,160},{192,224},{256,288},{320,352},{384,416},{... | collective-permute-start | bytes 6152 | tf_op jit(solution)/shard_map/ppermute | solution.py:435
  76.6 14.1 %collective-permute-start.17 = (f32[4,128]{1,0:T(4,128)S(1)}, f32[4,128]{1,0:T(4,128)S(1)}, u32[]{:S(2)}, u32[]{:S(2)}) collective-permute-start(f32[4,128]{1,0:T(4,128)S(1)} %get-tuple-element.83), channel_id=1, source_target_pairs={{32,64},{96,128},{160,192},{224,256},{288,320},{352,384},{416,448}... | collective-permute-start | bytes 6152 | tf_op jit(solution)/shard_map/ppermute | solution.py:436
  82.1 8.7 %collective-permute-start.18 = (f32[4,128]{1,0:T(4,128)S(1)}, f32[4,128]{1,0:T(4,128)S(1)}, u32[]{:S(2)}, u32[]{:S(2)}) collective-permute-start(f32[4,128]{1,0:T(4,128)S(1)} %get-tuple-element.84), channel_id=1, source_target_pairs={{0,1},{2,3},{4,5},{6,7},{8,9},{10,11},{12,13},{14,15},{16,17},{18,... | collective-permute-start | bytes 6152 | tf_op jit(solution)/shard_map/ppermute | solution.py:437
  93.8 12.5 %collective-permute-start.20 = (f32[4,128]{1,0:T(4,128)S(1)}, f32[4,128]{1,0:T(4,128)S(1)}, u32[]{:S(2)}, u32[]{:S(2)}) collective-permute-start(f32[4,128]{1,0:T(4,128)S(1)} %get-tuple-element.87), channel_id=1, source_target_pairs={{0,32},{64,96},{128,160},{192,224},{256,288},{320,352},{384,416},{... | collective-permute-start | bytes 6152 | tf_op jit(solution)/shard_map/ppermute | solution.py:435
  95.8 10.6 %collective-permute-start.21 = (f32[4,128]{1,0:T(4,128)S(1)}, f32[4,128]{1,0:T(4,128)S(1)}, u32[]{:S(2)}, u32[]{:S(2)}) collective-permute-start(f32[4,128]{1,0:T(4,128)S(1)} %get-tuple-element.88), channel_id=1, source_target_pairs={{32,64},{96,128},{160,192},{224,256},{288,320},{352,384},{416,448}... | collective-permute-start | bytes 6152 | tf_op jit(solution)/shard_map/ppermute | solution.py:436
  109.5 13.7 %collective-permute-start.24 = (f32[4,128]{1,0:T(4,128)S(1)}, f32[4,128]{1,0:T(4,128)S(1)}, u32[]{:S(2)}, u32[]{:S(2)}) collective-permute-start(f32[4,128]{1,0:T(4,128)S(1)} %get-tuple-element.93), channel_id=1, source_target_pairs={{0,32},{64,96},{128,160},{192,224},{256,288},{320,352},{384,416},{... | collective-permute-start | bytes 6152 | tf_op jit(solution)/shard_map/ppermute | solution.py:435
  111.4 11.7 %collective-permute-start.25 = (f32[4,128]{1,0:T(4,128)S(1)}, f32[4,128]{1,0:T(4,128)S(1)}, u32[]{:S(2)}, u32[]{:S(2)}) collective-permute-start(f32[4,128]{1,0:T(4,128)S(1)} %get-tuple-element.94), channel_id=1, source_target_pairs={{32,64},{96,128},{160,192},{224,256},{288,320},{352,384},{416,448}... | collective-permute-start | bytes 6152 | tf_op jit(solution)/shard_map/ppermute | solution.py:436
  126.6 11.8 %collective-permute-start.28 = (f32[4,128]{1,0:T(4,128)S(1)}, f32[4,128]{1,0:T(4,128)S(1)}, u32[]{:S(2)}, u32[]{:S(2)}) collective-permute-start(f32[4,128]{1,0:T(4,128)S(1)} %get-tuple-element.98), channel_id=1, source_target_pairs={{0,32},{64,96},{128,160},{192,224},{256,288},{320,352},{384,416},{... | collective-permute-start | bytes 6152 | tf_op jit(solution)/shard_map/ppermute | solution.py:435
  128.6 9.9 %collective-permute-start.29 = (f32[4,128]{1,0:T(4,128)S(1)}, f32[4,128]{1,0:T(4,128)S(1)}, u32[]{:S(2)}, u32[]{:S(2)}) collective-permute-start(f32[4,128]{1,0:T(4,128)S(1)} %get-tuple-element.99), channel_id=1, source_target_pairs={{32,64},{96,128},{160,192},{224,256},{288,320},{352,384},{416,448}... | collective-permute-start | bytes 6152 | tf_op jit(solution)/shard_map/ppermute | solution.py:436
  141.8 11.5 %collective-permute-start.35 = (f32[4,128]{1,0:T(4,128)S(1)}, f32[4,128]{1,0:T(4,128)S(1)}, u32[]{:S(2)}, u32[]{:S(2)}) collective-permute-start(f32[4,128]{1,0:T(4,128)S(1)} %node.3.y_ref), channel_id=1, source_target_pairs={{1,2},{3,4},{5,6},{7,8},{9,10},{11,12},{13,14},{15,16},{17,18},{19... | collective-permute-start | bytes 6152 | tf_op jit(solution)/shard_map/ppermute | solution.py:438
  155.0 15.2 %collective-permute-start.36 = (f32[4,128]{1,0:T(4,128)S(1)}, f32[4,128]{1,0:T(4,128)S(1)}, u32[]{:S(2)}, u32[]{:S(2)}) collective-permute-start(f32[4,128]{1,0:T(4,128)S(1)} %get-tuple-element.103), channel_id=1, source_target_pairs={{0,32},{64,96},{128,160},{192,224},{256,288},{320,352},{384,416},{... | collective-permute-start | bytes 6152 | tf_op jit(solution)/shard_map/ppermute | solution.py:435
  157.1 13.1 %collective-permute-start.37 = (f32[4,128]{1,0:T(4,128)S(1)}, f32[4,128]{1,0:T(4,128)S(1)}, u32[]{:S(2)}, u32[]{:S(2)}) collective-permute-start(f32[4,128]{1,0:T(4,128)S(1)} %get-tuple-element.104), channel_id=1, source_target_pairs={{32,64},{96,128},{160,192},{224,256},{288,320},{352,384},{416,448}... | collective-permute-start | bytes 6152 | tf_op jit(solution)/shard_map/ppermute | solution.py:436
  161.6 8.5 %collective-permute-start.38 = (f32[4,128]{1,0:T(4,128)S(1)}, f32[4,128]{1,0:T(4,128)S(1)}, u32[]{:S(2)}, u32[]{:S(2)}) collective-permute-start(f32[4,128]{1,0:T(4,128)S(1)} %get-tuple-element.105), channel_id=1, source_target_pairs={{0,1},{2,3},{4,5},{6,7},{8,9},{10,11},{12,13},{14,15},{16,17},{18,... | collective-permute-start | bytes 6152 | tf_op jit(solution)/shard_map/ppermute | solution.py:437
  (27 other events, 128.1 us)

commit v2 on v1

--- a/solution.py
+++ b/solution.py
@@ -15,6 +15,7 @@
 F32 = jnp.float32
 BF16 = jnp.bfloat16
 LIMIT = 20 * 1024 * 1024
+BEGIN_LIMIT = 60 * 1024 * 1024
 NT = (((1,), (1,)), ((), ()))
 
 
@@ -103,15 +104,15 @@
 
 def hand_out(refs, towards, at=0):
     even_lat, even_lon = parities()
-    refs[0][at : at + 4] = jnp.where(even_lat, towards[1], towards[0])
-    refs[1][at : at + 4] = jnp.where(even_lat, towards[0], towards[1])
-    refs[2][at : at + 4] = jnp.where(even_lon, towards[3], towards[2])
-    refs[3][at : at + 4] = jnp.where(even_lon, towards[2], towards[3])
+    refs[0][at : at + 4] = jnp.where(even_lon, towards[2], towards[3])
+    refs[1][at : at + 4] = jnp.where(even_lon, towards[3], towards[2])
+    refs[2][at : at + 4] = jnp.where(even_lat, towards[0], towards[1])
+    refs[3][at : at + 4] = jnp.where(even_lat, towards[1], towards[0])
 
 
 def collect(refs, at=0):
     even_lat, even_lon = parities()
-    core, far, near, wide = [ref[at : at + 4] for ref in refs]
+    wide, near, far, core = [ref[at : at + 4] for ref in refs]
     return (
         jnp.where(even_lat, far, core),
         jnp.where(even_lat, core, far),
@@ -178,14 +179,26 @@
 
 def begin_kernel(
     rhs_ref, cond_ref, diag_ref, idx_ref, cnt_ref, coup_ref, nodes_ref,
-    m0, m1, m2, m3, ohi_ref, oht_ref, ohh_ref, coef_ref, value_ref, scale_ref, right_ref, first_ref, own_ref,
-    blocks,
+    m0, m1, m2, m3, coef_ref, value_ref, scale_ref, right_ref, first_ref, own_ref,
+    ohi_ref, oht_ref, ohh_ref, blocks, rhs_got, cond_got, diag_got, idx_got, cnt_got, coup_got, nodes_got, sems,
 ):
     messages = (m0, m1, m2, m3)
+    pairs = (
+        (nodes_ref, nodes_got), (idx_ref, idx_got), (cnt_ref, cnt_got), (coup_ref, coup_got),
+        (cond_ref, cond_got), (rhs_ref, rhs_got), (diag_ref, diag_got),
+    )
+    copies = [pltpu.make_async_copy(here, there, sems.at[k]) for k, (here, there) in enumerate(pairs)]
+    for copy in copies:
+        copy.start()
+    for copy in copies[:2]:
+        copy.wait()
+    nodes_ref, idx_ref, cnt_ref, coup_ref, cond_ref, rhs_ref, diag_ref = [there for _, there in pairs]
     index = index_rows(idx_ref)
     ohi_ref[...] = lane_onehot(index)
     oht_ref[...] = lane_onehot(nodes_ref[0, 0, 0:1])
     ohh_ref[...] = lane_onehot(nodes_ref[0, 0, 1:2])
+    for copy in copies[2:]:
+        copy.wait()
     slot = lax.broadcasted_iota(jnp.int32, (1, IFC), 1)
     coef_ref[...] = jnp.concatenate(
         [jnp.where(slot < cnt_ref[0, 0, d], coup_ref[0, 0, d : d + 1], 0.0) for d in range(4)], axis=1
@@ -207,7 +220,10 @@
     nodal(rows, ohh_ref, oht_ref, nodes_ref, 1.0, messages, own_ref, 4)
 
 
-def weight_kernel(diag_ref, off_ref, w_ref):
+def weight_kernel(diag_ref, off_ref, idx_ref, nodes_ref, w_ref, ohi_ref, oht_ref, ohh_ref):
+    ohi_ref[...] = lane_onehot(index_rows(idx_ref))
+    oht_ref[...] = lane_onehot(nodes_ref[0, 0, 0:1])
+    ohh_ref[...] = lane_onehot(nodes_ref[0, 0, 1:2])
     eye = lax.broadcasted_iota(jnp.int32, (BS, BS), 0) == lax.broadcasted_iota(jnp.int32, (BS, BS), 1)
 
     def store(b, at, block):
@@ -293,13 +309,14 @@
     nodal(rows, ohh_ref, oht_ref, nodes_ref, -1.0, (m0, m1, m2, m3), own_ref, 0)
 
 
-def node_kernel(a0, a1, a2, a3, own_ref, ninv_ref, y_ref):
+def node_kernel(a0, a1, a2, a3, own_ref, ninv_ref, m0, m1, m2, m3, y_ref):
     sums = own_ref[0:4]
     for part in collect((a0, a1, a2, a3)):
         sums = sums + part
     result = complex_times((ninv_ref[0:2], ninv_ref[2:4]), (sums[0:2], sums[2:4]))
-    y_ref[0:2] = result[0]
-    y_ref[2:4] = result[1]
+    for ref in (m0, m1, m2, m3, y_ref):
+        ref[0:2] = result[0]
+        ref[2:4] = result[1]
 
 
 def prolong_kernel(
@@ -406,8 +423,8 @@
 MESSAGES = [shape(4, BS)] * 4
 
 
-def call(body, outs, args, name, scratch=(), smem=(), flops=0):
-    specs = [pl.BlockSpec(memory_space=pltpu.SMEM if k in smem else pltpu.VMEM) for k in range(len(args))]
+def call(body, outs, args, name, scratch=(), space=pltpu.VMEM, limit=LIMIT, flops=0):
+    specs = [pl.BlockSpec(memory_space=space)] * len(args)
     moved = sum(a.size * a.dtype.itemsize for a in args)
     return pl.pallas_call(
         body,
@@ -415,7 +432,7 @@
         in_specs=specs,
         out_specs=[pl.BlockSpec(memory_space=pltpu.VMEM)] * len(outs),
         scratch_shapes=scratch,
-        compiler_params=pltpu.CompilerParams(vmem_limit_bytes=LIMIT),
+        compiler_params=pltpu.CompilerParams(vmem_limit_bytes=limit),
         cost_estimate=pl.CostEstimate(flops=flops, bytes_accessed=moved, transcendentals=0),
         name=name,
     )(*args)
@@ -427,16 +444,13 @@
 
 def exchange(messages):
     lat, lon = lax.axis_size("lat"), lax.axis_size("lon")
-    core = swap([(k, k + 1) for k in range(0, lat, 2)])
-    far = swap([(k, k + 1) for k in range(1, lat - 1, 2)])
-    near = swap([(k, k + 1) for k in range(0, lon, 2)])
-    wide = swap([(k, (k + 1) % lon) for k in range(1, lon, 2)])
-    return [
-        lax.ppermute(messages[0], "lat", core),
-        lax.ppermute(messages[1], "lat", far),
-        lax.ppermute(messages[2], "lon", near),
-        lax.ppermute(messages[3], "lon", wide),
-    ]
+    swaps = (
+        ("lon", swap([(k, (k + 1) % lon) for k in range(1, lon, 2)])),
+        ("lon", swap([(k, k + 1) for k in range(0, lon, 2)])),
+        ("lat", swap([(k, k + 1) for k in range(1, lat - 1, 2)])),
+        ("lat", swap([(k, k + 1) for k in range(0, lat, 2)])),
+    )
+    return [lax.ppermute(message, *pairs) for message, pairs in zip(messages, swaps)]
 
 
 def everywhere(row, axis):
@@ -447,20 +461,28 @@
     blocks = pltpu.VMEM((EB, BS), F32)
     wide = pltpu.VMEM((8 * (EB + 2), BS), F32)
     out = pltpu.VMEM((8 * EB, BS), F32)
-    *sent, ohi, oht, ohh, coef, value, scale, right, first, own = call(
+    onehots = [(BS, 4 * IFC), (BS, E), (BS, E)]
+    *sent, coef, value, scale, right, first, own = call(
         begin_kernel,
-        [shape(8, BS)] * 4
-        + [shape(BS, 4 * IFC, dtype=BF16), shape(BS, E, dtype=BF16), shape(BS, E, dtype=BF16), shape(1, 4 * IFC)]
-        + [FIELD] * 4
-        + [shape(8, BS)],
+        [shape(8, BS)] * 4 + [shape(1, 4 * IFC)] + [FIELD] * 4 + [shape(8, BS)],
         (rhs, cond, blk_diag, idx, cnt, coup, nodes),
         "begin",
-        scratch=[blocks],
-        smem=(4,),
+        scratch=[pltpu.VMEM(dims, BF16) for dims in onehots]
+        + [blocks]
+        + [pltpu.VMEM(part.shape, part.dtype) for part in (rhs, cond, blk_diag, idx)]
+        + [pltpu.SMEM(cnt.shape, cnt.dtype)]
+        + [pltpu.VMEM(part.shape, part.dtype) for part in (coup, nodes)]
+        + [pltpu.SemaphoreType.DMA((7,))],
+        space=pltpu.HBM,
+        limit=BEGIN_LIMIT,
     )
     arrived = exchange(sent)
-    (weights,) = call(
-        weight_kernel, [shape(EB, 3 * BS, 2 * BS, dtype=BF16)], (blk_diag, blk_off), "weights", flops=10**7
+    weights, ohi, oht, ohh = call(
+        weight_kernel,
+        [shape(EB, 3 * BS, 2 * BS, dtype=BF16)] + [shape(*dims, dtype=BF16) for dims in onehots],
+        (blk_diag, blk_off, idx, nodes),
+        "weights",
+        flops=10**7,
     )
 
     def local(field):
@@ -495,8 +517,8 @@
             "restrict",
         )
         arrived = exchange(sent)
-        (y,) = call(node_kernel, [shape(4, BS)], (*arrived, own, ninv), "node")
-        arrived = exchange([y] * 4)
+        *sent, y = call(node_kernel, MESSAGES + [shape(4, BS)], (*arrived, own, ninv), "node")
+        arrived = exchange(sent)
         *sent, direction = call(
             prolong_kernel,
             MESSAGES + [FIELD],

time: 204 us -> 180 us (0.88)
  waiting for transfers between devices: 22.8 us -> 7.22 us
  starting transfers between devices: 132 us -> 126 us
  local copies, waits for them, and re-layouts: 8.33 us -> 5.8 us
    ppermute x40, waiting for transfers between devices: 22.8 us -> 7.22 us  [exchange(): lax.ppermute(message, *pairs)]
    ppermute x40, starting transfers between devices: 132 us -> 126 us  [exchange(): lax.ppermute(message, *pairs)]
    unnamed x22, local copies, waits for them, and re-layouts: 7.81 us -> 5.27 us
where the time goes in v2:
time: 180 us; the launch traced here: 179 us
  starting transfers between devices  126 us (70%)
  blocking collectives  26.7 us (15%)
  Pallas kernels  11.8 us (7%)
  waiting for transfers between devices  7.22 us (4%)
  local copies, waits for them, and re-layouts  5.8 us (3%)
    ppermute x40, starting transfers between devices, exchange(): lax.ppermute(message, *pairs)  126 us
    all_to_all x2, blocking collectives, everywhere(): return lax.all_to_all(row, axis, 0, 0)  26.7 us
    pallas_call x19, Pallas kernels, call(): pl.pallas_call(body, out_shape=outs, in_specs=specs, out_specs=[pl.BlockS...  11.8 us
    ppermute x40, waiting for transfers between devices, exchange(): lax.ppermute(message, *pairs)  7.22 us
    unnamed x22, local copies, waits for them, and re-layouts  5.27 us
  transfers between devices with their start and end apart: 40, of which 9 were waited for; matrix products, arithmetic and copies ran while one was open for 0% of the time, Pallas kernels for 2%

profile of v2, /device:TPU:1, one launch (start us, length us, event | category | flops | bytes accessed | tf_op | source)
XLA Modules:
  0.0 178.6 jit_solution(12202207858626989979)
XLA Ops:
  0.6 2.6 %begin.1 = (f32[8,128]{1,0:T(8,128)}, f32[8,128]{1,0:T(8,128)}, f32[8,128]{1,0:T(8,128)}, f32[8,128]{1,0:T(8,128)}, f32[1,1024]{1,0:T(1,128)}, /*index=5*/f32[32...) custom-call(f32[2,1,1,2048]{3,2,1,0:T(1,128)} %rhs_ref.1, ...), custom_call_target="tpu_custom_call" | custom-call | bytes 1097744 | tf_op jit(solution)/shard_map/begin/pallas_call | solution.py:429
  3.3 8.1 %collective-permute-start = (f32[8,128]{1,0:T(8,128)}, f32[8,128]{1,0:T(8,128)S(1)}, u32[]{:S(2)}, u32[]{:S(2)}) collective-permute-start(f32[8,128]{1,0:T(8,128)} %get-tuple-element.69), channel_id=1, source_target_pairs={{1,2},{3,4},{5,6},{7,8},{9,10},{11,12},{13,14},{15,16},{17,18},{19... | collective-permute-start | bytes 12296 | tf_op jit(solution)/shard_map/ppermute | solution.py:453
  13.3 4.8 %collective-permute-start.2 = (f32[8,128]{1,0:T(8,128)}, f32[8,128]{1,0:T(8,128)S(1)}, u32[]{:S(2)}, u32[]{:S(2)}) collective-permute-start(f32[8,128]{1,0:T(8,128)} %get-tuple-element.71), channel_id=1, source_target_pairs={{32,64},{96,128},{160,192},{224,256},{288,320},{352,384},{416,448}... | collective-permute-start | bytes 12296 | tf_op jit(solution)/shard_map/ppermute | solution.py:453
  27.6 4.3 %collective-permute-start.4 = (f32[4,128]{1,0:T(4,128)S(1)}, f32[4,128]{1,0:T(4,128)S(1)}, u32[]{:S(2)}, u32[]{:S(2)}) collective-permute-start(f32[4,128]{1,0:T(4,128)S(1)} %get-tuple-element.81), channel_id=1, source_target_pairs={{1,2},{3,4},{5,6},{7,8},{9,10},{11,12},{13,14},{15,16},{17,18},{19... | collective-permute-start | bytes 6152 | tf_op jit(solution)/shard_map/ppermute | solution.py:453
  31.9 1.9 %collective-permute-start.5 = (f32[4,128]{1,0:T(4,128)S(1)}, f32[4,128]{1,0:T(4,128)S(1)}, u32[]{:S(2)}, u32[]{:S(2)}) collective-permute-start(f32[4,128]{1,0:T(4,128)S(1)} %get-tuple-element.82), channel_id=1, source_target_pairs={{0,1},{2,3},{4,5},{6,7},{8,9},{10,11},{12,13},{14,15},{16,17},{18,... | collective-permute-start | bytes 6152 | tf_op jit(solution)/shard_map/ppermute | solution.py:453
  33.9 4.7 %collective-permute-start.6 = (f32[4,128]{1,0:T(4,128)S(1)}, f32[4,128]{1,0:T(4,128)S(1)}, u32[]{:S(2)}, u32[]{:S(2)}) collective-permute-start(f32[4,128]{1,0:T(4,128)S(1)} %get-tuple-element.83), channel_id=1, source_target_pairs={{32,64},{96,128},{160,192},{224,256},{288,320},{352,384},{416,448}... | collective-permute-start | bytes 6152 | tf_op jit(solution)/shard_map/ppermute | solution.py:453
  42.2 4.3 %collective-permute-start.8 = (f32[4,128]{1,0:T(4,128)S(1)}, f32[4,128]{1,0:T(4,128)S(1)}, u32[]{:S(2)}, u32[]{:S(2)}) collective-permute-start(f32[4,128]{1,0:T(4,128)S(1)} %get-tuple-element.88), channel_id=1, source_target_pairs={{1,2},{3,4},{5,6},{7,8},{9,10},{11,12},{13,14},{15,16},{17,18},{19... | collective-permute-start | bytes 6152 | tf_op jit(solution)/shard_map/ppermute | solution.py:453
  48.5 4.3 %collective-permute-start.10 = (f32[4,128]{1,0:T(4,128)S(1)}, f32[4,128]{1,0:T(4,128)S(1)}, u32[]{:S(2)}, u32[]{:S(2)}) collective-permute-start(f32[4,128]{1,0:T(4,128)S(1)} %get-tuple-element.90), channel_id=1, source_target_pairs={{32,64},{96,128},{160,192},{224,256},{288,320},{352,384},{416,448}... | collective-permute-start | bytes 6152 | tf_op jit(solution)/shard_map/ppermute | solution.py:453
  55.9 4.3 %collective-permute-start.12 = (f32[4,128]{1,0:T(4,128)S(1)}, f32[4,128]{1,0:T(4,128)S(1)}, u32[]{:S(2)}, u32[]{:S(2)}) collective-permute-start(f32[4,128]{1,0:T(4,128)S(1)} %get-tuple-element.94), channel_id=1, source_target_pairs={{1,2},{3,4},{5,6},{7,8},{9,10},{11,12},{13,14},{15,16},{17,18},{19... | collective-permute-start | bytes 6152 | tf_op jit(solution)/shard_map/ppermute | solution.py:453
  62.1 5.6 %collective-permute-start.14 = (f32[4,128]{1,0:T(4,128)S(1)}, f32[4,128]{1,0:T(4,128)S(1)}, u32[]{:S(2)}, u32[]{:S(2)}) collective-permute-start(f32[4,128]{1,0:T(4,128)S(1)} %get-tuple-element.96), channel_id=1, source_target_pairs={{32,64},{96,128},{160,192},{224,256},{288,320},{352,384},{416,448}... | collective-permute-start | bytes 6152 | tf_op jit(solution)/shard_map/ppermute | solution.py:453
  71.3 4.3 %collective-permute-start.16 = (f32[4,128]{1,0:T(4,128)S(1)}, f32[4,128]{1,0:T(4,128)S(1)}, u32[]{:S(2)}, u32[]{:S(2)}) collective-permute-start(f32[4,128]{1,0:T(4,128)S(1)} %get-tuple-element.99), channel_id=1, source_target_pairs={{1,2},{3,4},{5,6},{7,8},{9,10},{11,12},{13,14},{15,16},{17,18},{19... | collective-permute-start | bytes 6152 | tf_op jit(solution)/shard_map/ppermute | solution.py:453
  77.5 3.4 %collective-permute-start.18 = (f32[4,128]{1,0:T(4,128)S(1)}, f32[4,128]{1,0:T(4,128)S(1)}, u32[]{:S(2)}, u32[]{:S(2)}) collective-permute-start(f32[4,128]{1,0:T(4,128)S(1)} %get-tuple-element.101), channel_id=1, source_target_pairs={{32,64},{96,128},{160,192},{224,256},{288,320},{352,384},{416,448}... | collective-permute-start | bytes 6152 | tf_op jit(solution)/shard_map/ppermute | solution.py:453
  84.4 4.3 %collective-permute-start.20 = (f32[4,128]{1,0:T(4,128)S(1)}, f32[4,128]{1,0:T(4,128)S(1)}, u32[]{:S(2)}, u32[]{:S(2)}) collective-permute-start(f32[4,128]{1,0:T(4,128)S(1)} %get-tuple-element.104), channel_id=1, source_target_pairs={{1,2},{3,4},{5,6},{7,8},{9,10},{11,12},{13,14},{15,16},{17,18},{19... | collective-permute-start | bytes 6152 | tf_op jit(solution)/shard_map/ppermute | solution.py:453
  90.7 3.4 %collective-permute-start.22 = (f32[4,128]{1,0:T(4,128)S(1)}, f32[4,128]{1,0:T(4,128)S(1)}, u32[]{:S(2)}, u32[]{:S(2)}) collective-permute-start(f32[4,128]{1,0:T(4,128)S(1)} %get-tuple-element.106), channel_id=1, source_target_pairs={{32,64},{96,128},{160,192},{224,256},{288,320},{352,384},{416,448}... | collective-permute-start | bytes 6152 | tf_op jit(solution)/shard_map/ppermute | solution.py:453
  97.7 4.3 %collective-permute-start.24 = (f32[4,128]{1,0:T(4,128)S(1)}, f32[4,128]{1,0:T(4,128)S(1)}, u32[]{:S(2)}, u32[]{:S(2)}) collective-permute-start(f32[4,128]{1,0:T(4,128)S(1)} %get-tuple-element.110), channel_id=1, source_target_pairs={{1,2},{3,4},{5,6},{7,8},{9,10},{11,12},{13,14},{15,16},{17,18},{19... | collective-permute-start | bytes 6152 | tf_op jit(solution)/shard_map/ppermute | solution.py:453
  103.9 3.6 %collective-permute-start.26 = (f32[4,128]{1,0:T(4,128)S(1)}, f32[4,128]{1,0:T(4,128)S(1)}, u32[]{:S(2)}, u32[]{:S(2)}) collective-permute-start(f32[4,128]{1,0:T(4,128)S(1)} %get-tuple-element.112), channel_id=1, source_target_pairs={{32,64},{96,128},{160,192},{224,256},{288,320},{352,384},{416,448}... | collective-permute-start | bytes 6152 | tf_op jit(solution)/shard_map/ppermute | solution.py:453
  111.3 4.3 %collective-permute-start.28 = (f32[4,128]{1,0:T(4,128)S(1)}, f32[4,128]{1,0:T(4,128)S(1)}, u32[]{:S(2)}, u32[]{:S(2)}) collective-permute-start(f32[4,128]{1,0:T(4,128)S(1)} %get-tuple-element.115), channel_id=1, source_target_pairs={{1,2},{3,4},{5,6},{7,8},{9,10},{11,12},{13,14},{15,16},{17,18},{19... | collective-permute-start | bytes 6152 | tf_op jit(solution)/shard_map/ppermute | solution.py:453
  117.5 3.4 %collective-permute-start.30 = (f32[4,128]{1,0:T(4,128)S(1)}, f32[4,128]{1,0:T(4,128)S(1)}, u32[]{:S(2)}, u32[]{:S(2)}) collective-permute-start(f32[4,128]{1,0:T(4,128)S(1)} %get-tuple-element.117), channel_id=1, source_target_pairs={{32,64},{96,128},{160,192},{224,256},{288,320},{352,384},{416,448}... | collective-permute-start | bytes 6152 | tf_op jit(solution)/shard_map/ppermute | solution.py:453
  124.0 4.3 %collective-permute-start.32 = (f32[4,128]{1,0:T(4,128)S(1)}, f32[4,128]{1,0:T(4,128)S(1)}, u32[]{:S(2)}, u32[]{:S(2)}) collective-permute-start(f32[4,128]{1,0:T(4,128)S(1)} %get-tuple-element.120), channel_id=1, source_target_pairs={{1,2},{3,4},{5,6},{7,8},{9,10},{11,12},{13,14},{15,16},{17,18},{19... | collective-permute-start | bytes 6152 | tf_op jit(solution)/shard_map/ppermute | solution.py:453
  130.2 3.6 %collective-permute-start.34 = (f32[4,128]{1,0:T(4,128)S(1)}, f32[4,128]{1,0:T(4,128)S(1)}, u32[]{:S(2)}, u32[]{:S(2)}) collective-permute-start(f32[4,128]{1,0:T(4,128)S(1)} %get-tuple-element.122), channel_id=1, source_target_pairs={{32,64},{96,128},{160,192},{224,256},{288,320},{352,384},{416,448}... | collective-permute-start | bytes 6152 | tf_op jit(solution)/shard_map/ppermute | solution.py:453
  137.5 4.3 %collective-permute-start.36 = (f32[4,128]{1,0:T(4,128)S(1)}, f32[4,128]{1,0:T(4,128)S(1)}, u32[]{:S(2)}, u32[]{:S(2)}) collective-permute-start(f32[4,128]{1,0:T(4,128)S(1)} %get-tuple-element.125), channel_id=1, source_target_pairs={{1,2},{3,4},{5,6},{7,8},{9,10},{11,12},{13,14},{15,16},{17,18},{19... | collective-permute-start | bytes 6152 | tf_op jit(solution)/shard_map/ppermute | solution.py:453
  143.7 3.4 %collective-permute-start.38 = (f32[4,128]{1,0:T(4,128)S(1)}, f32[4,128]{1,0:T(4,128)S(1)}, u32[]{:S(2)}, u32[]{:S(2)}) collective-permute-start(f32[4,128]{1,0:T(4,128)S(1)} %get-tuple-element.127), channel_id=1, source_target_pairs={{32,64},{96,128},{160,192},{224,256},{288,320},{352,384},{416,448}... | collective-permute-start | bytes 6152 | tf_op jit(solution)/shard_map/ppermute | solution.py:453
  150.5 12.8 %all_to_all.10 = f32[16,1,128]{2,1,0:T(1,128)S(1)} all-to-all(f32[16,1,128]{2,1,0:T(1,128)S(1)} %get-tuple-element.130), channel_id=1, replica_groups=mesh['lat'=16,'lon'=32] {'lat'}, dimensions={0} | all-to-all | bytes 16384 | tf_op jit(solution)/shard_map/all_to_all | solution.py:457
  163.4 13.9 %all_to_all.11.sums_ref = f32[32,1,128]{2,1,0:T(1,128)S(1)} all-to-all(f32[32,1,128]{2,1,0:T(1,128)S(1)} %broadcast_in_dim.2), channel_id=1, replica_groups=mesh['lat'=16,'lon'=32] {'lon'}, dimensions={0} | all-to-all | bytes 32768 | tf_op jit(solution)/shard_map/all_to_all | solution.py:457
  (102 shorter events, 58.7 us)
Async XLA Ops:
  3.3 23.7 %collective-permute-start = (f32[8,128]{1,0:T(8,128)}, f32[8,128]{1,0:T(8,128)S(1)}, u32[]{:S(2)}, u32[]{:S(2)}) collective-permute-start(f32[8,128]{1,0:T(8,128)} %get-tuple-element.69), channel_id=1, source_target_pairs={{1,2},{3,4},{5,6},{7,8},{9,10},{11,12},{13,14},{15,16},{17,18},{19... | collective-permute-start | bytes 12296 | tf_op jit(solution)/shard_map/ppermute | solution.py:453
  11.4 15.6 %collective-permute-start.1 = (f32[8,128]{1,0:T(8,128)}, f32[8,128]{1,0:T(8,128)S(1)}, u32[]{:S(2)}, u32[]{:S(2)}) collective-permute-start(f32[8,128]{1,0:T(8,128)} %get-tuple-element.70), channel_id=1, source_target_pairs={{0,1},{2,3},{4,5},{6,7},{8,9},{10,11},{12,13},{14,15},{16,17},{18,... | collective-permute-start | bytes 12296 | tf_op jit(solution)/shard_map/ppermute | solution.py:453
  13.3 13.7 %collective-permute-start.2 = (f32[8,128]{1,0:T(8,128)}, f32[8,128]{1,0:T(8,128)S(1)}, u32[]{:S(2)}, u32[]{:S(2)}) collective-permute-start(f32[8,128]{1,0:T(8,128)} %get-tuple-element.71), channel_id=1, source_target_pairs={{32,64},{96,128},{160,192},{224,256},{288,320},{352,384},{416,448}... | collective-permute-start | bytes 12296 | tf_op jit(solution)/shard_map/ppermute | solution.py:453
  18.2 8.9 %collective-permute-start.3 = (f32[8,128]{1,0:T(8,128)}, f32[8,128]{1,0:T(8,128)S(1)}, u32[]{:S(2)}, u32[]{:S(2)}) collective-permute-start(f32[8,128]{1,0:T(8,128)} %get-tuple-element.72), channel_id=1, source_target_pairs={{0,32},{64,96},{128,160},{192,224},{256,288},{320,352},{384,416},{... | collective-permute-start | bytes 12296 | tf_op jit(solution)/shard_map/ppermute | solution.py:453
  27.6 13.4 %collective-permute-start.4 = (f32[4,128]{1,0:T(4,128)S(1)}, f32[4,128]{1,0:T(4,128)S(1)}, u32[]{:S(2)}, u32[]{:S(2)}) collective-permute-start(f32[4,128]{1,0:T(4,128)S(1)} %get-tuple-element.81), channel_id=1, source_target_pairs={{1,2},{3,4},{5,6},{7,8},{9,10},{11,12},{13,14},{15,16},{17,18},{19... | collective-permute-start | bytes 6152 | tf_op jit(solution)/shard_map/ppermute | solution.py:453
  31.9 9.1 %collective-permute-start.5 = (f32[4,128]{1,0:T(4,128)S(1)}, f32[4,128]{1,0:T(4,128)S(1)}, u32[]{:S(2)}, u32[]{:S(2)}) collective-permute-start(f32[4,128]{1,0:T(4,128)S(1)} %get-tuple-element.82), channel_id=1, source_target_pairs={{0,1},{2,3},{4,5},{6,7},{8,9},{10,11},{12,13},{14,15},{16,17},{18,... | collective-permute-start | bytes 6152 | tf_op jit(solution)/shard_map/ppermute | solution.py:453
  33.9 7.2 %collective-permute-start.6 = (f32[4,128]{1,0:T(4,128)S(1)}, f32[4,128]{1,0:T(4,128)S(1)}, u32[]{:S(2)}, u32[]{:S(2)}) collective-permute-start(f32[4,128]{1,0:T(4,128)S(1)} %get-tuple-element.83), channel_id=1, source_target_pairs={{32,64},{96,128},{160,192},{224,256},{288,320},{352,384},{416,448}... | collective-permute-start | bytes 6152 | tf_op jit(solution)/shard_map/ppermute | solution.py:453
  42.2 12.5 %collective-permute-start.8 = (f32[4,128]{1,0:T(4,128)S(1)}, f32[4,128]{1,0:T(4,128)S(1)}, u32[]{:S(2)}, u32[]{:S(2)}) collective-permute-start(f32[4,128]{1,0:T(4,128)S(1)} %get-tuple-element.88), channel_id=1, source_target_pairs={{1,2},{3,4},{5,6},{7,8},{9,10},{11,12},{13,14},{15,16},{17,18},{19... | collective-permute-start | bytes 6152 | tf_op jit(solution)/shard_map/ppermute | solution.py:453
  46.5 8.2 %collective-permute-start.9 = (f32[4,128]{1,0:T(4,128)S(1)}, f32[4,128]{1,0:T(4,128)S(1)}, u32[]{:S(2)}, u32[]{:S(2)}) collective-permute-start(f32[4,128]{1,0:T(4,128)S(1)} %get-tuple-element.89), channel_id=1, source_target_pairs={{0,1},{2,3},{4,5},{6,7},{8,9},{10,11},{12,13},{14,15},{16,17},{18,... | collective-permute-start | bytes 6152 | tf_op jit(solution)/shard_map/ppermute | solution.py:453
  55.9 13.7 %collective-permute-start.12 = (f32[4,128]{1,0:T(4,128)S(1)}, f32[4,128]{1,0:T(4,128)S(1)}, u32[]{:S(2)}, u32[]{:S(2)}) collective-permute-start(f32[4,128]{1,0:T(4,128)S(1)} %get-tuple-element.94), channel_id=1, source_target_pairs={{1,2},{3,4},{5,6},{7,8},{9,10},{11,12},{13,14},{15,16},{17,18},{19... | collective-permute-start | bytes 6152 | tf_op jit(solution)/shard_map/ppermute | solution.py:453
  60.2 9.4 %collective-permute-start.13 = (f32[4,128]{1,0:T(4,128)S(1)}, f32[4,128]{1,0:T(4,128)S(1)}, u32[]{:S(2)}, u32[]{:S(2)}) collective-permute-start(f32[4,128]{1,0:T(4,128)S(1)} %get-tuple-element.95), channel_id=1, source_target_pairs={{0,1},{2,3},{4,5},{6,7},{8,9},{10,11},{12,13},{14,15},{16,17},{18,... | collective-permute-start | bytes 6152 | tf_op jit(solution)/shard_map/ppermute | solution.py:453
  62.1 7.5 %collective-permute-start.14 = (f32[4,128]{1,0:T(4,128)S(1)}, f32[4,128]{1,0:T(4,128)S(1)}, u32[]{:S(2)}, u32[]{:S(2)}) collective-permute-start(f32[4,128]{1,0:T(4,128)S(1)} %get-tuple-element.96), channel_id=1, source_target_pairs={{32,64},{96,128},{160,192},{224,256},{288,320},{352,384},{416,448}... | collective-permute-start | bytes 6152 | tf_op jit(solution)/shard_map/ppermute | solution.py:453
  71.3 12.1 %collective-permute-start.16 = (f32[4,128]{1,0:T(4,128)S(1)}, f32[4,128]{1,0:T(4,128)S(1)}, u32[]{:S(2)}, u32[]{:S(2)}) collective-permute-start(f32[4,128]{1,0:T(4,128)S(1)} %get-tuple-element.99), channel_id=1, source_target_pairs={{1,2},{3,4},{5,6},{7,8},{9,10},{11,12},{13,14},{15,16},{17,18},{19... | collective-permute-start | bytes 6152 | tf_op jit(solution)/shard_map/ppermute | solution.py:453
  75.6 7.8 %collective-permute-start.17 = (f32[4,128]{1,0:T(4,128)S(1)}, f32[4,128]{1,0:T(4,128)S(1)}, u32[]{:S(2)}, u32[]{:S(2)}) collective-permute-start(f32[4,128]{1,0:T(4,128)S(1)} %get-tuple-element.100), channel_id=1, source_target_pairs={{0,1},{2,3},{4,5},{6,7},{8,9},{10,11},{12,13},{14,15},{16,17},{18,... | collective-permute-start | bytes 6152 | tf_op jit(solution)/shard_map/ppermute | solution.py:453
  84.4 12.2 %collective-permute-start.20 = (f32[4,128]{1,0:T(4,128)S(1)}, f32[4,128]{1,0:T(4,128)S(1)}, u32[]{:S(2)}, u32[]{:S(2)}) collective-permute-start(f32[4,128]{1,0:T(4,128)S(1)} %get-tuple-element.104), channel_id=1, source_target_pairs={{1,2},{3,4},{5,6},{7,8},{9,10},{11,12},{13,14},{15,16},{17,18},{19... | collective-permute-start | bytes 6152 | tf_op jit(solution)/shard_map/ppermute | solution.py:453
  88.7 7.9 %collective-permute-start.21 = (f32[4,128]{1,0:T(4,128)S(1)}, f32[4,128]{1,0:T(4,128)S(1)}, u32[]{:S(2)}, u32[]{:S(2)}) collective-permute-start(f32[4,128]{1,0:T(4,128)S(1)} %get-tuple-element.105), channel_id=1, source_target_pairs={{0,1},{2,3},{4,5},{6,7},{8,9},{10,11},{12,13},{14,15},{16,17},{18,... | collective-permute-start | bytes 6152 | tf_op jit(solution)/shard_map/ppermute | solution.py:453
  97.7 12.3 %collective-permute-start.24 = (f32[4,128]{1,0:T(4,128)S(1)}, f32[4,128]{1,0:T(4,128)S(1)}, u32[]{:S(2)}, u32[]{:S(2)}) collective-permute-start(f32[4,128]{1,0:T(4,128)S(1)} %get-tuple-element.110), channel_id=1, source_target_pairs={{1,2},{3,4},{5,6},{7,8},{9,10},{11,12},{13,14},{15,16},{17,18},{19... | collective-permute-start | bytes 6152 | tf_op jit(solution)/shard_map/ppermute | solution.py:453
  102.0 8.0 %collective-permute-start.25 = (f32[4,128]{1,0:T(4,128)S(1)}, f32[4,128]{1,0:T(4,128)S(1)}, u32[]{:S(2)}, u32[]{:S(2)}) collective-permute-start(f32[4,128]{1,0:T(4,128)S(1)} %get-tuple-element.111), channel_id=1, source_target_pairs={{0,1},{2,3},{4,5},{6,7},{8,9},{10,11},{12,13},{14,15},{16,17},{18,... | collective-permute-start | bytes 6152 | tf_op jit(solution)/shard_map/ppermute | solution.py:453
  111.3 11.6 %collective-permute-start.28 = (f32[4,128]{1,0:T(4,128)S(1)}, f32[4,128]{1,0:T(4,128)S(1)}, u32[]{:S(2)}, u32[]{:S(2)}) collective-permute-start(f32[4,128]{1,0:T(4,128)S(1)} %get-tuple-element.115), channel_id=1, source_target_pairs={{1,2},{3,4},{5,6},{7,8},{9,10},{11,12},{13,14},{15,16},{17,18},{19... | collective-permute-start | bytes 6152 | tf_op jit(solution)/shard_map/ppermute | solution.py:453
  115.6 7.3 %collective-permute-start.29 = (f32[4,128]{1,0:T(4,128)S(1)}, f32[4,128]{1,0:T(4,128)S(1)}, u32[]{:S(2)}, u32[]{:S(2)}) collective-permute-start(f32[4,128]{1,0:T(4,128)S(1)} %get-tuple-element.116), channel_id=1, source_target_pairs={{0,1},{2,3},{4,5},{6,7},{8,9},{10,11},{12,13},{14,15},{16,17},{18,... | collective-permute-start | bytes 6152 | tf_op jit(solution)/shard_map/ppermute | solution.py:453
  124.0 11.8 %collective-permute-start.32 = (f32[4,128]{1,0:T(4,128)S(1)}, f32[4,128]{1,0:T(4,128)S(1)}, u32[]{:S(2)}, u32[]{:S(2)}) collective-permute-start(f32[4,128]{1,0:T(4,128)S(1)} %get-tuple-element.120), channel_id=1, source_target_pairs={{1,2},{3,4},{5,6},{7,8},{9,10},{11,12},{13,14},{15,16},{17,18},{19... | collective-permute-start | bytes 6152 | tf_op jit(solution)/shard_map/ppermute | solution.py:453
  128.3 7.5 %collective-permute-start.33 = (f32[4,128]{1,0:T(4,128)S(1)}, f32[4,128]{1,0:T(4,128)S(1)}, u32[]{:S(2)}, u32[]{:S(2)}) collective-permute-start(f32[4,128]{1,0:T(4,128)S(1)} %get-tuple-element.121), channel_id=1, source_target_pairs={{0,1},{2,3},{4,5},{6,7},{8,9},{10,11},{12,13},{14,15},{16,17},{18,... | collective-permute-start | bytes 6152 | tf_op jit(solution)/shard_map/ppermute | solution.py:453
  137.5 12.2 %collective-permute-start.36 = (f32[4,128]{1,0:T(4,128)S(1)}, f32[4,128]{1,0:T(4,128)S(1)}, u32[]{:S(2)}, u32[]{:S(2)}) collective-permute-start(f32[4,128]{1,0:T(4,128)S(1)} %get-tuple-element.125), channel_id=1, source_target_pairs={{1,2},{3,4},{5,6},{7,8},{9,10},{11,12},{13,14},{15,16},{17,18},{19... | collective-permute-start | bytes 6152 | tf_op jit(solution)/shard_map/ppermute | solution.py:453
  141.8 7.8 %collective-permute-start.37 = (f32[4,128]{1,0:T(4,128)S(1)}, f32[4,128]{1,0:T(4,128)S(1)}, u32[]{:S(2)}, u32[]{:S(2)}) collective-permute-start(f32[4,128]{1,0:T(4,128)S(1)} %get-tuple-element.126), channel_id=1, source_target_pairs={{0,1},{2,3},{4,5},{6,7},{8,9},{10,11},{12,13},{14,15},{16,17},{18,... | collective-permute-start | bytes 6152 | tf_op jit(solution)/shard_map/ppermute | solution.py:453
  (27 other events, 123.5 us)

commit v3 on v2

--- a/solution.py
+++ b/solution.py
@@ -1,3 +1,5 @@
+import functools
+
 import jax
 import jax.numpy as jnp
 from jax import lax
@@ -161,20 +163,16 @@
     ref[EB : 2 * EB] = value[1]
 
 
-def nodal(rows, onehot_head, onehot_tail, nodes_ref, sign, out_refs, own_ref, at):
+def nodal(rows, onehot_head, onehot_tail, nodes_ref, sign):
     tails = nodes_ref[0, 0, 0:1]
     heads = nodes_ref[0, 0, 1:2]
     own = put_heads(rows, onehot_head, heads // BS)
     ext = put(rows, onehot_tail, block_mask(tails // BS, EB))
-    ext = [sign * ext[0], sign * ext[1]]
-    own_ref[...] = own
-    for c in range(2):
-        own_ref[2 * c : 2 * c + 2] += ext[c][0:2]
-    towards = [
-        jnp.concatenate([ext[0][2 * d : 2 * d + 2], ext[1][2 * d : 2 * d + 2]], axis=0)
-        for d in range(1, 5)
+    parts = [
+        sign * jnp.concatenate([ext[0][2 * d : 2 * d + 2], ext[1][2 * d : 2 * d + 2]], axis=0)
+        for d in range(5)
     ]
-    hand_out(out_refs, towards, at)
+    return own[0:4] + parts[0], parts[1:]
 
 
 def begin_kernel(
@@ -217,7 +215,11 @@
     keep(first_ref, first)
     hand_out(messages, interface_messages(first, ohi_ref, index), 0)
     rows = [lanes(value[c], EB) for c in range(2)]
-    nodal(rows, ohh_ref, oht_ref, nodes_ref, 1.0, messages, own_ref, 4)
+    own, towards = nodal(rows, ohh_ref, oht_ref, nodes_ref, 1.0)
+    own_ref[0:4] = own
+    hand_out(messages, towards, 4)
+    ends = [to_blocks(nodes_ref[0, 0, k : k + 1].astype(F32), blocks) for k in (1, 0)]
+    hand_out(messages, interface_messages(ends, ohi_ref, index), 8)
 
 
 def weight_kernel(diag_ref, off_ref, idx_ref, nodes_ref, w_ref, ohi_ref, oht_ref, ohh_ref):
@@ -278,7 +280,7 @@
 
 def smooth_first_kernel(
     a0, a1, a2, a3, own_ref, ohi_ref, coef_ref, idx_ref, first_ref, local_ref, scale_ref, right_ref,
-    m0, m1, m2, m3, second_ref, ninv_ref,
+    m0, m1, m2, m3, second_ref, ninv_ref, ends_ref, away_ref,
 ):
     arrived = collect((a0, a1, a2, a3))
     smooth(arrived, ohi_ref, coef_ref, idx_ref, first_ref, local_ref, scale_ref, right_ref, (m0, m1, m2, m3), second_ref)
@@ -288,6 +290,13 @@
     inverse = complex_inverse((sums[0:2], sums[2:4]))
     ninv_ref[0:2] = inverse[0]
     ninv_ref[2:4] = inverse[1]
+    for d, part in enumerate(collect((a0, a1, a2, a3), 8)):
+        for k in range(2):
+            row = jnp.concatenate([part[2 * k : 2 * k + 1], part[2 * k + 1 : 2 * k + 2]], axis=1)
+            row = row.astype(jnp.int32)
+            at = (2 * d + k) * IFC
+            ends_ref[:, at : at + IFC] = row
+            away_ref[:, at : at + IFC] = lane_onehot(row)
 
 
 def smooth_kernel(
@@ -300,58 +309,112 @@
 
 def restrict_kernel(
     a0, a1, a2, a3, ohi_ref, oht_ref, ohh_ref, coef_ref, idx_ref, nodes_ref, local_ref, right_ref,
-    m0, m1, m2, m3, own_ref,
+    far_ref, core_ref, row_ref, extra_ref,
 ):
     index = index_rows(idx_ref)
     extra = interface_sum(collect((a0, a1, a2, a3)), coef_ref[...], ohi_ref, index)
+    keep(extra_ref, extra)
     local, right = pair(local_ref), pair(right_ref)
     rows = [lanes(right[c] - local[c] - extra[c], EB) for c in range(2)]
-    nodal(rows, ohh_ref, oht_ref, nodes_ref, -1.0, (m0, m1, m2, m3), own_ref, 0)
-
-
-def node_kernel(a0, a1, a2, a3, own_ref, ninv_ref, m0, m1, m2, m3, y_ref):
-    sums = own_ref[0:4]
-    for part in collect((a0, a1, a2, a3)):
-        sums = sums + part
-    result = complex_times((ninv_ref[0:2], ninv_ref[2:4]), (sums[0:2], sums[2:4]))
-    for ref in (m0, m1, m2, m3, y_ref):
-        ref[0:2] = result[0]
-        ref[2:4] = result[1]
-
-
-def prolong_kernel(
-    a0, a1, a2, a3, y_ref, ohi_ref, oht_ref, ohh_ref, idx_ref, nodes_ref, second_ref,
-    m0, m1, m2, m3, direction_ref,
-    blocks, wide,
-):
-    tails = nodes_ref[0, 0, 0:1]
-    heads = nodes_ref[0, 0, 1:2]
-    wide[...] = jnp.zeros((2 * EB, BS), F32)
-    nodes = (y_ref[...],) + collect((a0, a1, a2, a3))
+    own, towards = nodal(rows, ohh_ref, oht_ref, nodes_ref, -1.0)
+    even_lat, _ = parities()
+    far_ref[...] = jnp.where(even_lat, towards[0], towards[1])
+    core_ref[...] = jnp.where(even_lat, towards[1], towards[0])
+    for k, part in enumerate((own, towards[2], towards[3])):
+        row_ref[4 * k : 4 * k + 4] = part
+
+
+def row_kernel(far_ref, core_ref, row_ref, *refs):
+    out_ref = refs[-1]
+    parts = [row_ref[0:4] + far_ref[...] + core_ref[...], row_ref[4:8], row_ref[8:12]]
+    parts += [ref[...] for ref in refs[:-1]]
+    out_ref[...] = jnp.broadcast_to(jnp.concatenate(parts, axis=0)[None], out_ref.shape)
+
+
+def column_kernel(known, lon, row_ref, *refs):
+    inverse_ref, near_ref, out_ref = refs if known else (refs[2], refs[0], refs[1])
+    me = lax.axis_index("lon")
+
+    def at(step):
+        return lax.rem(me + (lon + step), lon)
+
+    for k in range(5):
+        sums = row_ref[at(k - 2), 0:4] + row_ref[at(k - 1), 4:8] + row_ref[at(k - 3), 8:12]
+        if not known:
+            inverse_ref[4 * k : 4 * k + 4] = row_ref[at(k - 2), 12:16]
+        inverse = inverse_ref[4 * k : 4 * k + 4]
+        result = complex_times((inverse[0:2], inverse[2:4]), (sums[0:2], sums[2:4]))
+        near_ref[4 * k : 4 * k + 4] = jnp.concatenate(result, axis=0)
+    out_ref[...] = jnp.broadcast_to(near_ref[4:16][None], out_ref.shape)
+
+
+def extend(nodes, ref):
     for d in range(5):
         for c in range(2):
-            wide[EB * c + 2 * d : EB * c + 2 * d + 2] = nodes[d][2 * c : 2 * c + 2]
-    low = take(pair(wide), oht_ref, block_mask(tails // BS, EB))
-    own = jnp.concatenate([nodes[0], nodes[0]], axis=0)
-    high = take_heads(own, ohh_ref, heads // BS)
+            ref[EB * c + 2 * d : EB * c + 2 * d + 2] = nodes[d][2 * c : 2 * c + 2]
+    return pair(ref)
+
+
+def gradient(nodes, ref, onehot_head, onehot_tail, heads, tails):
+    low = take(extend(nodes, ref), onehot_tail, block_mask(tails // BS, EB))
+    high = take_heads(jnp.concatenate([nodes[0], nodes[0]], axis=0), onehot_head, heads // BS)
+    return [high[c] - low[c] for c in range(2)]
+
+
+def prolong(
+    lat, column_ref, near_ref, ohi_ref, oht_ref, ohh_ref, coef_ref, idx_ref, nodes_ref, second_ref, extra_ref,
+    ends_ref, away_ref, value_ref, w_ref, direction_ref, blocks, ext, wide, out,
+):
+    me = lax.axis_index("lat")
+
+    def node(down, right):
+        if down == 0:
+            return near_ref[4 * right + 8 : 4 * right + 12]
+        there = jnp.clip(me + down, 0, lat - 1)
+        return column_ref[there, 4 * right + 4 : 4 * right + 8]
+
+    def around(down, right):
+        steps = ((0, 0), (-1, 0), (1, 0), (0, -1), (0, 1))
+        return [node(down + i, right + j) for i, j in steps]
+
+    ext[...] = jnp.zeros((2 * EB, BS), F32)
+    rise = gradient(around(0, 0), ext, ohh_ref, oht_ref, nodes_ref[0, 0, 1:2], nodes_ref[0, 0, 0:1])
     second = pair(second_ref)
-    direction = [second[c] + to_blocks(high[c] - low[c], blocks) for c in range(2)]
+    direction = [second[c] + to_blocks(rise[c], blocks) for c in range(2)]
     keep(direction_ref, direction)
-    hand_out((m0, m1, m2, m3), interface_messages(direction, ohi_ref, index_rows(idx_ref)))
-
-
-def image_kernel(
-    a0, a1, a2, a3, ohi_ref, coef_ref, idx_ref, local_ref, scale_ref,
-    m0, m1, m2, m3, image_ref, first_ref,
-):
-    index = index_rows(idx_ref)
-    extra = interface_sum(collect((a0, a1, a2, a3)), coef_ref[...], ohi_ref, index)
-    local = pair(local_ref)
-    image = (local[0] + extra[0], local[1] + extra[1])
+    rises = []
+    for d, step in enumerate(((-1, 0), (1, 0), (0, -1), (0, 1))):
+        spots = [pl.ds((2 * d + k) * IFC, IFC) for k in range(2)]
+        rise = gradient(
+            around(*step), ext, away_ref.at[:, spots[0]], away_ref.at[:, spots[1]],
+            ends_ref[:, spots[0]], ends_ref[:, spots[1]],
+        )
+        if d < 2:
+            there = me + step[0]
+            real = (there >= 0) & (there < lat)
+            rise = [jnp.where(real, part, 0.0) for part in rise]
+        rises.append(rise)
+    rows = [jnp.concatenate([rise[c] for rise in rises], axis=1) * coef_ref[...] for c in range(2)]
+    more = put(rows, ohi_ref, block_mask(index_rows(idx_ref) // BS, EB))
+    extra = pair(extra_ref)
+    local = stiffness(direction, pair(value_ref), w_ref, wide, out)
+    return [local[c] + extra[c] + more[c] for c in range(2)]
+
+
+def prolong_first_kernel(
+    lat, column_ref, near_ref, ohi_ref, oht_ref, ohh_ref, coef_ref, idx_ref, nodes_ref, second_ref, extra_ref,
+    ends_ref, away_ref, value_ref, w_ref, scale_ref,
+    m0, m1, m2, m3, direction_ref, image_ref, first_ref,
+    *scratch,
+):
+    image = prolong(
+        lat, column_ref, near_ref, ohi_ref, oht_ref, ohh_ref, coef_ref, idx_ref, nodes_ref, second_ref, extra_ref,
+        ends_ref, away_ref, value_ref, w_ref, direction_ref, *scratch,
+    )
     keep(image_ref, image)
     first = complex_times(pair(scale_ref), image)
     keep(first_ref, first)
-    hand_out((m0, m1, m2, m3), interface_messages(first, ohi_ref, index))
+    hand_out((m0, m1, m2, m3), interface_messages(first, ohi_ref, index_rows(idx_ref)))
 
 
 def total(x):
@@ -362,14 +425,17 @@
     return total(a[0] * b[0] + a[1] * b[1]), total(a[0] * b[1] - a[1] * b[0])
 
 
-def sums_kernel(
-    a0, a1, a2, a3, ohi_ref, coef_ref, idx_ref, local_ref, right_ref, image_ref,
-    image2_ref, sums_ref,
-):
-    index = index_rows(idx_ref)
-    extra = interface_sum(collect((a0, a1, a2, a3)), coef_ref[...], ohi_ref, index)
-    local, right, image = pair(local_ref), pair(right_ref), pair(image_ref)
-    image2 = (local[0] + extra[0], local[1] + extra[1])
+def prolong_last_kernel(
+    lat, column_ref, near_ref, ohi_ref, oht_ref, ohh_ref, coef_ref, idx_ref, nodes_ref, second_ref, extra_ref,
+    ends_ref, away_ref, value_ref, w_ref, right_ref, image_ref,
+    direction_ref, image2_ref, sums_ref,
+    *scratch,
+):
+    image2 = prolong(
+        lat, column_ref, near_ref, ohi_ref, oht_ref, ohh_ref, coef_ref, idx_ref, nodes_ref, second_ref, extra_ref,
+        ends_ref, away_ref, value_ref, w_ref, direction_ref, *scratch,
+    )
+    right, image = pair(right_ref), pair(image_ref)
     keep(image2_ref, image2)
     rest = (right[0] - image[0], right[1] - image[1])
     turn = (image[0] - image2[0], image[1] - image2[1])
@@ -450,7 +516,7 @@
         ("lat", swap([(k, k + 1) for k in range(1, lat - 1, 2)])),
         ("lat", swap([(k, k + 1) for k in range(0, lat, 2)])),
     )
-    return [lax.ppermute(message, *pairs) for message, pairs in zip(messages, swaps)]
+    return [lax.ppermute(message, *pairs) for message, pairs in zip(messages, swaps[4 - len(messages) :])]
 
 
 def everywhere(row, axis):
@@ -464,7 +530,7 @@
     onehots = [(BS, 4 * IFC), (BS, E), (BS, E)]
     *sent, coef, value, scale, right, first, own = call(
         begin_kernel,
-        [shape(8, BS)] * 4 + [shape(1, 4 * IFC)] + [FIELD] * 4 + [shape(8, BS)],
+        [shape(12, BS)] * 4 + [shape(1, 4 * IFC)] + [FIELD] * 4 + [shape(4, BS)],
         (rhs, cond, blk_diag, idx, cnt, coup, nodes),
         "begin",
         scratch=[pltpu.VMEM(dims, BF16) for dims in onehots]
@@ -490,13 +556,15 @@
             local_kernel, [FIELD], (field, value, weights), "local", scratch=[wide, out], flops=2 * 8 * EB * 3 * BS * 2 * BS
         )[0]
 
-    images, directions = [], []
+    lat, lon = lax.axis_size("lat"), lax.axis_size("lon")
+    scratch = [blocks, pltpu.VMEM((2 * EB, BS), F32), wide, out]
+    directions = []
     for step in range(ITERS):
         stiff = local(first)
         if step == 0:
-            *sent, second, ninv = call(
+            *sent, second, ninv, ends, away = call(
                 smooth_first_kernel,
-                MESSAGES + [FIELD, shape(4, BS)],
+                MESSAGES + [FIELD, shape(4, BS), shape(1, 8 * IFC, dtype=jnp.int32), shape(BS, 8 * IFC, dtype=BF16)],
                 (*arrived, own, ohi, coef, idx, first, stiff, scale, right),
                 "smooth_first",
             )
@@ -510,40 +578,48 @@
             )
         arrived = exchange(sent)
         stiff = local(second)
-        *sent, own = call(
+        *sent, row, extra = call(
             restrict_kernel,
-            MESSAGES + [shape(8, BS)],
+            MESSAGES[:2] + [shape(12, BS), FIELD],
             (*arrived, ohi, oht, ohh, coef, idx, nodes, stiff, source),
             "restrict",
         )
         arrived = exchange(sent)
-        *sent, y = call(node_kernel, MESSAGES + [shape(4, BS)], (*arrived, own, ninv), "node")
-        arrived = exchange(sent)
-        *sent, direction = call(
-            prolong_kernel,
-            MESSAGES + [FIELD],
-            (*arrived, y, ohi, oht, ohh, idx, nodes, second),
-            "prolong",
-            scratch=[blocks, pltpu.VMEM((2 * EB, BS), F32)],
+        known = step > 0
+        (row,) = call(
+            row_kernel,
+            [shape(lon, 12 if known else 16, BS)],
+            (*arrived, row) + (() if known else (ninv,)),
+            "row",
         )
-        directions.append(direction)
-        arrived = exchange(sent)
-        stiff = local(direction)
+        near, column, *found = call(
+            functools.partial(column_kernel, known, lon),
+            [shape(20, BS), shape(lat, 12, BS)] + ([] if known else [shape(20, BS)]),
+            (everywhere(row, "lon"),) + ((inverses,) if known else ()),
+            "column",
+        )
+        column = everywhere(column, "lat")
+        args = (column, near, ohi, oht, ohh, coef, idx, nodes, second, extra, ends, away, value, weights)
         if step == 0:
-            *sent, image, first = call(
-                image_kernel,
-                MESSAGES + [FIELD, FIELD],
-                (*arrived, ohi, coef, idx, stiff, scale),
-                "image",
+            (inverses,) = found
+            *sent, direction, image, first = call(
+                functools.partial(prolong_first_kernel, lat),
+                MESSAGES + [FIELD] * 3,
+                args + (scale,),
+                "prolong_first",
+                scratch=scratch,
             )
             source = image
             arrived = exchange(sent)
-    image2, sums = call(
-        sums_kernel,
-        [FIELD, shape(lax.axis_size("lat"), 1, BS)],
-        (*arrived, ohi, coef, idx, stiff, right, image),
-        "sums",
-    )
+        else:
+            direction, image2, sums = call(
+                functools.partial(prolong_last_kernel, lat),
+                [FIELD, FIELD, shape(lat, 1, BS)],
+                args + (right, image),
+                "prolong_last",
+                scratch=scratch,
+            )
+        directions.append(direction)
     sums = jnp.sum(everywhere(sums, "lat"), axis=0, keepdims=True)
     sums = everywhere(jnp.broadcast_to(sums, (lax.axis_size("lon"), 1, BS)), "lon")
     solution, residual, history = call(

time: 180 us -> 176 us (0.978)
  starting transfers between devices: 126 us -> 61.7 us
  blocking collectives: 26.7 us -> 90.6 us
  waiting for transfers between devices: 7.22 us -> 3.94 us
    ppermute x40 -> x20, starting transfers between devices: 126 us -> 61.7 us  [exchange(): lax.ppermute(message, *pairs)]
    all_to_all x2 -> x6, blocking collectives: 26.7 us -> 90.6 us  [everywhere(): return lax.all_to_all(row, axis, 0, 0)]
    ppermute x40 -> x20, waiting for transfers between devices: 7.22 us -> 3.94 us  [exchange(): lax.ppermute(message, *pairs)]
    pallas_call x19 -> x17, Pallas kernels: 11.8 us -> 11.6 us  [call(): pl.pallas_call(body, out_shape=outs, in_specs=specs, out_specs=[pl.BlockS...]
  transfers between devices with their start and end apart: 40 -> 20, of which waited for: 9 -> 7; matrix products, arithmetic and copies ran while one was open for 0% -> 0% of each run, Pallas kernels for 2% -> 2%
where the time goes in v3:
time: 176 us; the launch traced here: 175 us
  blocking collectives  90.6 us (51%)
  starting transfers between devices  61.7 us (35%)
  Pallas kernels  11.6 us (7%)
  local copies, waits for them, and re-layouts  5.8 us (3%)
  waiting for transfers between devices  3.94 us (2%)
    all_to_all x6, blocking collectives, everywhere(): return lax.all_to_all(row, axis, 0, 0)  90.6 us
    ppermute x20, starting transfers between devices, exchange(): lax.ppermute(message, *pairs)  61.7 us
    pallas_call x17, Pallas kernels, call(): pl.pallas_call(body, out_shape=outs, in_specs=specs, out_specs=[pl.BlockS...  11.6 us
    unnamed x22, local copies, waits for them, and re-layouts  5.27 us
    ppermute x20, waiting for transfers between devices, exchange(): lax.ppermute(message, *pairs)  3.94 us
  transfers between devices with their start and end apart: 20, of which 7 were waited for; matrix products, arithmetic and copies ran while one was open for 0% of the time, Pallas kernels for 2%

profile of v3, /device:TPU:1, one launch (start us, length us, event | category | flops | bytes accessed | tf_op | source)
XLA Modules:
  0.0 174.7 jit_solution(346799260300522459)
XLA Ops:
  0.6 2.7 %begin.1 = (f32[12,128]{1,0:T(8,128)}, f32[12,128]{1,0:T(8,128)}, f32[12,128]{1,0:T(8,128)}, f32[12,128]{1,0:T(8,128)}, f32[1,1024]{1,0:T(1,128)}, /*index=5*/f3...) custom-call(f32[2,1,1,2048]{3,2,1,0:T(1,128)} %rhs_ref.1, ...), custom_call_target="tpu_custom_call" | custom-call | bytes 1097744 | tf_op jit(solution)/shard_map/begin/pallas_call | solution.py:495
  3.4 8.1 %collective-permute-start = (f32[12,128]{1,0:T(8,128)}, f32[12,128]{1,0:T(8,128)S(1)}, u32[]{:S(2)}, u32[]{:S(2)}) collective-permute-start(f32[12,128]{1,0:T(8,128)} %get-tuple-element.56), channel_id=1, source_target_pairs={{1,2},{3,4},{5,6},{7,8},{9,10},{11,12},{13,14},{15,16},{17,18},{19... | collective-permute-start | bytes 18440 | tf_op jit(solution)/shard_map/ppermute | solution.py:519
  13.4 4.8 %collective-permute-start.2 = (f32[12,128]{1,0:T(8,128)}, f32[12,128]{1,0:T(8,128)S(1)}, u32[]{:S(2)}, u32[]{:S(2)}) collective-permute-start(f32[12,128]{1,0:T(8,128)} %get-tuple-element.58), channel_id=1, source_target_pairs={{32,64},{96,128},{160,192},{224,256},{288,320},{352,384},{416,448}... | collective-permute-start | bytes 18440 | tf_op jit(solution)/shard_map/ppermute | solution.py:519
  27.8 4.3 %collective-permute-start.4 = (f32[4,128]{1,0:T(4,128)S(1)}, f32[4,128]{1,0:T(4,128)S(1)}, u32[]{:S(2)}, u32[]{:S(2)}) collective-permute-start(f32[4,128]{1,0:T(4,128)S(1)} %get-tuple-element.68), channel_id=1, source_target_pairs={{1,2},{3,4},{5,6},{7,8},{9,10},{11,12},{13,14},{15,16},{17,18},{19... | collective-permute-start | bytes 6152 | tf_op jit(solution)/shard_map/ppermute | solution.py:519
  32.2 1.9 %collective-permute-start.5 = (f32[4,128]{1,0:T(4,128)S(1)}, f32[4,128]{1,0:T(4,128)S(1)}, u32[]{:S(2)}, u32[]{:S(2)}) collective-permute-start(f32[4,128]{1,0:T(4,128)S(1)} %get-tuple-element.69), channel_id=1, source_target_pairs={{0,1},{2,3},{4,5},{6,7},{8,9},{10,11},{12,13},{14,15},{16,17},{18,... | collective-permute-start | bytes 6152 | tf_op jit(solution)/shard_map/ppermute | solution.py:519
  34.1 4.7 %collective-permute-start.6 = (f32[4,128]{1,0:T(4,128)S(1)}, f32[4,128]{1,0:T(4,128)S(1)}, u32[]{:S(2)}, u32[]{:S(2)}) collective-permute-start(f32[4,128]{1,0:T(4,128)S(1)} %get-tuple-element.70), channel_id=1, source_target_pairs={{32,64},{96,128},{160,192},{224,256},{288,320},{352,384},{416,448}... | collective-permute-start | bytes 6152 | tf_op jit(solution)/shard_map/ppermute | solution.py:519
  38.8 1.9 %collective-permute-start.7 = (f32[4,128]{1,0:T(4,128)S(1)}, f32[4,128]{1,0:T(4,128)S(1)}, u32[]{:S(2)}, u32[]{:S(2)}) collective-permute-start(f32[4,128]{1,0:T(4,128)S(1)} %get-tuple-element.71), channel_id=1, source_target_pairs={{0,32},{64,96},{128,160},{192,224},{256,288},{320,352},{384,416},{... | collective-permute-start | bytes 6152 | tf_op jit(solution)/shard_map/ppermute | solution.py:519
  42.5 4.1 %collective-permute-start.8 = (f32[4,128]{1,0:T(4,128)S(1)}, f32[4,128]{1,0:T(4,128)S(1)}, u32[]{:S(2)}, u32[]{:S(2)}) collective-permute-start(f32[4,128]{1,0:T(4,128)S(1)} %get-tuple-element.75), channel_id=1, source_target_pairs={{32,64},{96,128},{160,192},{224,256},{288,320},{352,384},{416,448}... | collective-permute-start | bytes 6152 | tf_op jit(solution)/shard_map/ppermute | solution.py:519
  46.5 1.9 %collective-permute-start.9 = (f32[4,128]{1,0:T(4,128)S(1)}, f32[4,128]{1,0:T(4,128)S(1)}, u32[]{:S(2)}, u32[]{:S(2)}) collective-permute-start(f32[4,128]{1,0:T(4,128)S(1)} %get-tuple-element.76), channel_id=1, source_target_pairs={{0,32},{64,96},{128,160},{192,224},{256,288},{320,352},{384,416},{... | collective-permute-start | bytes 6152 | tf_op jit(solution)/shard_map/ppermute | solution.py:519
  49.6 15.4 %all_to_all.30.row_ref = f32[32,16,128]{2,1,0:T(8,128)S(1)} all-to-all(f32[32,16,128]{2,1,0:T(8,128)S(1)} %row.2), channel_id=1, replica_groups=mesh['lat'=16,'lon'=32] {'lon'}, dimensions={0} | all-to-all | bytes 524288 | tf_op jit(solution)/shard_map/all_to_all | solution.py:523
  65.0 20.1 %all_to_all.31.column_ref = f32[16,12,128]{2,1,0:T(8,128)S(1)} all-to-all(f32[16,12,128]{2,1,0:T(8,128)S(1)} %get-tuple-element.79), channel_id=1, replica_groups=mesh['lat'=16,'lon'=32] {'lat'}, dimensions={0} | all-to-all | bytes 196608 | tf_op jit(solution)/shard_map/all_to_all | solution.py:523
  86.4 3.4 %collective-permute-start.10 = (f32[4,128]{1,0:T(4,128)S(1)}, f32[4,128]{1,0:T(4,128)S(1)}, u32[]{:S(2)}, u32[]{:S(2)}) collective-permute-start(f32[4,128]{1,0:T(4,128)S(1)} %get-tuple-element.84), channel_id=1, source_target_pairs={{1,2},{3,4},{5,6},{7,8},{9,10},{11,12},{13,14},{15,16},{17,18},{19... | collective-permute-start | bytes 6152 | tf_op jit(solution)/shard_map/ppermute | solution.py:519
  89.8 2.3 %collective-permute-start.11 = (f32[4,128]{1,0:T(4,128)S(1)}, f32[4,128]{1,0:T(4,128)S(1)}, u32[]{:S(2)}, u32[]{:S(2)}) collective-permute-start(f32[4,128]{1,0:T(4,128)S(1)} %get-tuple-element.85), channel_id=1, source_target_pairs={{0,1},{2,3},{4,5},{6,7},{8,9},{10,11},{12,13},{14,15},{16,17},{18,... | collective-permute-start | bytes 6152 | tf_op jit(solution)/shard_map/ppermute | solution.py:519
  92.1 2.3 %collective-permute-start.12 = (f32[4,128]{1,0:T(4,128)S(1)}, f32[4,128]{1,0:T(4,128)S(1)}, u32[]{:S(2)}, u32[]{:S(2)}) collective-permute-start(f32[4,128]{1,0:T(4,128)S(1)} %get-tuple-element.86), channel_id=1, source_target_pairs={{32,64},{96,128},{160,192},{224,256},{288,320},{352,384},{416,448}... | collective-permute-start | bytes 6152 | tf_op jit(solution)/shard_map/ppermute | solution.py:519
  94.4 1.9 %collective-permute-start.13 = (f32[4,128]{1,0:T(4,128)S(1)}, f32[4,128]{1,0:T(4,128)S(1)}, u32[]{:S(2)}, u32[]{:S(2)}) collective-permute-start(f32[4,128]{1,0:T(4,128)S(1)} %get-tuple-element.87), channel_id=1, source_target_pairs={{0,32},{64,96},{128,160},{192,224},{256,288},{320,352},{384,416},{... | collective-permute-start | bytes 6152 | tf_op jit(solution)/shard_map/ppermute | solution.py:519
  98.0 4.5 %collective-permute-start.14 = (f32[4,128]{1,0:T(4,128)S(1)}, f32[4,128]{1,0:T(4,128)S(1)}, u32[]{:S(2)}, u32[]{:S(2)}) collective-permute-start(f32[4,128]{1,0:T(4,128)S(1)} %get-tuple-element.90), channel_id=1, source_target_pairs={{1,2},{3,4},{5,6},{7,8},{9,10},{11,12},{13,14},{15,16},{17,18},{19... | collective-permute-start | bytes 6152 | tf_op jit(solution)/shard_map/ppermute | solution.py:519
  102.5 1.9 %collective-permute-start.15 = (f32[4,128]{1,0:T(4,128)S(1)}, f32[4,128]{1,0:T(4,128)S(1)}, u32[]{:S(2)}, u32[]{:S(2)}) collective-permute-start(f32[4,128]{1,0:T(4,128)S(1)} %get-tuple-element.91), channel_id=1, source_target_pairs={{0,1},{2,3},{4,5},{6,7},{8,9},{10,11},{12,13},{14,15},{16,17},{18,... | collective-permute-start | bytes 6152 | tf_op jit(solution)/shard_map/ppermute | solution.py:519
  104.4 3.8 %collective-permute-start.16 = (f32[4,128]{1,0:T(4,128)S(1)}, f32[4,128]{1,0:T(4,128)S(1)}, u32[]{:S(2)}, u32[]{:S(2)}) collective-permute-start(f32[4,128]{1,0:T(4,128)S(1)} %get-tuple-element.92), channel_id=1, source_target_pairs={{32,64},{96,128},{160,192},{224,256},{288,320},{352,384},{416,448}... | collective-permute-start | bytes 6152 | tf_op jit(solution)/shard_map/ppermute | solution.py:519
  108.3 1.9 %collective-permute-start.17 = (f32[4,128]{1,0:T(4,128)S(1)}, f32[4,128]{1,0:T(4,128)S(1)}, u32[]{:S(2)}, u32[]{:S(2)}) collective-permute-start(f32[4,128]{1,0:T(4,128)S(1)} %get-tuple-element.93), channel_id=1, source_target_pairs={{0,32},{64,96},{128,160},{192,224},{256,288},{320,352},{384,416},{... | collective-permute-start | bytes 6152 | tf_op jit(solution)/shard_map/ppermute | solution.py:519
  112.0 2.0 %collective-permute-start.18 = (f32[4,128]{1,0:T(4,128)S(1)}, f32[4,128]{1,0:T(4,128)S(1)}, u32[]{:S(2)}, u32[]{:S(2)}) collective-permute-start(f32[4,128]{1,0:T(4,128)S(1)} %get-tuple-element.95), channel_id=1, source_target_pairs={{32,64},{96,128},{160,192},{224,256},{288,320},{352,384},{416,448}... | collective-permute-start | bytes 6152 | tf_op jit(solution)/shard_map/ppermute | solution.py:519
  117.1 15.4 %all_to_all.32.row_ref = f32[32,12,128]{2,1,0:T(8,128)S(1)} all-to-all(f32[32,12,128]{2,1,0:T(8,128)S(1)} %row.3), channel_id=1, replica_groups=mesh['lat'=16,'lon'=32] {'lon'}, dimensions={0} | all-to-all | bytes 393216 | tf_op jit(solution)/shard_map/all_to_all | solution.py:523
  132.5 17.7 %all_to_all.33.column_ref = f32[16,12,128]{2,1,0:T(8,128)S(1)} all-to-all(f32[16,12,128]{2,1,0:T(8,128)S(1)} %get-tuple-element.99), channel_id=1, replica_groups=mesh['lat'=16,'lon'=32] {'lat'}, dimensions={0} | all-to-all | bytes 196608 | tf_op jit(solution)/shard_map/all_to_all | solution.py:523
  151.3 9.4 %all_to_all.34 = f32[16,1,128]{2,1,0:T(1,128)S(1)} all-to-all(f32[16,1,128]{2,1,0:T(1,128)S(1)} %get-tuple-element.102), channel_id=1, replica_groups=mesh['lat'=16,'lon'=32] {'lat'}, dimensions={0} | all-to-all | bytes 16384 | tf_op jit(solution)/shard_map/all_to_all | solution.py:523
  160.8 12.6 %all_to_all.35.sums_ref = f32[32,1,128]{2,1,0:T(1,128)S(1)} all-to-all(f32[32,1,128]{2,1,0:T(1,128)S(1)} %broadcast_in_dim.2), channel_id=1, replica_groups=mesh['lat'=16,'lon'=32] {'lon'}, dimensions={0} | all-to-all | bytes 32768 | tf_op jit(solution)/shard_map/all_to_all | solution.py:523
  (64 shorter events, 24.4 us)
Async XLA Ops:
  3.3 23.8 %copy-start.8 = (f32[1,1024]{1,0:T(1,128)S(1)}, f32[1,1024]{1,0:T(1,128)}, u32[]{:S(2)}) copy-start(f32[1,1024]{1,0:T(1,128)} %get-tuple-element.62.coef_ref) | copy-start | bytes 12292
  3.3 23.8 %copy-start.10 = (f32[4,128]{1,0:T(4,128)S(1)}, f32[4,128]{1,0:T(4,128)}, u32[]{:S(2)}) copy-start(f32[4,128]{1,0:T(4,128)} %get-tuple-element.60.own_ref) | copy-start | bytes 6148
  3.4 23.7 %collective-permute-start = (f32[12,128]{1,0:T(8,128)}, f32[12,128]{1,0:T(8,128)S(1)}, u32[]{:S(2)}, u32[]{:S(2)}) collective-permute-start(f32[12,128]{1,0:T(8,128)} %get-tuple-element.56), channel_id=1, source_target_pairs={{1,2},{3,4},{5,6},{7,8},{9,10},{11,12},{13,14},{15,16},{17,18},{19... | collective-permute-start | bytes 18440 | tf_op jit(solution)/shard_map/ppermute | solution.py:519
  11.5 15.6 %collective-permute-start.1 = (f32[12,128]{1,0:T(8,128)}, f32[12,128]{1,0:T(8,128)S(1)}, u32[]{:S(2)}, u32[]{:S(2)}) collective-permute-start(f32[12,128]{1,0:T(8,128)} %get-tuple-element.57), channel_id=1, source_target_pairs={{0,1},{2,3},{4,5},{6,7},{8,9},{10,11},{12,13},{14,15},{16,17},{18,... | collective-permute-start | bytes 18440 | tf_op jit(solution)/shard_map/ppermute | solution.py:519
  13.4 13.7 %collective-permute-start.2 = (f32[12,128]{1,0:T(8,128)}, f32[12,128]{1,0:T(8,128)S(1)}, u32[]{:S(2)}, u32[]{:S(2)}) collective-permute-start(f32[12,128]{1,0:T(8,128)} %get-tuple-element.58), channel_id=1, source_target_pairs={{32,64},{96,128},{160,192},{224,256},{288,320},{352,384},{416,448}... | collective-permute-start | bytes 18440 | tf_op jit(solution)/shard_map/ppermute | solution.py:519
  18.3 8.8 %collective-permute-start.3 = (f32[12,128]{1,0:T(8,128)}, f32[12,128]{1,0:T(8,128)S(1)}, u32[]{:S(2)}, u32[]{:S(2)}) collective-permute-start(f32[12,128]{1,0:T(8,128)} %get-tuple-element.59), channel_id=1, source_target_pairs={{0,32},{64,96},{128,160},{192,224},{256,288},{320,352},{384,416},{... | collective-permute-start | bytes 18440 | tf_op jit(solution)/shard_map/ppermute | solution.py:519
  24.0 3.1 %copy-start.7 = (f32[32,128]{1,0:T(8,128)S(1)}, f32[32,128]{1,0:T(8,128)}, u32[]{:S(2)}) copy-start(f32[32,128]{1,0:T(8,128)} %get-tuple-element.66.scale_ref) | copy-start | bytes 49156
  24.0 16.7 %copy-start.4 = (f32[32,128]{1,0:T(8,128)S(1)}, f32[32,128]{1,0:T(8,128)}, u32[]{:S(2)}) copy-start(f32[32,128]{1,0:T(8,128)} %get-tuple-element.64.value_ref) | copy-start | bytes 49156
  27.8 13.4 %collective-permute-start.4 = (f32[4,128]{1,0:T(4,128)S(1)}, f32[4,128]{1,0:T(4,128)S(1)}, u32[]{:S(2)}, u32[]{:S(2)}) collective-permute-start(f32[4,128]{1,0:T(4,128)S(1)} %get-tuple-element.68), channel_id=1, source_target_pairs={{1,2},{3,4},{5,6},{7,8},{9,10},{11,12},{13,14},{15,16},{17,18},{19... | collective-permute-start | bytes 6152 | tf_op jit(solution)/shard_map/ppermute | solution.py:519
  32.2 9.1 %collective-permute-start.5 = (f32[4,128]{1,0:T(4,128)S(1)}, f32[4,128]{1,0:T(4,128)S(1)}, u32[]{:S(2)}, u32[]{:S(2)}) collective-permute-start(f32[4,128]{1,0:T(4,128)S(1)} %get-tuple-element.69), channel_id=1, source_target_pairs={{0,1},{2,3},{4,5},{6,7},{8,9},{10,11},{12,13},{14,15},{16,17},{18,... | collective-permute-start | bytes 6152 | tf_op jit(solution)/shard_map/ppermute | solution.py:519
  34.1 7.2 %collective-permute-start.6 = (f32[4,128]{1,0:T(4,128)S(1)}, f32[4,128]{1,0:T(4,128)S(1)}, u32[]{:S(2)}, u32[]{:S(2)}) collective-permute-start(f32[4,128]{1,0:T(4,128)S(1)} %get-tuple-element.70), channel_id=1, source_target_pairs={{32,64},{96,128},{160,192},{224,256},{288,320},{352,384},{416,448}... | collective-permute-start | bytes 6152 | tf_op jit(solution)/shard_map/ppermute | solution.py:519
  38.8 3.1 %collective-permute-start.7 = (f32[4,128]{1,0:T(4,128)S(1)}, f32[4,128]{1,0:T(4,128)S(1)}, u32[]{:S(2)}, u32[]{:S(2)}) collective-permute-start(f32[4,128]{1,0:T(4,128)S(1)} %get-tuple-element.71), channel_id=1, source_target_pairs={{0,32},{64,96},{128,160},{192,224},{256,288},{320,352},{384,416},{... | collective-permute-start | bytes 6152 | tf_op jit(solution)/shard_map/ppermute | solution.py:519
  42.5 6.0 %collective-permute-start.8 = (f32[4,128]{1,0:T(4,128)S(1)}, f32[4,128]{1,0:T(4,128)S(1)}, u32[]{:S(2)}, u32[]{:S(2)}) collective-permute-start(f32[4,128]{1,0:T(4,128)S(1)} %get-tuple-element.75), channel_id=1, source_target_pairs={{32,64},{96,128},{160,192},{224,256},{288,320},{352,384},{416,448}... | collective-permute-start | bytes 6152 | tf_op jit(solution)/shard_map/ppermute | solution.py:519
  46.5 3.1 %collective-permute-start.9 = (f32[4,128]{1,0:T(4,128)S(1)}, f32[4,128]{1,0:T(4,128)S(1)}, u32[]{:S(2)}, u32[]{:S(2)}) collective-permute-start(f32[4,128]{1,0:T(4,128)S(1)} %get-tuple-element.76), channel_id=1, source_target_pairs={{0,32},{64,96},{128,160},{192,224},{256,288},{320,352},{384,416},{... | collective-permute-start | bytes 6152 | tf_op jit(solution)/shard_map/ppermute | solution.py:519
  86.4 10.5 %collective-permute-start.10 = (f32[4,128]{1,0:T(4,128)S(1)}, f32[4,128]{1,0:T(4,128)S(1)}, u32[]{:S(2)}, u32[]{:S(2)}) collective-permute-start(f32[4,128]{1,0:T(4,128)S(1)} %get-tuple-element.84), channel_id=1, source_target_pairs={{1,2},{3,4},{5,6},{7,8},{9,10},{11,12},{13,14},{15,16},{17,18},{19... | collective-permute-start | bytes 6152 | tf_op jit(solution)/shard_map/ppermute | solution.py:519
  89.8 7.1 %collective-permute-start.11 = (f32[4,128]{1,0:T(4,128)S(1)}, f32[4,128]{1,0:T(4,128)S(1)}, u32[]{:S(2)}, u32[]{:S(2)}) collective-permute-start(f32[4,128]{1,0:T(4,128)S(1)} %get-tuple-element.85), channel_id=1, source_target_pairs={{0,1},{2,3},{4,5},{6,7},{8,9},{10,11},{12,13},{14,15},{16,17},{18,... | collective-permute-start | bytes 6152 | tf_op jit(solution)/shard_map/ppermute | solution.py:519
  92.1 4.9 %collective-permute-start.12 = (f32[4,128]{1,0:T(4,128)S(1)}, f32[4,128]{1,0:T(4,128)S(1)}, u32[]{:S(2)}, u32[]{:S(2)}) collective-permute-start(f32[4,128]{1,0:T(4,128)S(1)} %get-tuple-element.86), channel_id=1, source_target_pairs={{32,64},{96,128},{160,192},{224,256},{288,320},{352,384},{416,448}... | collective-permute-start | bytes 6152 | tf_op jit(solution)/shard_map/ppermute | solution.py:519
  94.4 3.1 %collective-permute-start.13 = (f32[4,128]{1,0:T(4,128)S(1)}, f32[4,128]{1,0:T(4,128)S(1)}, u32[]{:S(2)}, u32[]{:S(2)}) collective-permute-start(f32[4,128]{1,0:T(4,128)S(1)} %get-tuple-element.87), channel_id=1, source_target_pairs={{0,32},{64,96},{128,160},{192,224},{256,288},{320,352},{384,416},{... | collective-permute-start | bytes 6152 | tf_op jit(solution)/shard_map/ppermute | solution.py:519
  98.0 12.8 %collective-permute-start.14 = (f32[4,128]{1,0:T(4,128)S(1)}, f32[4,128]{1,0:T(4,128)S(1)}, u32[]{:S(2)}, u32[]{:S(2)}) collective-permute-start(f32[4,128]{1,0:T(4,128)S(1)} %get-tuple-element.90), channel_id=1, source_target_pairs={{1,2},{3,4},{5,6},{7,8},{9,10},{11,12},{13,14},{15,16},{17,18},{19... | collective-permute-start | bytes 6152 | tf_op jit(solution)/shard_map/ppermute | solution.py:519
  102.5 8.2 %collective-permute-start.15 = (f32[4,128]{1,0:T(4,128)S(1)}, f32[4,128]{1,0:T(4,128)S(1)}, u32[]{:S(2)}, u32[]{:S(2)}) collective-permute-start(f32[4,128]{1,0:T(4,128)S(1)} %get-tuple-element.91), channel_id=1, source_target_pairs={{0,1},{2,3},{4,5},{6,7},{8,9},{10,11},{12,13},{14,15},{16,17},{18,... | collective-permute-start | bytes 6152 | tf_op jit(solution)/shard_map/ppermute | solution.py:519
  104.4 6.3 %collective-permute-start.16 = (f32[4,128]{1,0:T(4,128)S(1)}, f32[4,128]{1,0:T(4,128)S(1)}, u32[]{:S(2)}, u32[]{:S(2)}) collective-permute-start(f32[4,128]{1,0:T(4,128)S(1)} %get-tuple-element.92), channel_id=1, source_target_pairs={{32,64},{96,128},{160,192},{224,256},{288,320},{352,384},{416,448}... | collective-permute-start | bytes 6152 | tf_op jit(solution)/shard_map/ppermute | solution.py:519
  108.3 3.1 %collective-permute-start.17 = (f32[4,128]{1,0:T(4,128)S(1)}, f32[4,128]{1,0:T(4,128)S(1)}, u32[]{:S(2)}, u32[]{:S(2)}) collective-permute-start(f32[4,128]{1,0:T(4,128)S(1)} %get-tuple-element.93), channel_id=1, source_target_pairs={{0,32},{64,96},{128,160},{192,224},{256,288},{320,352},{384,416},{... | collective-permute-start | bytes 6152 | tf_op jit(solution)/shard_map/ppermute | solution.py:519
  112.0 4.9 %collective-permute-start.18 = (f32[4,128]{1,0:T(4,128)S(1)}, f32[4,128]{1,0:T(4,128)S(1)}, u32[]{:S(2)}, u32[]{:S(2)}) collective-permute-start(f32[4,128]{1,0:T(4,128)S(1)} %get-tuple-element.95), channel_id=1, source_target_pairs={{32,64},{96,128},{160,192},{224,256},{288,320},{352,384},{416,448}... | collective-permute-start | bytes 6152 | tf_op jit(solution)/shard_map/ppermute | solution.py:519
  114.0 3.1 %collective-permute-start.19 = (f32[4,128]{1,0:T(4,128)S(1)}, f32[4,128]{1,0:T(4,128)S(1)}, u32[]{:S(2)}, u32[]{:S(2)}) collective-permute-start(f32[4,128]{1,0:T(4,128)S(1)} %get-tuple-element.96), channel_id=1, source_target_pairs={{0,32},{64,96},{128,160},{192,224},{256,288},{320,352},{384,416},{... | collective-permute-start | bytes 6152 | tf_op jit(solution)/shard_map/ppermute | solution.py:519
  (7 other events, 8.4 us)

commit v4 on v3

--- a/solution.py
+++ b/solution.py
@@ -280,7 +280,7 @@
 
 def smooth_first_kernel(
     a0, a1, a2, a3, own_ref, ohi_ref, coef_ref, idx_ref, first_ref, local_ref, scale_ref, right_ref,
-    m0, m1, m2, m3, second_ref, ninv_ref, ends_ref, away_ref,
+    m0, m1, m2, m3, second_ref, ninv_ref, ends_ref, oha_ref,
 ):
     arrived = collect((a0, a1, a2, a3))
     smooth(arrived, ohi_ref, coef_ref, idx_ref, first_ref, local_ref, scale_ref, right_ref, (m0, m1, m2, m3), second_ref)
@@ -296,7 +296,7 @@
             row = row.astype(jnp.int32)
             at = (2 * d + k) * IFC
             ends_ref[:, at : at + IFC] = row
-            away_ref[:, at : at + IFC] = lane_onehot(row)
+            oha_ref[:, at : at + IFC] = lane_onehot(row)
 
 
 def smooth_kernel(
@@ -321,14 +321,17 @@
     far_ref[...] = jnp.where(even_lat, towards[0], towards[1])
     core_ref[...] = jnp.where(even_lat, towards[1], towards[0])
     for k, part in enumerate((own, towards[2], towards[3])):
-        row_ref[4 * k : 4 * k + 4] = part
+        row_ref[k] = part
 
 
 def row_kernel(far_ref, core_ref, row_ref, *refs):
     out_ref = refs[-1]
-    parts = [row_ref[0:4] + far_ref[...] + core_ref[...], row_ref[4:8], row_ref[8:12]]
+    even_lat, _ = parities()
+    core = jnp.where(even_lat, core_ref[1], core_ref[0])
+    parts = [row_ref[0] + far_ref[...] + core, row_ref[1], row_ref[2]]
     parts += [ref[...] for ref in refs[:-1]]
-    out_ref[...] = jnp.broadcast_to(jnp.concatenate(parts, axis=0)[None], out_ref.shape)
+    for k, part in enumerate(parts):
+        out_ref[:, k] = jnp.broadcast_to(part[None], (out_ref.shape[0], 4, BS))
 
 
 def column_kernel(known, lon, row_ref, *refs):
@@ -339,13 +342,14 @@
         return lax.rem(me + (lon + step), lon)
 
     for k in range(5):
-        sums = row_ref[at(k - 2), 0:4] + row_ref[at(k - 1), 4:8] + row_ref[at(k - 3), 8:12]
+        sums = row_ref[at(k - 2), 0] + row_ref[at(k - 1), 1] + row_ref[at(k - 3), 2]
         if not known:
-            inverse_ref[4 * k : 4 * k + 4] = row_ref[at(k - 2), 12:16]
-        inverse = inverse_ref[4 * k : 4 * k + 4]
+            inverse_ref[k] = row_ref[at(k - 2), 3]
+        inverse = inverse_ref[k]
         result = complex_times((inverse[0:2], inverse[2:4]), (sums[0:2], sums[2:4]))
-        near_ref[4 * k : 4 * k + 4] = jnp.concatenate(result, axis=0)
-    out_ref[...] = jnp.broadcast_to(near_ref[4:16][None], out_ref.shape)
+        near_ref[k] = jnp.concatenate(result, axis=0)
+    for k in range(3):
+        out_ref[k] = near_ref[k + 1]
 
 
 def extend(nodes, ref):
@@ -362,16 +366,21 @@
 
 
 def prolong(
-    lat, column_ref, near_ref, ohi_ref, oht_ref, ohh_ref, coef_ref, idx_ref, nodes_ref, second_ref, extra_ref,
-    ends_ref, away_ref, value_ref, w_ref, direction_ref, blocks, ext, wide, out,
+    lat, chip_ref, away_ref, near_ref, ohi_ref, oht_ref, ohh_ref, coef_ref, idx_ref, nodes_ref, second_ref, extra_ref,
+    ends_ref, oha_ref, value_ref, w_ref, direction_ref, blocks, ext, wide, out, column,
 ):
     me = lax.axis_index("lat")
+
+    for k in range(2):
+        column[k] = away_ref[0, 3 * k : 3 * k + 3]
+        column[2 + k] = chip_ref[k]
+        column[4 + k] = away_ref[1, 3 * k : 3 * k + 3]
+    here = 2 + me % 2
 
     def node(down, right):
         if down == 0:
-            return near_ref[4 * right + 8 : 4 * right + 12]
-        there = jnp.clip(me + down, 0, lat - 1)
-        return column_ref[there, 4 * right + 4 : 4 * right + 8]
+            return near_ref[right + 2]
+        return column[here + down, right + 1]
 
     def around(down, right):
         steps = ((0, 0), (-1, 0), (1, 0), (0, -1), (0, 1))
@@ -386,7 +395,7 @@
     for d, step in enumerate(((-1, 0), (1, 0), (0, -1), (0, 1))):
         spots = [pl.ds((2 * d + k) * IFC, IFC) for k in range(2)]
         rise = gradient(
-            around(*step), ext, away_ref.at[:, spots[0]], away_ref.at[:, spots[1]],
+            around(*step), ext, oha_ref.at[:, spots[0]], oha_ref.at[:, spots[1]],
             ends_ref[:, spots[0]], ends_ref[:, spots[1]],
         )
         if d < 2:
@@ -402,14 +411,14 @@
 
 
 def prolong_first_kernel(
-    lat, column_ref, near_ref, ohi_ref, oht_ref, ohh_ref, coef_ref, idx_ref, nodes_ref, second_ref, extra_ref,
-    ends_ref, away_ref, value_ref, w_ref, scale_ref,
+    lat, chip_ref, away_ref, near_ref, ohi_ref, oht_ref, ohh_ref, coef_ref, idx_ref, nodes_ref, second_ref, extra_ref,
+    ends_ref, oha_ref, value_ref, w_ref, scale_ref,
     m0, m1, m2, m3, direction_ref, image_ref, first_ref,
     *scratch,
 ):
     image = prolong(
-        lat, column_ref, near_ref, ohi_ref, oht_ref, ohh_ref, coef_ref, idx_ref, nodes_ref, second_ref, extra_ref,
-        ends_ref, away_ref, value_ref, w_ref, direction_ref, *scratch,
+        lat, chip_ref, away_ref, near_ref, ohi_ref, oht_ref, ohh_ref, coef_ref, idx_ref, nodes_ref, second_ref, extra_ref,
+        ends_ref, oha_ref, value_ref, w_ref, direction_ref, *scratch,
     )
     keep(image_ref, image)
     first = complex_times(pair(scale_ref), image)
@@ -426,14 +435,14 @@
 
 
 def prolong_last_kernel(
-    lat, column_ref, near_ref, ohi_ref, oht_ref, ohh_ref, coef_ref, idx_ref, nodes_ref, second_ref, extra_ref,
-    ends_ref, away_ref, value_ref, w_ref, right_ref, image_ref,
+    lat, chip_ref, away_ref, near_ref, ohi_ref, oht_ref, ohh_ref, coef_ref, idx_ref, nodes_ref, second_ref, extra_ref,
+    ends_ref, oha_ref, value_ref, w_ref, right_ref, image_ref,
     direction_ref, image2_ref, sums_ref,
     *scratch,
 ):
     image2 = prolong(
-        lat, column_ref, near_ref, ohi_ref, oht_ref, ohh_ref, coef_ref, idx_ref, nodes_ref, second_ref, extra_ref,
-        ends_ref, away_ref, value_ref, w_ref, direction_ref, *scratch,
+        lat, chip_ref, away_ref, near_ref, ohi_ref, oht_ref, ohh_ref, coef_ref, idx_ref, nodes_ref, second_ref, extra_ref,
+        ends_ref, oha_ref, value_ref, w_ref, direction_ref, *scratch,
     )
     right, image = pair(right_ref), pair(image_ref)
     keep(image2_ref, image2)
@@ -508,15 +517,26 @@
     return [(a, b) for a, b in pairs] + [(b, a) for a, b in pairs]
 
 
+def lat_pairs(first):
+    return [(k, k + 1) for k in range(first, lax.axis_size("lat") - 1, 2)]
+
+
+def swap_far(message):
+    return lax.ppermute(message, "lat", swap(lat_pairs(1)))
+
+
+def on_chip(message):
+    return lax.all_gather(message, "lat", axis_index_groups=lat_pairs(0))
+
+
 def exchange(messages):
-    lat, lon = lax.axis_size("lat"), lax.axis_size("lon")
-    swaps = (
-        ("lon", swap([(k, (k + 1) % lon) for k in range(1, lon, 2)])),
-        ("lon", swap([(k, k + 1) for k in range(0, lon, 2)])),
-        ("lat", swap([(k, k + 1) for k in range(1, lat - 1, 2)])),
-        ("lat", swap([(k, k + 1) for k in range(0, lat, 2)])),
-    )
-    return [lax.ppermute(message, *pairs) for message, pairs in zip(messages, swaps[4 - len(messages) :])]
+    lon = lax.axis_size("lon")
+    return [
+        lax.ppermute(messages[0], "lon", swap([(k, (k + 1) % lon) for k in range(1, lon, 2)])),
+        lax.ppermute(messages[1], "lon", swap([(k, k + 1) for k in range(0, lon, 2)])),
+        swap_far(messages[2]),
+        lax.ppermute(messages[3], "lat", swap(lat_pairs(0))),
+    ]
 
 
 def everywhere(row, axis):
@@ -557,12 +577,12 @@
         )[0]
 
     lat, lon = lax.axis_size("lat"), lax.axis_size("lon")
-    scratch = [blocks, pltpu.VMEM((2 * EB, BS), F32), wide, out]
+    scratch = [blocks, pltpu.VMEM((2 * EB, BS), F32), wide, out, pltpu.VMEM((6, 3, 4, BS), F32)]
     directions = []
     for step in range(ITERS):
         stiff = local(first)
         if step == 0:
-            *sent, second, ninv, ends, away = call(
+            *sent, second, ninv, ends, oha = call(
                 smooth_first_kernel,
                 MESSAGES + [FIELD, shape(4, BS), shape(1, 8 * IFC, dtype=jnp.int32), shape(BS, 8 * IFC, dtype=BF16)],
                 (*arrived, own, ohi, coef, idx, first, stiff, scale, right),
@@ -578,28 +598,28 @@
             )
         arrived = exchange(sent)
         stiff = local(second)
-        *sent, row, extra = call(
+        far, core, row, extra = call(
             restrict_kernel,
-            MESSAGES[:2] + [shape(12, BS), FIELD],
+            MESSAGES[:2] + [shape(3, 4, BS), FIELD],
             (*arrived, ohi, oht, ohh, coef, idx, nodes, stiff, source),
             "restrict",
         )
-        arrived = exchange(sent)
         known = step > 0
         (row,) = call(
             row_kernel,
-            [shape(lon, 12 if known else 16, BS)],
-            (*arrived, row) + (() if known else (ninv,)),
+            [shape(lon, 3 if known else 4, 4, BS)],
+            (swap_far(far), on_chip(core), row) + (() if known else (ninv,)),
             "row",
         )
         near, column, *found = call(
             functools.partial(column_kernel, known, lon),
-            [shape(20, BS), shape(lat, 12, BS)] + ([] if known else [shape(20, BS)]),
+            [shape(5, 4, BS), shape(3, 4, BS)] + ([] if known else [shape(5, 4, BS)]),
             (everywhere(row, "lon"),) + ((inverses,) if known else ()),
             "column",
         )
-        column = everywhere(column, "lat")
-        args = (column, near, ohi, oht, ohh, coef, idx, nodes, second, extra, ends, away, value, weights)
+        chip = on_chip(column)
+        away = on_chip(swap_far(chip.reshape(6, 4, BS)))
+        args = (chip, away, near, ohi, oht, ohh, coef, idx, nodes, second, extra, ends, oha, value, weights)
         if step == 0:
             (inverses,) = found
             *sent, direction, image, first = call(

time: 176 us -> 168 us (0.955)
  blocking collectives: 90.6 us -> 73.3 us
  starting transfers between devices: 61.7 us -> 70.7 us
    all_to_all x6 -> x4, blocking collectives: 90.6 us -> 57.1 us  [everywhere(): return lax.all_to_all(row, axis, 0, 0)]
    all_gather x0 -> x6, blocking collectives: none -> 16.2 us  [on_chip(): return lax.all_gather(message, 'lat', axis_index_groups=lat_pairs(0))]
    ppermute x20, starting transfers between devices: 61.7 us -> 70.7 us  [the longest x8 34.5 us: swap_far(): return lax.ppermute(message, 'lat', swap(lat_pairs(1)))]
    unnamed x22 -> x26, local copies, waits for them, and re-layouts: 5.27 us -> 5.28 us
  transfers between devices with their start and end apart: 20 -> 20, of which waited for: 7 -> 5; matrix products, arithmetic and copies ran while one was open for 0% -> 0% of each run, Pallas kernels for 2% -> 2%
where the time goes in v4:
time: 168 us; the launch traced here: 167 us
  blocking collectives  73.3 us (44%)
  starting transfers between devices  70.7 us (42%)
  Pallas kernels  11.6 us (7%)
  local copies, waits for them, and re-layouts  5.81 us (3%)
  waiting for transfers between devices  4.43 us (3%)
    all_to_all x4, blocking collectives, everywhere(): return lax.all_to_all(row, axis, 0, 0)  57.1 us
    ppermute x8, starting transfers between devices, swap_far(): return lax.ppermute(message, 'lat', swap(lat_pairs(1)))  34.5 us
    ppermute x4, starting transfers between devices, exchange(): lax.ppermute(messages[0], 'lon', swap([(k, (k + 1) % lon) for k in range(...  20.4 us
    all_gather x6, blocking collectives, on_chip(): return lax.all_gather(message, 'lat', axis_index_groups=lat_pairs(0))  16.2 us
    pallas_call x17, Pallas kernels, call(): pl.pallas_call(body, out_shape=outs, in_specs=specs, out_specs=[pl.BlockS...  11.6 us
    ppermute x4, starting transfers between devices, exchange(): lax.ppermute(messages[1], 'lon', swap([(k, k + 1) for k in range(0, lon,...  8.08 us
    ppermute x4, starting transfers between devices, exchange(): lax.ppermute(messages[3], 'lat', swap(lat_pairs(0)))  7.68 us
    unnamed x26, local copies, waits for them, and re-layouts  5.28 us
  transfers between devices with their start and end apart: 20, of which 5 were waited for; matrix products, arithmetic and copies ran while one was open for 0% of the time, Pallas kernels for 2%

profile of v4, /device:TPU:1, one launch (start us, length us, event | category | flops | bytes accessed | tf_op | source)
XLA Modules:
  0.0 166.9 jit_solution(10790201178045702454)
XLA Ops:
  0.6 2.7 %begin.1 = (f32[12,128]{1,0:T(8,128)}, f32[12,128]{1,0:T(8,128)}, f32[12,128]{1,0:T(8,128)}, f32[12,128]{1,0:T(8,128)}, f32[1,1024]{1,0:T(1,128)}, /*index=5*/f3...) custom-call(f32[2,1,1,2048]{3,2,1,0:T(1,128)} %rhs_ref.1, ...), custom_call_target="tpu_custom_call" | custom-call | bytes 1097744 | tf_op jit(solution)/shard_map/begin/pallas_call | solution.py:504
  3.3 8.1 %collective-permute-start = (f32[12,128]{1,0:T(8,128)}, f32[12,128]{1,0:T(8,128)S(1)}, u32[]{:S(2)}, u32[]{:S(2)}) collective-permute-start(f32[12,128]{1,0:T(8,128)} %get-tuple-element.56), channel_id=1, source_target_pairs={{1,2},{3,4},{5,6},{7,8},{9,10},{11,12},{13,14},{15,16},{17,18},{19... | collective-permute-start | bytes 18440 | tf_op jit(solution)/shard_map/ppermute | solution.py:535
  13.4 4.8 %collective-permute-start.2 = (f32[12,128]{1,0:T(8,128)}, f32[12,128]{1,0:T(8,128)S(1)}, u32[]{:S(2)}, u32[]{:S(2)}) collective-permute-start(f32[12,128]{1,0:T(8,128)} %get-tuple-element.58), channel_id=1, source_target_pairs={{32,64},{96,128},{160,192},{224,256},{288,320},{352,384},{416,448}... | collective-permute-start | bytes 18440 | tf_op jit(solution)/shard_map/ppermute | solution.py:525
  27.8 4.3 %collective-permute-start.4 = (f32[4,128]{1,0:T(4,128)S(1)}, f32[4,128]{1,0:T(4,128)S(1)}, u32[]{:S(2)}, u32[]{:S(2)}) collective-permute-start(f32[4,128]{1,0:T(4,128)S(1)} %get-tuple-element.68), channel_id=1, source_target_pairs={{1,2},{3,4},{5,6},{7,8},{9,10},{11,12},{13,14},{15,16},{17,18},{19... | collective-permute-start | bytes 6152 | tf_op jit(solution)/shard_map/ppermute | solution.py:535
  32.2 1.9 %collective-permute-start.5 = (f32[4,128]{1,0:T(4,128)S(1)}, f32[4,128]{1,0:T(4,128)S(1)}, u32[]{:S(2)}, u32[]{:S(2)}) collective-permute-start(f32[4,128]{1,0:T(4,128)S(1)} %get-tuple-element.69), channel_id=1, source_target_pairs={{0,1},{2,3},{4,5},{6,7},{8,9},{10,11},{12,13},{14,15},{16,17},{18,... | collective-permute-start | bytes 6152 | tf_op jit(solution)/shard_map/ppermute | solution.py:536
  34.1 4.7 %collective-permute-start.6 = (f32[4,128]{1,0:T(4,128)S(1)}, f32[4,128]{1,0:T(4,128)S(1)}, u32[]{:S(2)}, u32[]{:S(2)}) collective-permute-start(f32[4,128]{1,0:T(4,128)S(1)} %get-tuple-element.70), channel_id=1, source_target_pairs={{32,64},{96,128},{160,192},{224,256},{288,320},{352,384},{416,448}... | collective-permute-start | bytes 6152 | tf_op jit(solution)/shard_map/ppermute | solution.py:525
  38.8 1.9 %collective-permute-start.7 = (f32[4,128]{1,0:T(4,128)S(1)}, f32[4,128]{1,0:T(4,128)S(1)}, u32[]{:S(2)}, u32[]{:S(2)}) collective-permute-start(f32[4,128]{1,0:T(4,128)S(1)} %get-tuple-element.71), channel_id=1, source_target_pairs={{0,32},{64,96},{128,160},{192,224},{256,288},{320,352},{384,416},{... | collective-permute-start | bytes 6152 | tf_op jit(solution)/shard_map/ppermute | solution.py:538
  42.5 4.1 %collective-permute-start.8 = (f32[4,128]{1,0:T(4,128)S(1)}, f32[4,128]{1,0:T(4,128)S(1)}, u32[]{:S(2)}, u32[]{:S(2)}) collective-permute-start(f32[4,128]{1,0:T(4,128)S(1)} %get-tuple-element.75), channel_id=1, source_target_pairs={{32,64},{96,128},{160,192},{224,256},{288,320},{352,384},{416,448}... | collective-permute-start | bytes 6152 | tf_op jit(solution)/shard_map/ppermute | solution.py:525
  48.4 15.4 %all_to_all.20.row_ref = f32[32,4,4,128]{3,2,1,0:T(4,128)S(1)} all-to-all(f32[32,4,4,128]{3,2,1,0:T(4,128)S(1)} %row.2), channel_id=1, replica_groups=mesh['lat'=16,'lon'=32] {'lon'}, dimensions={0} | all-to-all | bytes 524288 | tf_op jit(solution)/shard_map/all_to_all | solution.py:543
  63.8 4.5 %all-gather.1 = f32[6,4,128]{2,1,0:T(4,128)S(1)} all-gather(f32[3,4,128]{2,1,0:T(4,128)S(1)} %get-tuple-element.79), channel_id=3, replica_groups={{0,32},{64,96},{128,160},{192,224},{256,288},{320,352},{384,416},{448,4..., dimensions={0}, use_global_device_ids=true | all-gather | bytes 18432 | tf_op jit(solution)/shard_map/all_gather | solution.py:529
  68.3 5.4 %collective-permute-start.9 = (f32[6,4,128]{2,1,0:T(4,128)S(1)}, f32[6,4,128]{2,1,0:T(4,128)S(1)}, u32[]{:S(2)}, u32[]{:S(2)}) collective-permute-start(f32[6,4,128]{2,1,0:T(4,128)S(1)} %all-gather.1), channel_id=1, source_target_pairs={{32,64},{96,128},{160,192},{224,256},{288,320},{352,384},{416,448}... | collective-permute-start | bytes 36872 | tf_op jit(solution)/shard_map/ppermute | solution.py:525
  78.1 3.7 %collective-permute-start.10 = (f32[4,128]{1,0:T(4,128)S(1)}, f32[4,128]{1,0:T(4,128)S(1)}, u32[]{:S(2)}, u32[]{:S(2)}) collective-permute-start(f32[4,128]{1,0:T(4,128)S(1)} %get-tuple-element.84), channel_id=1, source_target_pairs={{1,2},{3,4},{5,6},{7,8},{9,10},{11,12},{13,14},{15,16},{17,18},{19... | collective-permute-start | bytes 6152 | tf_op jit(solution)/shard_map/ppermute | solution.py:535
  81.8 2.3 %collective-permute-start.11 = (f32[4,128]{1,0:T(4,128)S(1)}, f32[4,128]{1,0:T(4,128)S(1)}, u32[]{:S(2)}, u32[]{:S(2)}) collective-permute-start(f32[4,128]{1,0:T(4,128)S(1)} %get-tuple-element.85), channel_id=1, source_target_pairs={{0,1},{2,3},{4,5},{6,7},{8,9},{10,11},{12,13},{14,15},{16,17},{18,... | collective-permute-start | bytes 6152 | tf_op jit(solution)/shard_map/ppermute | solution.py:536
  84.1 4.2 %collective-permute-start.12 = (f32[4,128]{1,0:T(4,128)S(1)}, f32[4,128]{1,0:T(4,128)S(1)}, u32[]{:S(2)}, u32[]{:S(2)}) collective-permute-start(f32[4,128]{1,0:T(4,128)S(1)} %get-tuple-element.86), channel_id=1, source_target_pairs={{32,64},{96,128},{160,192},{224,256},{288,320},{352,384},{416,448}... | collective-permute-start | bytes 6152 | tf_op jit(solution)/shard_map/ppermute | solution.py:525
  88.3 1.9 %collective-permute-start.13 = (f32[4,128]{1,0:T(4,128)S(1)}, f32[4,128]{1,0:T(4,128)S(1)}, u32[]{:S(2)}, u32[]{:S(2)}) collective-permute-start(f32[4,128]{1,0:T(4,128)S(1)} %get-tuple-element.87), channel_id=1, source_target_pairs={{0,32},{64,96},{128,160},{192,224},{256,288},{320,352},{384,416},{... | collective-permute-start | bytes 6152 | tf_op jit(solution)/shard_map/ppermute | solution.py:538
  91.8 4.3 %collective-permute-start.14 = (f32[4,128]{1,0:T(4,128)S(1)}, f32[4,128]{1,0:T(4,128)S(1)}, u32[]{:S(2)}, u32[]{:S(2)}) collective-permute-start(f32[4,128]{1,0:T(4,128)S(1)} %get-tuple-element.90), channel_id=1, source_target_pairs={{1,2},{3,4},{5,6},{7,8},{9,10},{11,12},{13,14},{15,16},{17,18},{19... | collective-permute-start | bytes 6152 | tf_op jit(solution)/shard_map/ppermute | solution.py:535
  96.1 1.9 %collective-permute-start.15 = (f32[4,128]{1,0:T(4,128)S(1)}, f32[4,128]{1,0:T(4,128)S(1)}, u32[]{:S(2)}, u32[]{:S(2)}) collective-permute-start(f32[4,128]{1,0:T(4,128)S(1)} %get-tuple-element.91), channel_id=1, source_target_pairs={{0,1},{2,3},{4,5},{6,7},{8,9},{10,11},{12,13},{14,15},{16,17},{18,... | collective-permute-start | bytes 6152 | tf_op jit(solution)/shard_map/ppermute | solution.py:536
  98.1 3.4 %collective-permute-start.16 = (f32[4,128]{1,0:T(4,128)S(1)}, f32[4,128]{1,0:T(4,128)S(1)}, u32[]{:S(2)}, u32[]{:S(2)}) collective-permute-start(f32[4,128]{1,0:T(4,128)S(1)} %get-tuple-element.92), channel_id=1, source_target_pairs={{32,64},{96,128},{160,192},{224,256},{288,320},{352,384},{416,448}... | collective-permute-start | bytes 6152 | tf_op jit(solution)/shard_map/ppermute | solution.py:525
  105.2 4.2 %collective-permute-start.18 = (f32[4,128]{1,0:T(4,128)S(1)}, f32[4,128]{1,0:T(4,128)S(1)}, u32[]{:S(2)}, u32[]{:S(2)}) collective-permute-start(f32[4,128]{1,0:T(4,128)S(1)} %get-tuple-element.95), channel_id=1, source_target_pairs={{32,64},{96,128},{160,192},{224,256},{288,320},{352,384},{416,448}... | collective-permute-start | bytes 6152 | tf_op jit(solution)/shard_map/ppermute | solution.py:525
  111.2 15.2 %all_to_all.21.row_ref = f32[32,3,4,128]{3,2,1,0:T(4,128)S(1)} all-to-all(f32[32,3,4,128]{3,2,1,0:T(4,128)S(1)} %row.3), channel_id=1, replica_groups=mesh['lat'=16,'lon'=32] {'lon'}, dimensions={0} | all-to-all | bytes 393216 | tf_op jit(solution)/shard_map/all_to_all | solution.py:543
  126.5 4.5 %all-gather.4 = f32[6,4,128]{2,1,0:T(4,128)S(1)} all-gather(f32[3,4,128]{2,1,0:T(4,128)S(1)} %get-tuple-element.99), channel_id=6, replica_groups={{0,32},{64,96},{128,160},{192,224},{256,288},{320,352},{384,416},{448,4..., dimensions={0}, use_global_device_ids=true | all-gather | bytes 18432 | tf_op jit(solution)/shard_map/all_gather | solution.py:529
  131.0 3.7 %collective-permute-start.19 = (f32[6,4,128]{2,1,0:T(4,128)S(1)}, f32[6,4,128]{2,1,0:T(4,128)S(1)}, u32[]{:S(2)}, u32[]{:S(2)}) collective-permute-start(f32[6,4,128]{2,1,0:T(4,128)S(1)} %all-gather.4), channel_id=1, source_target_pairs={{32,64},{96,128},{160,192},{224,256},{288,320},{352,384},{416,448}... | collective-permute-start | bytes 36872 | tf_op jit(solution)/shard_map/ppermute | solution.py:525
  139.0 14.2 %all_to_all.22 = f32[16,1,128]{2,1,0:T(1,128)S(1)} all-to-all(f32[16,1,128]{2,1,0:T(1,128)S(1)} %get-tuple-element.102), channel_id=1, replica_groups=mesh['lat'=16,'lon'=32] {'lat'}, dimensions={0} | all-to-all | bytes 16384 | tf_op jit(solution)/shard_map/all_to_all | solution.py:543
  153.2 12.3 %all_to_all.23.sums_ref = f32[32,1,128]{2,1,0:T(1,128)S(1)} all-to-all(f32[32,1,128]{2,1,0:T(1,128)S(1)} %broadcast_in_dim.2), channel_id=1, replica_groups=mesh['lat'=16,'lon'=32] {'lon'}, dimensions={0} | all-to-all | bytes 32768 | tf_op jit(solution)/shard_map/all_to_all | solution.py:543
  (72 shorter events, 32.1 us)
Async XLA Ops:
  3.3 23.8 %copy-start.10 = (f32[1,1024]{1,0:T(1,128)S(1)}, f32[1,1024]{1,0:T(1,128)}, u32[]{:S(2)}) copy-start(f32[1,1024]{1,0:T(1,128)} %get-tuple-element.62.coef_ref) | copy-start | bytes 12292
  3.3 23.8 %copy-start.12 = (f32[4,128]{1,0:T(4,128)S(1)}, f32[4,128]{1,0:T(4,128)}, u32[]{:S(2)}) copy-start(f32[4,128]{1,0:T(4,128)} %get-tuple-element.60.own_ref) | copy-start | bytes 6148
  3.3 23.7 %collective-permute-start = (f32[12,128]{1,0:T(8,128)}, f32[12,128]{1,0:T(8,128)S(1)}, u32[]{:S(2)}, u32[]{:S(2)}) collective-permute-start(f32[12,128]{1,0:T(8,128)} %get-tuple-element.56), channel_id=1, source_target_pairs={{1,2},{3,4},{5,6},{7,8},{9,10},{11,12},{13,14},{15,16},{17,18},{19... | collective-permute-start | bytes 18440 | tf_op jit(solution)/shard_map/ppermute | solution.py:535
  11.5 15.6 %collective-permute-start.1 = (f32[12,128]{1,0:T(8,128)}, f32[12,128]{1,0:T(8,128)S(1)}, u32[]{:S(2)}, u32[]{:S(2)}) collective-permute-start(f32[12,128]{1,0:T(8,128)} %get-tuple-element.57), channel_id=1, source_target_pairs={{0,1},{2,3},{4,5},{6,7},{8,9},{10,11},{12,13},{14,15},{16,17},{18,... | collective-permute-start | bytes 18440 | tf_op jit(solution)/shard_map/ppermute | solution.py:536
  13.4 13.7 %collective-permute-start.2 = (f32[12,128]{1,0:T(8,128)}, f32[12,128]{1,0:T(8,128)S(1)}, u32[]{:S(2)}, u32[]{:S(2)}) collective-permute-start(f32[12,128]{1,0:T(8,128)} %get-tuple-element.58), channel_id=1, source_target_pairs={{32,64},{96,128},{160,192},{224,256},{288,320},{352,384},{416,448}... | collective-permute-start | bytes 18440 | tf_op jit(solution)/shard_map/ppermute | solution.py:525
  18.2 8.9 %collective-permute-start.3 = (f32[12,128]{1,0:T(8,128)}, f32[12,128]{1,0:T(8,128)S(1)}, u32[]{:S(2)}, u32[]{:S(2)}) collective-permute-start(f32[12,128]{1,0:T(8,128)} %get-tuple-element.59), channel_id=1, source_target_pairs={{0,32},{64,96},{128,160},{192,224},{256,288},{320,352},{384,416},{... | collective-permute-start | bytes 18440 | tf_op jit(solution)/shard_map/ppermute | solution.py:538
  27.1 49.8 %copy-start.3 = (s32[1,1,2,2048]{3,2,1,0:T(2,128)S(1)}, s32[1,1,2,2048]{3,2,1,0:T(2,128)}, u32[]{:S(2)}) copy-start(s32[1,1,2,2048]{3,2,1,0:T(2,128)} %nodes_ref.11) | copy-start | bytes 49156
  27.1 49.8 %copy-start.8 = (s32[1,1,4,256]{3,2,1,0:T(4,128)S(1)}, s32[1,1,4,256]{3,2,1,0:T(4,128)}, u32[]{:S(2)}) copy-start(s32[1,1,4,256]{3,2,1,0:T(4,128)} %idx_ref.15) | copy-start | bytes 12292
  27.8 13.4 %collective-permute-start.4 = (f32[4,128]{1,0:T(4,128)S(1)}, f32[4,128]{1,0:T(4,128)S(1)}, u32[]{:S(2)}, u32[]{:S(2)}) collective-permute-start(f32[4,128]{1,0:T(4,128)S(1)} %get-tuple-element.68), channel_id=1, source_target_pairs={{1,2},{3,4},{5,6},{7,8},{9,10},{11,12},{13,14},{15,16},{17,18},{19... | collective-permute-start | bytes 6152 | tf_op jit(solution)/shard_map/ppermute | solution.py:535
  32.2 9.1 %collective-permute-start.5 = (f32[4,128]{1,0:T(4,128)S(1)}, f32[4,128]{1,0:T(4,128)S(1)}, u32[]{:S(2)}, u32[]{:S(2)}) collective-permute-start(f32[4,128]{1,0:T(4,128)S(1)} %get-tuple-element.69), channel_id=1, source_target_pairs={{0,1},{2,3},{4,5},{6,7},{8,9},{10,11},{12,13},{14,15},{16,17},{18,... | collective-permute-start | bytes 6152 | tf_op jit(solution)/shard_map/ppermute | solution.py:536
  34.1 7.2 %collective-permute-start.6 = (f32[4,128]{1,0:T(4,128)S(1)}, f32[4,128]{1,0:T(4,128)S(1)}, u32[]{:S(2)}, u32[]{:S(2)}) collective-permute-start(f32[4,128]{1,0:T(4,128)S(1)} %get-tuple-element.70), channel_id=1, source_target_pairs={{32,64},{96,128},{160,192},{224,256},{288,320},{352,384},{416,448}... | collective-permute-start | bytes 6152 | tf_op jit(solution)/shard_map/ppermute | solution.py:525
  38.8 3.1 %collective-permute-start.7 = (f32[4,128]{1,0:T(4,128)S(1)}, f32[4,128]{1,0:T(4,128)S(1)}, u32[]{:S(2)}, u32[]{:S(2)}) collective-permute-start(f32[4,128]{1,0:T(4,128)S(1)} %get-tuple-element.71), channel_id=1, source_target_pairs={{0,32},{64,96},{128,160},{192,224},{256,288},{320,352},{384,416},{... | collective-permute-start | bytes 6152 | tf_op jit(solution)/shard_map/ppermute | solution.py:538
  42.5 5.9 %collective-permute-start.8 = (f32[4,128]{1,0:T(4,128)S(1)}, f32[4,128]{1,0:T(4,128)S(1)}, u32[]{:S(2)}, u32[]{:S(2)}) collective-permute-start(f32[4,128]{1,0:T(4,128)S(1)} %get-tuple-element.75), channel_id=1, source_target_pairs={{32,64},{96,128},{160,192},{224,256},{288,320},{352,384},{416,448}... | collective-permute-start | bytes 6152 | tf_op jit(solution)/shard_map/ppermute | solution.py:525
  68.3 6.8 %collective-permute-start.9 = (f32[6,4,128]{2,1,0:T(4,128)S(1)}, f32[6,4,128]{2,1,0:T(4,128)S(1)}, u32[]{:S(2)}, u32[]{:S(2)}) collective-permute-start(f32[6,4,128]{2,1,0:T(4,128)S(1)} %all-gather.1), channel_id=1, source_target_pairs={{32,64},{96,128},{160,192},{224,256},{288,320},{352,384},{416,448}... | collective-permute-start | bytes 36872 | tf_op jit(solution)/shard_map/ppermute | solution.py:525
  78.1 12.7 %collective-permute-start.10 = (f32[4,128]{1,0:T(4,128)S(1)}, f32[4,128]{1,0:T(4,128)S(1)}, u32[]{:S(2)}, u32[]{:S(2)}) collective-permute-start(f32[4,128]{1,0:T(4,128)S(1)} %get-tuple-element.84), channel_id=1, source_target_pairs={{1,2},{3,4},{5,6},{7,8},{9,10},{11,12},{13,14},{15,16},{17,18},{19... | collective-permute-start | bytes 6152 | tf_op jit(solution)/shard_map/ppermute | solution.py:535
  81.8 9.0 %collective-permute-start.11 = (f32[4,128]{1,0:T(4,128)S(1)}, f32[4,128]{1,0:T(4,128)S(1)}, u32[]{:S(2)}, u32[]{:S(2)}) collective-permute-start(f32[4,128]{1,0:T(4,128)S(1)} %get-tuple-element.85), channel_id=1, source_target_pairs={{0,1},{2,3},{4,5},{6,7},{8,9},{10,11},{12,13},{14,15},{16,17},{18,... | collective-permute-start | bytes 6152 | tf_op jit(solution)/shard_map/ppermute | solution.py:536
  84.1 6.7 %collective-permute-start.12 = (f32[4,128]{1,0:T(4,128)S(1)}, f32[4,128]{1,0:T(4,128)S(1)}, u32[]{:S(2)}, u32[]{:S(2)}) collective-permute-start(f32[4,128]{1,0:T(4,128)S(1)} %get-tuple-element.86), channel_id=1, source_target_pairs={{32,64},{96,128},{160,192},{224,256},{288,320},{352,384},{416,448}... | collective-permute-start | bytes 6152 | tf_op jit(solution)/shard_map/ppermute | solution.py:525
  88.3 3.1 %collective-permute-start.13 = (f32[4,128]{1,0:T(4,128)S(1)}, f32[4,128]{1,0:T(4,128)S(1)}, u32[]{:S(2)}, u32[]{:S(2)}) collective-permute-start(f32[4,128]{1,0:T(4,128)S(1)} %get-tuple-element.87), channel_id=1, source_target_pairs={{0,32},{64,96},{128,160},{192,224},{256,288},{320,352},{384,416},{... | collective-permute-start | bytes 6152 | tf_op jit(solution)/shard_map/ppermute | solution.py:538
  91.8 12.1 %collective-permute-start.14 = (f32[4,128]{1,0:T(4,128)S(1)}, f32[4,128]{1,0:T(4,128)S(1)}, u32[]{:S(2)}, u32[]{:S(2)}) collective-permute-start(f32[4,128]{1,0:T(4,128)S(1)} %get-tuple-element.90), channel_id=1, source_target_pairs={{1,2},{3,4},{5,6},{7,8},{9,10},{11,12},{13,14},{15,16},{17,18},{19... | collective-permute-start | bytes 6152 | tf_op jit(solution)/shard_map/ppermute | solution.py:535
  96.1 7.9 %collective-permute-start.15 = (f32[4,128]{1,0:T(4,128)S(1)}, f32[4,128]{1,0:T(4,128)S(1)}, u32[]{:S(2)}, u32[]{:S(2)}) collective-permute-start(f32[4,128]{1,0:T(4,128)S(1)} %get-tuple-element.91), channel_id=1, source_target_pairs={{0,1},{2,3},{4,5},{6,7},{8,9},{10,11},{12,13},{14,15},{16,17},{18,... | collective-permute-start | bytes 6152 | tf_op jit(solution)/shard_map/ppermute | solution.py:536
  98.1 5.9 %collective-permute-start.16 = (f32[4,128]{1,0:T(4,128)S(1)}, f32[4,128]{1,0:T(4,128)S(1)}, u32[]{:S(2)}, u32[]{:S(2)}) collective-permute-start(f32[4,128]{1,0:T(4,128)S(1)} %get-tuple-element.92), channel_id=1, source_target_pairs={{32,64},{96,128},{160,192},{224,256},{288,320},{352,384},{416,448}... | collective-permute-start | bytes 6152 | tf_op jit(solution)/shard_map/ppermute | solution.py:525
  101.5 3.1 %collective-permute-start.17 = (f32[4,128]{1,0:T(4,128)S(1)}, f32[4,128]{1,0:T(4,128)S(1)}, u32[]{:S(2)}, u32[]{:S(2)}) collective-permute-start(f32[4,128]{1,0:T(4,128)S(1)} %get-tuple-element.93), channel_id=1, source_target_pairs={{0,32},{64,96},{128,160},{192,224},{256,288},{320,352},{384,416},{... | collective-permute-start | bytes 6152 | tf_op jit(solution)/shard_map/ppermute | solution.py:538
  105.2 6.0 %collective-permute-start.18 = (f32[4,128]{1,0:T(4,128)S(1)}, f32[4,128]{1,0:T(4,128)S(1)}, u32[]{:S(2)}, u32[]{:S(2)}) collective-permute-start(f32[4,128]{1,0:T(4,128)S(1)} %get-tuple-element.95), channel_id=1, source_target_pairs={{32,64},{96,128},{160,192},{224,256},{288,320},{352,384},{416,448}... | collective-permute-start | bytes 6152 | tf_op jit(solution)/shard_map/ppermute | solution.py:525
  131.0 5.1 %collective-permute-start.19 = (f32[6,4,128]{2,1,0:T(4,128)S(1)}, f32[6,4,128]{2,1,0:T(4,128)S(1)}, u32[]{:S(2)}, u32[]{:S(2)}) collective-permute-start(f32[6,4,128]{2,1,0:T(4,128)S(1)} %all-gather.4), channel_id=1, source_target_pairs={{32,64},{96,128},{160,192},{224,256},{288,320},{352,384},{416,448}... | collective-permute-start | bytes 36872 | tf_op jit(solution)/shard_map/ppermute | solution.py:525
  (9 other events, 28.2 us)

commit v5 on v4

--- a/solution.py
+++ b/solution.py
@@ -17,7 +17,8 @@
 F32 = jnp.float32
 BF16 = jnp.bfloat16
 LIMIT = 20 * 1024 * 1024
-BEGIN_LIMIT = 60 * 1024 * 1024
+PACK_LIMIT = 60 * 1024 * 1024
+RIGHT, COND, COEF, INDEX, TAILS, HEADS, PACKED = 0, 32, 48, 56, 64, 80, 96
 NT = (((1,), (1,)), ((), ()))
 
 
@@ -35,6 +36,11 @@
     rest = x - first
     second = rest.astype(BF16).astype(F32)
     return first, second, rest - second
+
+
+def split(block):
+    high = block.astype(BF16)
+    return jnp.concatenate([high, (block - high.astype(F32)).astype(BF16)], axis=1)
 
 
 def lanes(x, count):
@@ -123,9 +129,16 @@
     )
 
 
-def index_rows(idx_ref):
-    idx = idx_ref[0, 0]
-    return jnp.concatenate([idx[d : d + 1] for d in range(4)], axis=1)
+def index_rows(pack_ref):
+    return lanes(pack_ref[INDEX : INDEX + 8], 8).astype(jnp.int32)
+
+
+def ends_rows(pack_ref):
+    return [lanes(pack_ref[at : at + EB], EB).astype(jnp.int32) for at in (TAILS, HEADS)]
+
+
+def coef_row(pack_ref):
+    return lanes(pack_ref[COEF : COEF + 8], 8)
 
 
 def interface_messages(field, onehot, index):
@@ -154,8 +167,8 @@
     return put(rows, onehot, block_mask(index // BS, EB))
 
 
-def pair(ref):
-    return ref[0:EB], ref[EB : 2 * EB]
+def pair(ref, at=0):
+    return ref[at : at + EB], ref[at + EB : at + 2 * EB]
 
 
 def keep(ref, value):
@@ -163,9 +176,8 @@
     ref[EB : 2 * EB] = value[1]
 
 
-def nodal(rows, onehot_head, onehot_tail, nodes_ref, sign):
-    tails = nodes_ref[0, 0, 0:1]
-    heads = nodes_ref[0, 0, 1:2]
+def nodal(rows, onehot_head, onehot_tail, pack_ref, sign):
+    tails, heads = ends_rows(pack_ref)
     own = put_heads(rows, onehot_head, heads // BS)
     ext = put(rows, onehot_tail, block_mask(tails // BS, EB))
     parts = [
@@ -175,76 +187,77 @@
     return own[0:4] + parts[0], parts[1:]
 
 
-def begin_kernel(
-    rhs_ref, cond_ref, diag_ref, idx_ref, cnt_ref, coup_ref, nodes_ref,
-    m0, m1, m2, m3, coef_ref, value_ref, scale_ref, right_ref, first_ref, own_ref,
-    ohi_ref, oht_ref, ohh_ref, blocks, rhs_got, cond_got, diag_got, idx_got, cnt_got, coup_got, nodes_got, sems,
-):
-    messages = (m0, m1, m2, m3)
+def pack_kernel(
+    rhs_ref, cond_ref, coup_ref, cnt_ref, idx_ref, nodes_ref, pack_ref,
+    rhs_got, cond_got, coup_got, cnt_got, idx_got, nodes_got, sems,
+):
     pairs = (
-        (nodes_ref, nodes_got), (idx_ref, idx_got), (cnt_ref, cnt_got), (coup_ref, coup_got),
-        (cond_ref, cond_got), (rhs_ref, rhs_got), (diag_ref, diag_got),
+        (rhs_ref, rhs_got), (cond_ref, cond_got), (coup_ref, coup_got),
+        (cnt_ref, cnt_got), (idx_ref, idx_got), (nodes_ref, nodes_got),
     )
     copies = [pltpu.make_async_copy(here, there, sems.at[k]) for k, (here, there) in enumerate(pairs)]
     for copy in copies:
         copy.start()
-    for copy in copies[:2]:
+    for copy in copies:
         copy.wait()
-    nodes_ref, idx_ref, cnt_ref, coup_ref, cond_ref, rhs_ref, diag_ref = [there for _, there in pairs]
-    index = index_rows(idx_ref)
+
+    def rows(at, row):
+        for k in range(row.shape[1] // BS):
+            pack_ref[at + k : at + k + 1] = row[:, k * BS : (k + 1) * BS]
+
+    for c in range(2):
+        rows(RIGHT + EB * c, rhs_got[c, 0])
+        rows((TAILS, HEADS)[c], nodes_got[0, 0, c : c + 1].astype(F32))
+    rows(COND, cond_got[0])
+    slot = lax.broadcasted_iota(jnp.int32, (1, IFC), 1)
+    for d in range(4):
+        rows(COEF + 2 * d, jnp.where(slot < cnt_got[0, 0, d], coup_got[0, 0, d : d + 1], 0.0))
+        rows(INDEX + 2 * d, idx_got[0, 0, d : d + 1].astype(F32))
+
+
+def begin_kernel(
+    pack_ref, diag_ref,
+    m0, m1, m2, m3, value_ref, scale_ref, first_ref, own_ref,
+    ohi_ref, oht_ref, ohh_ref, wd_ref,
+):
+    messages = (m0, m1, m2, m3)
+    index = index_rows(pack_ref)
+    tails, heads = ends_rows(pack_ref)
     ohi_ref[...] = lane_onehot(index)
-    oht_ref[...] = lane_onehot(nodes_ref[0, 0, 0:1])
-    ohh_ref[...] = lane_onehot(nodes_ref[0, 0, 1:2])
-    for copy in copies[2:]:
-        copy.wait()
-    slot = lax.broadcasted_iota(jnp.int32, (1, IFC), 1)
-    coef_ref[...] = jnp.concatenate(
-        [jnp.where(slot < cnt_ref[0, 0, d], coup_ref[0, 0, d : d + 1], 0.0) for d in range(4)], axis=1
-    )
+    oht_ref[...] = lane_onehot(tails)
+    ohh_ref[...] = lane_onehot(heads)
     eye = lax.broadcasted_iota(jnp.int32, (BS, BS), 0) == lax.broadcasted_iota(jnp.int32, (BS, BS), 1)
     for b in range(EB):
-        value_ref[b : b + 1] = jnp.sum(jnp.where(eye, diag_ref[0, 0, b], 0.0), axis=0, keepdims=True)
-    value_ref[EB : 2 * EB] = to_blocks(cond_ref[0], blocks)
+        block = diag_ref[0, 0, b]
+        value_ref[b : b + 1] = jnp.sum(jnp.where(eye, block, 0.0), axis=0, keepdims=True)
+        wd_ref[b] = split(jnp.where(eye, 0.0, block))
+    value_ref[EB : 2 * EB] = pack_ref[COND : COND + EB]
     value = pair(value_ref)
     inverse = complex_inverse(value)
     scale = (OMEGA * inverse[0], OMEGA * inverse[1])
     keep(scale_ref, scale)
-    for c in range(2):
-        right_ref[EB * c : EB * c + EB] = to_blocks(rhs_ref[c, 0], blocks)
-    first = complex_times(scale, pair(right_ref))
+    first = complex_times(scale, pair(pack_ref, RIGHT))
     keep(first_ref, first)
     hand_out(messages, interface_messages(first, ohi_ref, index), 0)
     rows = [lanes(value[c], EB) for c in range(2)]
-    own, towards = nodal(rows, ohh_ref, oht_ref, nodes_ref, 1.0)
+    own, towards = nodal(rows, ohh_ref, oht_ref, pack_ref, 1.0)
     own_ref[0:4] = own
     hand_out(messages, towards, 4)
-    ends = [to_blocks(nodes_ref[0, 0, k : k + 1].astype(F32), blocks) for k in (1, 0)]
+    ends = [pack_ref[at : at + EB] for at in (HEADS, TAILS)]
     hand_out(messages, interface_messages(ends, ohi_ref, index), 8)
 
 
-def weight_kernel(diag_ref, off_ref, idx_ref, nodes_ref, w_ref, ohi_ref, oht_ref, ohh_ref):
-    ohi_ref[...] = lane_onehot(index_rows(idx_ref))
-    oht_ref[...] = lane_onehot(nodes_ref[0, 0, 0:1])
-    ohh_ref[...] = lane_onehot(nodes_ref[0, 0, 1:2])
-    eye = lax.broadcasted_iota(jnp.int32, (BS, BS), 0) == lax.broadcasted_iota(jnp.int32, (BS, BS), 1)
-
-    def store(b, at, block):
-        high = block.astype(BF16)
-        w_ref[b, at : at + BS, 0:BS] = high
-        w_ref[b, at : at + BS, BS:] = (block - high.astype(F32)).astype(BF16)
-
+def weight_kernel(off_ref, wo_ref):
     zero = jnp.zeros((BS, 2 * BS), BF16)
-    w_ref[0, 0:BS] = zero
-    w_ref[EB - 1, 2 * BS :] = zero
-    for b in range(EB):
-        store(b, BS, jnp.where(eye, 0.0, diag_ref[0, 0, b]))
-        if b < EB - 1:
-            off = off_ref[0, 0, b]
-            store(b + 1, 0, off)
-            store(b, 2 * BS, off.T)
-
-
-def stiffness(field, value, w_ref, wide, out):
+    wo_ref[0, 0:BS] = zero
+    wo_ref[EB - 1, BS:] = zero
+    for b in range(EB - 1):
+        off = off_ref[0, 0, b]
+        wo_ref[b + 1, 0:BS] = split(off)
+        wo_ref[b, BS:] = split(off.T)
+
+
+def stiffness(field, value, wd_ref, wo_ref, wide, out):
     wide[0:8] = jnp.zeros((8, BS), F32)
     wide[8 * (EB + 1) :] = jnp.zeros((8, BS), F32)
     for c in range(2):
@@ -253,8 +266,10 @@
     for k in (6, 7):
         wide[pl.ds(8 + k, EB, stride=8)] = jnp.zeros((EB, BS), F32)
     for b in range(EB):
-        around = jnp.concatenate([wide[8 * (b + k) : 8 * (b + k) + 8] for k in range(3)], axis=1)
-        got = jnp.dot(around.astype(BF16), w_ref[b], preferred_element_type=F32)
+        low, here, high = [wide[8 * (b + k) : 8 * (b + k) + 8] for k in range(3)]
+        beside = jnp.concatenate([low, high], axis=1)
+        got = jnp.dot(here.astype(BF16), wd_ref[b], preferred_element_type=F32)
+        got = got + jnp.dot(beside.astype(BF16), wo_ref[b], preferred_element_type=F32)
         out[8 * b : 8 * b + 8] = got[:, :BS] + got[:, BS:]
     sums = [
         out[pl.ds(c, EB, stride=8)] + out[pl.ds(2 + c, EB, stride=8)] + out[pl.ds(4 + c, EB, stride=8)]
@@ -264,13 +279,13 @@
     return sums[0] + turned[0], sums[1] + turned[1]
 
 
-def local_kernel(field_ref, value_ref, w_ref, out_ref, wide, out):
-    keep(out_ref, stiffness(pair(field_ref), pair(value_ref), w_ref, wide, out))
-
-
-def smooth(arrived, ohi_ref, coef_ref, idx_ref, first_ref, local_ref, scale_ref, right_ref, m, second_ref):
-    index = index_rows(idx_ref)
-    extra = interface_sum(arrived, coef_ref[...], ohi_ref, index)
+def local_kernel(field_ref, value_ref, wd_ref, wo_ref, out_ref, wide, out):
+    keep(out_ref, stiffness(pair(field_ref), pair(value_ref), wd_ref, wo_ref, wide, out))
+
+
+def smooth(arrived, ohi_ref, pack_ref, first_ref, local_ref, scale_ref, right_ref, m, second_ref):
+    index = index_rows(pack_ref)
+    extra = interface_sum(arrived, coef_row(pack_ref), ohi_ref, index)
     first, local, right = pair(first_ref), pair(local_ref), pair(right_ref)
     change = complex_times(pair(scale_ref), [right[c] - local[c] - extra[c] for c in range(2)])
     second = (first[0] + change[0], first[1] + change[1])
@@ -279,11 +294,11 @@
 
 
 def smooth_first_kernel(
-    a0, a1, a2, a3, own_ref, ohi_ref, coef_ref, idx_ref, first_ref, local_ref, scale_ref, right_ref,
+    a0, a1, a2, a3, own_ref, ohi_ref, pack_ref, first_ref, local_ref, scale_ref,
     m0, m1, m2, m3, second_ref, ninv_ref, ends_ref, oha_ref,
 ):
     arrived = collect((a0, a1, a2, a3))
-    smooth(arrived, ohi_ref, coef_ref, idx_ref, first_ref, local_ref, scale_ref, right_ref, (m0, m1, m2, m3), second_ref)
+    smooth(arrived, ohi_ref, pack_ref, first_ref, local_ref, scale_ref, pack_ref, (m0, m1, m2, m3), second_ref)
     sums = own_ref[0:4]
     for part in collect((a0, a1, a2, a3), 4):
         sums = sums + part
@@ -300,23 +315,23 @@
 
 
 def smooth_kernel(
-    a0, a1, a2, a3, ohi_ref, coef_ref, idx_ref, first_ref, local_ref, scale_ref, right_ref,
+    a0, a1, a2, a3, ohi_ref, pack_ref, first_ref, local_ref, scale_ref, right_ref,
     m0, m1, m2, m3, second_ref,
 ):
     arrived = collect((a0, a1, a2, a3))
-    smooth(arrived, ohi_ref, coef_ref, idx_ref, first_ref, local_ref, scale_ref, right_ref, (m0, m1, m2, m3), second_ref)
+    smooth(arrived, ohi_ref, pack_ref, first_ref, local_ref, scale_ref, right_ref, (m0, m1, m2, m3), second_ref)
 
 
 def restrict_kernel(
-    a0, a1, a2, a3, ohi_ref, oht_ref, ohh_ref, coef_ref, idx_ref, nodes_ref, local_ref, right_ref,
+    a0, a1, a2, a3, ohi_ref, oht_ref, ohh_ref, pack_ref, local_ref, right_ref,
     far_ref, core_ref, row_ref, extra_ref,
 ):
-    index = index_rows(idx_ref)
-    extra = interface_sum(collect((a0, a1, a2, a3)), coef_ref[...], ohi_ref, index)
+    index = index_rows(pack_ref)
+    extra = interface_sum(collect((a0, a1, a2, a3)), coef_row(pack_ref), ohi_ref, index)
     keep(extra_ref, extra)
     local, right = pair(local_ref), pair(right_ref)
     rows = [lanes(right[c] - local[c] - extra[c], EB) for c in range(2)]
-    own, towards = nodal(rows, ohh_ref, oht_ref, nodes_ref, -1.0)
+    own, towards = nodal(rows, ohh_ref, oht_ref, pack_ref, -1.0)
     even_lat, _ = parities()
     far_ref[...] = jnp.where(even_lat, towards[0], towards[1])
     core_ref[...] = jnp.where(even_lat, towards[1], towards[0])
@@ -366,8 +381,8 @@
 
 
 def prolong(
-    lat, chip_ref, away_ref, near_ref, ohi_ref, oht_ref, ohh_ref, coef_ref, idx_ref, nodes_ref, second_ref, extra_ref,
-    ends_ref, oha_ref, value_ref, w_ref, direction_ref, blocks, ext, wide, out, column,
+    lat, chip_ref, away_ref, near_ref, ohi_ref, oht_ref, ohh_ref, pack_ref, second_ref, extra_ref,
+    ends_ref, oha_ref, value_ref, wd_ref, wo_ref, direction_ref, blocks, ext, wide, out, column,
 ):
     me = lax.axis_index("lat")
 
@@ -387,7 +402,8 @@
         return [node(down + i, right + j) for i, j in steps]
 
     ext[...] = jnp.zeros((2 * EB, BS), F32)
-    rise = gradient(around(0, 0), ext, ohh_ref, oht_ref, nodes_ref[0, 0, 1:2], nodes_ref[0, 0, 0:1])
+    tails, heads = ends_rows(pack_ref)
+    rise = gradient(around(0, 0), ext, ohh_ref, oht_ref, heads, tails)
     second = pair(second_ref)
     direction = [second[c] + to_blocks(rise[c], blocks) for c in range(2)]
     keep(direction_ref, direction)
@@ -403,27 +419,27 @@
             real = (there >= 0) & (there < lat)
             rise = [jnp.where(real, part, 0.0) for part in rise]
         rises.append(rise)
-    rows = [jnp.concatenate([rise[c] for rise in rises], axis=1) * coef_ref[...] for c in range(2)]
-    more = put(rows, ohi_ref, block_mask(index_rows(idx_ref) // BS, EB))
+    rows = [jnp.concatenate([rise[c] for rise in rises], axis=1) * coef_row(pack_ref) for c in range(2)]
+    more = put(rows, ohi_ref, block_mask(index_rows(pack_ref) // BS, EB))
     extra = pair(extra_ref)
-    local = stiffness(direction, pair(value_ref), w_ref, wide, out)
+    local = stiffness(direction, pair(value_ref), wd_ref, wo_ref, wide, out)
     return [local[c] + extra[c] + more[c] for c in range(2)]
 
 
 def prolong_first_kernel(
-    lat, chip_ref, away_ref, near_ref, ohi_ref, oht_ref, ohh_ref, coef_ref, idx_ref, nodes_ref, second_ref, extra_ref,
-    ends_ref, oha_ref, value_ref, w_ref, scale_ref,
+    lat, chip_ref, away_ref, near_ref, ohi_ref, oht_ref, ohh_ref, pack_ref, second_ref, extra_ref,
+    ends_ref, oha_ref, value_ref, wd_ref, wo_ref, scale_ref,
     m0, m1, m2, m3, direction_ref, image_ref, first_ref,
     *scratch,
 ):
     image = prolong(
-        lat, chip_ref, away_ref, near_ref, ohi_ref, oht_ref, ohh_ref, coef_ref, idx_ref, nodes_ref, second_ref, extra_ref,
-        ends_ref, oha_ref, value_ref, w_ref, direction_ref, *scratch,
+        lat, chip_ref, away_ref, near_ref, ohi_ref, oht_ref, ohh_ref, pack_ref, second_ref, extra_ref,
+        ends_ref, oha_ref, value_ref, wd_ref, wo_ref, direction_ref, *scratch,
     )
     keep(image_ref, image)
     first = complex_times(pair(scale_ref), image)
     keep(first_ref, first)
-    hand_out((m0, m1, m2, m3), interface_messages(first, ohi_ref, index_rows(idx_ref)))
+    hand_out((m0, m1, m2, m3), interface_messages(first, ohi_ref, index_rows(pack_ref)))
 
 
 def total(x):
@@ -435,16 +451,16 @@
 
 
 def prolong_last_kernel(
-    lat, chip_ref, away_ref, near_ref, ohi_ref, oht_ref, ohh_ref, coef_ref, idx_ref, nodes_ref, second_ref, extra_ref,
-    ends_ref, oha_ref, value_ref, w_ref, right_ref, image_ref,
+    lat, chip_ref, away_ref, near_ref, ohi_ref, oht_ref, ohh_ref, pack_ref, second_ref, extra_ref,
+    ends_ref, oha_ref, value_ref, wd_ref, wo_ref, image_ref,
     direction_ref, image2_ref, sums_ref,
     *scratch,
 ):
     image2 = prolong(
-        lat, chip_ref, away_ref, near_ref, ohi_ref, oht_ref, ohh_ref, coef_ref, idx_ref, nodes_ref, second_ref, extra_ref,
-        ends_ref, oha_ref, value_ref, w_ref, direction_ref, *scratch,
-    )
-    right, image = pair(right_ref), pair(image_ref)
+        lat, chip_ref, away_ref, near_ref, ohi_ref, oht_ref, ohh_ref, pack_ref, second_ref, extra_ref,
+        ends_ref, oha_ref, value_ref, wd_ref, wo_ref, direction_ref, *scratch,
+    )
+    right, image = pair(pack_ref, RIGHT), pair(image_ref)
     keep(image2_ref, image2)
     rest = (right[0] - image[0], right[1] - image[1])
     turn = (image[0] - image2[0], image[1] - image2[1])
@@ -458,7 +474,7 @@
 
 
 def finish_kernel(
-    sums_ref, right_ref, image_ref, image2_ref, direction_ref, direction2_ref,
+    sums_ref, pack_ref, image_ref, image2_ref, direction_ref, direction2_ref,
     solution_ref, residual_ref, history_ref,
 ):
     row = jnp.sum(sums_ref[...], axis=0)
@@ -476,8 +492,9 @@
     ww2 = ww2 + (extra[0] * extra[0] + extra[1] * extra[1]) * ww - 2.0 * cross[0]
     alpha2 = (c2[0] / ww2, c2[1] / ww2)
     fresh2 = fresh - (c2[0] * alpha2[0] + c2[1] * alpha2[1])
-    history_ref[...] = jnp.where(lane == 0, fresh / start, fresh2 / start)
-    right, image, image2 = pair(right_ref), pair(image_ref), pair(image2_ref)
+    history_ref[0] = (fresh / start)[0, 0]
+    history_ref[1] = (fresh2 / start)[0, 0]
+    right, image, image2 = pair(pack_ref, RIGHT), pair(image_ref), pair(image2_ref)
     direction, direction2 = pair(direction_ref), pair(direction2_ref)
     step = complex_times(alpha, direction)
     other = complex_times(alpha, direction2)
@@ -498,14 +515,14 @@
 MESSAGES = [shape(4, BS)] * 4
 
 
-def call(body, outs, args, name, scratch=(), space=pltpu.VMEM, limit=LIMIT, flops=0):
+def call(body, outs, args, name, scratch=(), space=pltpu.VMEM, out_spaces=None, limit=LIMIT, flops=0):
     specs = [pl.BlockSpec(memory_space=space)] * len(args)
     moved = sum(a.size * a.dtype.itemsize for a in args)
     return pl.pallas_call(
         body,
         out_shape=outs,
         in_specs=specs,
-        out_specs=[pl.BlockSpec(memory_space=pltpu.VMEM)] * len(outs),
+        out_specs=[pl.BlockSpec(memory_space=place) for place in out_spaces or [pltpu.VMEM] * len(outs)],
         scratch_shapes=scratch,
         compiler_params=pltpu.CompilerParams(vmem_limit_bytes=limit),
         cost_estimate=pl.CostEstimate(flops=flops, bytes_accessed=moved, transcendentals=0),
@@ -547,33 +564,31 @@
     blocks = pltpu.VMEM((EB, BS), F32)
     wide = pltpu.VMEM((8 * (EB + 2), BS), F32)
     out = pltpu.VMEM((8 * EB, BS), F32)
+    small = (rhs, cond, coup, cnt, idx, nodes)
+    (pack,) = call(
+        pack_kernel,
+        [shape(PACKED, BS)],
+        small,
+        "pack",
+        scratch=[(pltpu.SMEM if part is cnt else pltpu.VMEM)(part.shape, part.dtype) for part in small]
+        + [pltpu.SemaphoreType.DMA((6,))],
+        space=pltpu.HBM,
+        limit=PACK_LIMIT,
+    )
     onehots = [(BS, 4 * IFC), (BS, E), (BS, E)]
-    *sent, coef, value, scale, right, first, own = call(
+    *sent, value, scale, first, own, ohi, oht, ohh, inside = call(
         begin_kernel,
-        [shape(12, BS)] * 4 + [shape(1, 4 * IFC)] + [FIELD] * 4 + [shape(4, BS)],
-        (rhs, cond, blk_diag, idx, cnt, coup, nodes),
+        [shape(12, BS)] * 4 + [FIELD] * 3 + [shape(4, BS)] + [shape(*dims, dtype=BF16) for dims in onehots]
+        + [shape(EB, BS, 2 * BS, dtype=BF16)],
+        (pack, blk_diag),
         "begin",
-        scratch=[pltpu.VMEM(dims, BF16) for dims in onehots]
-        + [blocks]
-        + [pltpu.VMEM(part.shape, part.dtype) for part in (rhs, cond, blk_diag, idx)]
-        + [pltpu.SMEM(cnt.shape, cnt.dtype)]
-        + [pltpu.VMEM(part.shape, part.dtype) for part in (coup, nodes)]
-        + [pltpu.SemaphoreType.DMA((7,))],
-        space=pltpu.HBM,
-        limit=BEGIN_LIMIT,
     )
     arrived = exchange(sent)
-    weights, ohi, oht, ohh = call(
-        weight_kernel,
-        [shape(EB, 3 * BS, 2 * BS, dtype=BF16)] + [shape(*dims, dtype=BF16) for dims in onehots],
-        (blk_diag, blk_off, idx, nodes),
-        "weights",
-        flops=10**7,
-    )
+    (beside,) = call(weight_kernel, [shape(EB, 2 * BS, 2 * BS, dtype=BF16)], (blk_off,), "weights", flops=10**7)
 
     def local(field):
         return call(
-            local_kernel, [FIELD], (field, value, weights), "local", scratch=[wide, out], flops=2 * 8 * EB * 3 * BS * 2 * BS
+            local_kernel, [FIELD], (field, value, inside, beside), "local", scratch=[wide, out], flops=2 * 8 * EB * 3 * BS * 2 * BS
         )[0]
 
     lat, lon = lax.axis_size("lat"), lax.axis_size("lon")
@@ -585,15 +600,15 @@
             *sent, second, ninv, ends, oha = call(
                 smooth_first_kernel,
                 MESSAGES + [FIELD, shape(4, BS), shape(1, 8 * IFC, dtype=jnp.int32), shape(BS, 8 * IFC, dtype=BF16)],
-                (*arrived, own, ohi, coef, idx, first, stiff, scale, right),
+                (*arrived, own, ohi, pack, first, stiff, scale),
                 "smooth_first",
             )
-            source = right
+            source = pack
         else:
             *sent, second = call(
                 smooth_kernel,
                 MESSAGES + [FIELD],
-                (*arrived, ohi, coef, idx, first, stiff, scale, source),
+                (*arrived, ohi, pack, first, stiff, scale, source),
                 "smooth",
             )
         arrived = exchange(sent)
@@ -601,7 +616,7 @@
         far, core, row, extra = call(
             restrict_kernel,
             MESSAGES[:2] + [shape(3, 4, BS), FIELD],
-            (*arrived, ohi, oht, ohh, coef, idx, nodes, stiff, source),
+            (*arrived, ohi, oht, ohh, pack, stiff, source),
             "restrict",
         )
         known = step > 0
@@ -619,7 +634,7 @@
         )
         chip = on_chip(column)
         away = on_chip(swap_far(chip.reshape(6, 4, BS)))
-        args = (chip, away, near, ohi, oht, ohh, coef, idx, nodes, second, extra, ends, oha, value, weights)
+        args = (chip, away, near, ohi, oht, ohh, pack, second, extra, ends, oha, value, inside, beside)
         if step == 0:
             (inverses,) = found
             *sent, direction, image, first = call(
@@ -635,7 +650,7 @@
             direction, image2, sums = call(
                 functools.partial(prolong_last_kernel, lat),
                 [FIELD, FIELD, shape(lat, 1, BS)],
-                args + (right, image),
+                args + (image,),
                 "prolong_last",
                 scratch=scratch,
             )
@@ -644,11 +659,12 @@
     sums = everywhere(jnp.broadcast_to(sums, (lax.axis_size("lon"), 1, BS)), "lon")
     solution, residual, history = call(
         finish_kernel,
-        [shape(2, 1, 1, E), shape(2, 1, 1, E), shape(1, BS)],
-        (sums, right, image, image2, directions[0], directions[1]),
+        [shape(2, 1, 1, E), shape(2, 1, 1, E), shape(ITERS)],
+        (sums, pack, image, image2, directions[0], directions[1]),
         "finish",
-    )
-    return solution, residual, history[0, :ITERS]
+        out_spaces=[pltpu.VMEM, pltpu.VMEM, pltpu.SMEM],
+    )
+    return solution, residual, history
 
 
 def solution(mesh):

time: 168 us -> 165 us (0.982)
  local copies, waits for them, and re-layouts: 5.81 us -> 3.44 us
    unnamed x26 -> x8, local copies, waits for them, and re-layouts: 5.28 us -> 3.42 us
    pallas_call x17 -> x18, Pallas kernels: 11.6 us -> 10.8 us  [call(): pl.pallas_call(body, out_shape=outs, in_specs=specs, out_specs=[pl.BlockS...]
where the time goes in v5:
time: 165 us; the launch traced here: 164 us
  blocking collectives  73.3 us (44%)
  starting transfers between devices  70.6 us (43%)
  Pallas kernels  10.8 us (7%)
  waiting for transfers between devices  4.43 us (3%)
  local copies, waits for them, and re-layouts  3.44 us (2%)
    all_to_all x4, blocking collectives, everywhere(): return lax.all_to_all(row, axis, 0, 0)  57.1 us
    ppermute x8, starting transfers between devices, swap_far(): return lax.ppermute(message, 'lat', swap(lat_pairs(1)))  34.5 us
    ppermute x4, starting transfers between devices, exchange(): lax.ppermute(messages[0], 'lon', swap([(k, (k + 1) % lon) for k in range(...  20.4 us
    all_gather x6, blocking collectives, on_chip(): return lax.all_gather(message, 'lat', axis_index_groups=lat_pairs(0))  16.2 us
    pallas_call x18, Pallas kernels, call(): pl.pallas_call(body, out_shape=outs, in_specs=specs, out_specs=[pl.BlockS...  10.8 us
    ppermute x4, starting transfers between devices, exchange(): lax.ppermute(messages[1], 'lon', swap([(k, k + 1) for k in range(0, lon,...  8.08 us
    ppermute x4, starting transfers between devices, exchange(): lax.ppermute(messages[3], 'lat', swap(lat_pairs(0)))  7.68 us
    unnamed x8, local copies, waits for them, and re-layouts  3.42 us
  transfers between devices with their start and end apart: 20, of which 5 were waited for; matrix products, arithmetic and copies ran while one was open for 0% of the time, Pallas kernels for 2%

profile of v5, /device:TPU:1, one launch (start us, length us, event | category | flops | bytes accessed | tf_op | source)
XLA Modules:
  0.0 163.7 jit_solution(10653936446043698897)
XLA Ops:
  5.2 8.1 %collective-permute-start = (f32[12,128]{1,0:T(8,128)S(1)}, f32[12,128]{1,0:T(8,128)S(1)}, u32[]{:S(2)}, u32[]{:S(2)}) collective-permute-start(f32[12,128]{1,0:T(8,128)S(1)} %get-tuple-element.51), channel_id=1, source_target_pairs={{1,2},{3,4},{5,6},{7,8},{9,10},{11,12},{13,14},{15,16},{17,18},{19... | collective-permute-start | bytes 18440 | tf_op jit(solution)/shard_map/ppermute | solution.py:552
  13.4 1.9 %collective-permute-start.1 = (f32[12,128]{1,0:T(8,128)S(1)}, f32[12,128]{1,0:T(8,128)S(1)}, u32[]{:S(2)}, u32[]{:S(2)}) collective-permute-start(f32[12,128]{1,0:T(8,128)S(1)} %get-tuple-element.52), channel_id=1, source_target_pairs={{0,1},{2,3},{4,5},{6,7},{8,9},{10,11},{12,13},{14,15},{16,17},{18,... | collective-permute-start | bytes 18440 | tf_op jit(solution)/shard_map/ppermute | solution.py:553
  15.3 4.8 %collective-permute-start.2 = (f32[12,128]{1,0:T(8,128)S(1)}, f32[12,128]{1,0:T(8,128)S(1)}, u32[]{:S(2)}, u32[]{:S(2)}) collective-permute-start(f32[12,128]{1,0:T(8,128)S(1)} %get-tuple-element.53), channel_id=1, source_target_pairs={{32,64},{96,128},{160,192},{224,256},{288,320},{352,384},{416,448}... | collective-permute-start | bytes 18440 | tf_op jit(solution)/shard_map/ppermute | solution.py:542
  20.2 1.9 %collective-permute-start.3 = (f32[12,128]{1,0:T(8,128)S(1)}, f32[12,128]{1,0:T(8,128)S(1)}, u32[]{:S(2)}, u32[]{:S(2)}) collective-permute-start(f32[12,128]{1,0:T(8,128)S(1)} %get-tuple-element.54), channel_id=1, source_target_pairs={{0,32},{64,96},{128,160},{192,224},{256,288},{320,352},{384,416},{... | collective-permute-start | bytes 18440 | tf_op jit(solution)/shard_map/ppermute | solution.py:555
  25.1 4.3 %collective-permute-start.4 = (f32[4,128]{1,0:T(4,128)S(1)}, f32[4,128]{1,0:T(4,128)S(1)}, u32[]{:S(2)}, u32[]{:S(2)}) collective-permute-start(f32[4,128]{1,0:T(4,128)S(1)} %get-tuple-element.61), channel_id=1, source_target_pairs={{1,2},{3,4},{5,6},{7,8},{9,10},{11,12},{13,14},{15,16},{17,18},{19... | collective-permute-start | bytes 6152 | tf_op jit(solution)/shard_map/ppermute | solution.py:552
  29.4 1.9 %collective-permute-start.5 = (f32[4,128]{1,0:T(4,128)S(1)}, f32[4,128]{1,0:T(4,128)S(1)}, u32[]{:S(2)}, u32[]{:S(2)}) collective-permute-start(f32[4,128]{1,0:T(4,128)S(1)} %get-tuple-element.62), channel_id=1, source_target_pairs={{0,1},{2,3},{4,5},{6,7},{8,9},{10,11},{12,13},{14,15},{16,17},{18,... | collective-permute-start | bytes 6152 | tf_op jit(solution)/shard_map/ppermute | solution.py:553
  31.4 4.7 %collective-permute-start.6 = (f32[4,128]{1,0:T(4,128)S(1)}, f32[4,128]{1,0:T(4,128)S(1)}, u32[]{:S(2)}, u32[]{:S(2)}) collective-permute-start(f32[4,128]{1,0:T(4,128)S(1)} %get-tuple-element.63), channel_id=1, source_target_pairs={{32,64},{96,128},{160,192},{224,256},{288,320},{352,384},{416,448}... | collective-permute-start | bytes 6152 | tf_op jit(solution)/shard_map/ppermute | solution.py:542
  36.0 1.9 %collective-permute-start.7 = (f32[4,128]{1,0:T(4,128)S(1)}, f32[4,128]{1,0:T(4,128)S(1)}, u32[]{:S(2)}, u32[]{:S(2)}) collective-permute-start(f32[4,128]{1,0:T(4,128)S(1)} %get-tuple-element.64), channel_id=1, source_target_pairs={{0,32},{64,96},{128,160},{192,224},{256,288},{320,352},{384,416},{... | collective-permute-start | bytes 6152 | tf_op jit(solution)/shard_map/ppermute | solution.py:555
  39.7 4.1 %collective-permute-start.8 = (f32[4,128]{1,0:T(4,128)S(1)}, f32[4,128]{1,0:T(4,128)S(1)}, u32[]{:S(2)}, u32[]{:S(2)}) collective-permute-start(f32[4,128]{1,0:T(4,128)S(1)} %get-tuple-element.68), channel_id=1, source_target_pairs={{32,64},{96,128},{160,192},{224,256},{288,320},{352,384},{416,448}... | collective-permute-start | bytes 6152 | tf_op jit(solution)/shard_map/ppermute | solution.py:542
  45.6 15.4 %all_to_all.20.row_ref = f32[32,4,4,128]{3,2,1,0:T(4,128)S(1)} all-to-all(f32[32,4,4,128]{3,2,1,0:T(4,128)S(1)} %row.2), channel_id=1, replica_groups=mesh['lat'=16,'lon'=32] {'lon'}, dimensions={0} | all-to-all | bytes 524288 | tf_op jit(solution)/shard_map/all_to_all | solution.py:560
  61.1 4.5 %all-gather.1 = f32[6,4,128]{2,1,0:T(4,128)S(1)} all-gather(f32[3,4,128]{2,1,0:T(4,128)S(1)} %get-tuple-element.72), channel_id=3, replica_groups={{0,32},{64,96},{128,160},{192,224},{256,288},{320,352},{384,416},{448,4..., dimensions={0}, use_global_device_ids=true | all-gather | bytes 18432 | tf_op jit(solution)/shard_map/all_gather | solution.py:546
  65.5 5.4 %collective-permute-start.9 = (f32[6,4,128]{2,1,0:T(4,128)S(1)}, f32[6,4,128]{2,1,0:T(4,128)S(1)}, u32[]{:S(2)}, u32[]{:S(2)}) collective-permute-start(f32[6,4,128]{2,1,0:T(4,128)S(1)} %all-gather.1), channel_id=1, source_target_pairs={{32,64},{96,128},{160,192},{224,256},{288,320},{352,384},{416,448}... | collective-permute-start | bytes 36872 | tf_op jit(solution)/shard_map/ppermute | solution.py:542
  75.4 3.7 %collective-permute-start.10 = (f32[4,128]{1,0:T(4,128)S(1)}, f32[4,128]{1,0:T(4,128)S(1)}, u32[]{:S(2)}, u32[]{:S(2)}) collective-permute-start(f32[4,128]{1,0:T(4,128)S(1)} %get-tuple-element.77), channel_id=1, source_target_pairs={{1,2},{3,4},{5,6},{7,8},{9,10},{11,12},{13,14},{15,16},{17,18},{19... | collective-permute-start | bytes 6152 | tf_op jit(solution)/shard_map/ppermute | solution.py:552
  79.1 2.3 %collective-permute-start.11 = (f32[4,128]{1,0:T(4,128)S(1)}, f32[4,128]{1,0:T(4,128)S(1)}, u32[]{:S(2)}, u32[]{:S(2)}) collective-permute-start(f32[4,128]{1,0:T(4,128)S(1)} %get-tuple-element.78), channel_id=1, source_target_pairs={{0,1},{2,3},{4,5},{6,7},{8,9},{10,11},{12,13},{14,15},{16,17},{18,... | collective-permute-start | bytes 6152 | tf_op jit(solution)/shard_map/ppermute | solution.py:553
  81.4 4.2 %collective-permute-start.12 = (f32[4,128]{1,0:T(4,128)S(1)}, f32[4,128]{1,0:T(4,128)S(1)}, u32[]{:S(2)}, u32[]{:S(2)}) collective-permute-start(f32[4,128]{1,0:T(4,128)S(1)} %get-tuple-element.79), channel_id=1, source_target_pairs={{32,64},{96,128},{160,192},{224,256},{288,320},{352,384},{416,448}... | collective-permute-start | bytes 6152 | tf_op jit(solution)/shard_map/ppermute | solution.py:542
  85.6 1.9 %collective-permute-start.13 = (f32[4,128]{1,0:T(4,128)S(1)}, f32[4,128]{1,0:T(4,128)S(1)}, u32[]{:S(2)}, u32[]{:S(2)}) collective-permute-start(f32[4,128]{1,0:T(4,128)S(1)} %get-tuple-element.80), channel_id=1, source_target_pairs={{0,32},{64,96},{128,160},{192,224},{256,288},{320,352},{384,416},{... | collective-permute-start | bytes 6152 | tf_op jit(solution)/shard_map/ppermute | solution.py:555
  89.2 4.3 %collective-permute-start.14 = (f32[4,128]{1,0:T(4,128)S(1)}, f32[4,128]{1,0:T(4,128)S(1)}, u32[]{:S(2)}, u32[]{:S(2)}) collective-permute-start(f32[4,128]{1,0:T(4,128)S(1)} %get-tuple-element.83), channel_id=1, source_target_pairs={{1,2},{3,4},{5,6},{7,8},{9,10},{11,12},{13,14},{15,16},{17,18},{19... | collective-permute-start | bytes 6152 | tf_op jit(solution)/shard_map/ppermute | solution.py:552
  95.4 3.4 %collective-permute-start.16 = (f32[4,128]{1,0:T(4,128)S(1)}, f32[4,128]{1,0:T(4,128)S(1)}, u32[]{:S(2)}, u32[]{:S(2)}) collective-permute-start(f32[4,128]{1,0:T(4,128)S(1)} %get-tuple-element.85), channel_id=1, source_target_pairs={{32,64},{96,128},{160,192},{224,256},{288,320},{352,384},{416,448}... | collective-permute-start | bytes 6152 | tf_op jit(solution)/shard_map/ppermute | solution.py:542
  102.5 4.2 %collective-permute-start.18 = (f32[4,128]{1,0:T(4,128)S(1)}, f32[4,128]{1,0:T(4,128)S(1)}, u32[]{:S(2)}, u32[]{:S(2)}) collective-permute-start(f32[4,128]{1,0:T(4,128)S(1)} %get-tuple-element.88), channel_id=1, source_target_pairs={{32,64},{96,128},{160,192},{224,256},{288,320},{352,384},{416,448}... | collective-permute-start | bytes 6152 | tf_op jit(solution)/shard_map/ppermute | solution.py:542
  108.5 15.2 %all_to_all.21.row_ref = f32[32,3,4,128]{3,2,1,0:T(4,128)S(1)} all-to-all(f32[32,3,4,128]{3,2,1,0:T(4,128)S(1)} %row.3), channel_id=1, replica_groups=mesh['lat'=16,'lon'=32] {'lon'}, dimensions={0} | all-to-all | bytes 393216 | tf_op jit(solution)/shard_map/all_to_all | solution.py:560
  123.8 4.5 %all-gather.4 = f32[6,4,128]{2,1,0:T(4,128)S(1)} all-gather(f32[3,4,128]{2,1,0:T(4,128)S(1)} %get-tuple-element.92), channel_id=6, replica_groups={{0,32},{64,96},{128,160},{192,224},{256,288},{320,352},{384,416},{448,4..., dimensions={0}, use_global_device_ids=true | all-gather | bytes 18432 | tf_op jit(solution)/shard_map/all_gather | solution.py:546
  128.3 3.7 %collective-permute-start.19 = (f32[6,4,128]{2,1,0:T(4,128)S(1)}, f32[6,4,128]{2,1,0:T(4,128)S(1)}, u32[]{:S(2)}, u32[]{:S(2)}) collective-permute-start(f32[6,4,128]{2,1,0:T(4,128)S(1)} %all-gather.4), channel_id=1, source_target_pairs={{32,64},{96,128},{160,192},{224,256},{288,320},{352,384},{416,448}... | collective-permute-start | bytes 36872 | tf_op jit(solution)/shard_map/ppermute | solution.py:542
  136.4 14.2 %all_to_all.22 = f32[16,1,128]{2,1,0:T(1,128)S(1)} all-to-all(f32[16,1,128]{2,1,0:T(1,128)S(1)} %get-tuple-element.95), channel_id=1, replica_groups=mesh['lat'=16,'lon'=32] {'lat'}, dimensions={0} | all-to-all | bytes 16384 | tf_op jit(solution)/shard_map/all_to_all | solution.py:560
  150.6 12.3 %all_to_all.23.sums_ref = f32[32,1,128]{2,1,0:T(1,128)S(1)} all-to-all(f32[32,1,128]{2,1,0:T(1,128)S(1)} %broadcast_in_dim.2), channel_id=1, replica_groups=mesh['lat'=16,'lon'=32] {'lon'}, dimensions={0} | all-to-all | bytes 32768 | tf_op jit(solution)/shard_map/all_to_all | solution.py:560
  (54 shorter events, 29.8 us)
Async XLA Ops:
  2.1 0.8 copy-start
  2.9 1.2 copy-start.2
  5.2 18.9 %collective-permute-start = (f32[12,128]{1,0:T(8,128)S(1)}, f32[12,128]{1,0:T(8,128)S(1)}, u32[]{:S(2)}, u32[]{:S(2)}) collective-permute-start(f32[12,128]{1,0:T(8,128)S(1)} %get-tuple-element.51), channel_id=1, source_target_pairs={{1,2},{3,4},{5,6},{7,8},{9,10},{11,12},{13,14},{15,16},{17,18},{19... | collective-permute-start | bytes 18440 | tf_op jit(solution)/shard_map/ppermute | solution.py:552
  13.4 10.8 %collective-permute-start.1 = (f32[12,128]{1,0:T(8,128)S(1)}, f32[12,128]{1,0:T(8,128)S(1)}, u32[]{:S(2)}, u32[]{:S(2)}) collective-permute-start(f32[12,128]{1,0:T(8,128)S(1)} %get-tuple-element.52), channel_id=1, source_target_pairs={{0,1},{2,3},{4,5},{6,7},{8,9},{10,11},{12,13},{14,15},{16,17},{18,... | collective-permute-start | bytes 18440 | tf_op jit(solution)/shard_map/ppermute | solution.py:553
  15.3 8.9 %collective-permute-start.2 = (f32[12,128]{1,0:T(8,128)S(1)}, f32[12,128]{1,0:T(8,128)S(1)}, u32[]{:S(2)}, u32[]{:S(2)}) collective-permute-start(f32[12,128]{1,0:T(8,128)S(1)} %get-tuple-element.53), channel_id=1, source_target_pairs={{32,64},{96,128},{160,192},{224,256},{288,320},{352,384},{416,448}... | collective-permute-start | bytes 18440 | tf_op jit(solution)/shard_map/ppermute | solution.py:542
  20.2 4.1 %collective-permute-start.3 = (f32[12,128]{1,0:T(8,128)S(1)}, f32[12,128]{1,0:T(8,128)S(1)}, u32[]{:S(2)}, u32[]{:S(2)}) collective-permute-start(f32[12,128]{1,0:T(8,128)S(1)} %get-tuple-element.54), channel_id=1, source_target_pairs={{0,32},{64,96},{128,160},{192,224},{256,288},{320,352},{384,416},{... | collective-permute-start | bytes 18440 | tf_op jit(solution)/shard_map/ppermute | solution.py:555
  22.1 1.2 copy-start.3
  23.6 0.8 copy-start.1
  25.1 13.4 %collective-permute-start.4 = (f32[4,128]{1,0:T(4,128)S(1)}, f32[4,128]{1,0:T(4,128)S(1)}, u32[]{:S(2)}, u32[]{:S(2)}) collective-permute-start(f32[4,128]{1,0:T(4,128)S(1)} %get-tuple-element.61), channel_id=1, source_target_pairs={{1,2},{3,4},{5,6},{7,8},{9,10},{11,12},{13,14},{15,16},{17,18},{19... | collective-permute-start | bytes 6152 | tf_op jit(solution)/shard_map/ppermute | solution.py:552
  29.4 9.1 %collective-permute-start.5 = (f32[4,128]{1,0:T(4,128)S(1)}, f32[4,128]{1,0:T(4,128)S(1)}, u32[]{:S(2)}, u32[]{:S(2)}) collective-permute-start(f32[4,128]{1,0:T(4,128)S(1)} %get-tuple-element.62), channel_id=1, source_target_pairs={{0,1},{2,3},{4,5},{6,7},{8,9},{10,11},{12,13},{14,15},{16,17},{18,... | collective-permute-start | bytes 6152 | tf_op jit(solution)/shard_map/ppermute | solution.py:553
  31.4 7.2 %collective-permute-start.6 = (f32[4,128]{1,0:T(4,128)S(1)}, f32[4,128]{1,0:T(4,128)S(1)}, u32[]{:S(2)}, u32[]{:S(2)}) collective-permute-start(f32[4,128]{1,0:T(4,128)S(1)} %get-tuple-element.63), channel_id=1, source_target_pairs={{32,64},{96,128},{160,192},{224,256},{288,320},{352,384},{416,448}... | collective-permute-start | bytes 6152 | tf_op jit(solution)/shard_map/ppermute | solution.py:542
  36.0 3.1 %collective-permute-start.7 = (f32[4,128]{1,0:T(4,128)S(1)}, f32[4,128]{1,0:T(4,128)S(1)}, u32[]{:S(2)}, u32[]{:S(2)}) collective-permute-start(f32[4,128]{1,0:T(4,128)S(1)} %get-tuple-element.64), channel_id=1, source_target_pairs={{0,32},{64,96},{128,160},{192,224},{256,288},{320,352},{384,416},{... | collective-permute-start | bytes 6152 | tf_op jit(solution)/shard_map/ppermute | solution.py:555
  39.7 5.9 %collective-permute-start.8 = (f32[4,128]{1,0:T(4,128)S(1)}, f32[4,128]{1,0:T(4,128)S(1)}, u32[]{:S(2)}, u32[]{:S(2)}) collective-permute-start(f32[4,128]{1,0:T(4,128)S(1)} %get-tuple-element.68), channel_id=1, source_target_pairs={{32,64},{96,128},{160,192},{224,256},{288,320},{352,384},{416,448}... | collective-permute-start | bytes 6152 | tf_op jit(solution)/shard_map/ppermute | solution.py:542
  65.5 6.8 %collective-permute-start.9 = (f32[6,4,128]{2,1,0:T(4,128)S(1)}, f32[6,4,128]{2,1,0:T(4,128)S(1)}, u32[]{:S(2)}, u32[]{:S(2)}) collective-permute-start(f32[6,4,128]{2,1,0:T(4,128)S(1)} %all-gather.1), channel_id=1, source_target_pairs={{32,64},{96,128},{160,192},{224,256},{288,320},{352,384},{416,448}... | collective-permute-start | bytes 36872 | tf_op jit(solution)/shard_map/ppermute | solution.py:542
  75.4 12.7 %collective-permute-start.10 = (f32[4,128]{1,0:T(4,128)S(1)}, f32[4,128]{1,0:T(4,128)S(1)}, u32[]{:S(2)}, u32[]{:S(2)}) collective-permute-start(f32[4,128]{1,0:T(4,128)S(1)} %get-tuple-element.77), channel_id=1, source_target_pairs={{1,2},{3,4},{5,6},{7,8},{9,10},{11,12},{13,14},{15,16},{17,18},{19... | collective-permute-start | bytes 6152 | tf_op jit(solution)/shard_map/ppermute | solution.py:552
  79.1 9.0 %collective-permute-start.11 = (f32[4,128]{1,0:T(4,128)S(1)}, f32[4,128]{1,0:T(4,128)S(1)}, u32[]{:S(2)}, u32[]{:S(2)}) collective-permute-start(f32[4,128]{1,0:T(4,128)S(1)} %get-tuple-element.78), channel_id=1, source_target_pairs={{0,1},{2,3},{4,5},{6,7},{8,9},{10,11},{12,13},{14,15},{16,17},{18,... | collective-permute-start | bytes 6152 | tf_op jit(solution)/shard_map/ppermute | solution.py:553
  81.4 6.7 %collective-permute-start.12 = (f32[4,128]{1,0:T(4,128)S(1)}, f32[4,128]{1,0:T(4,128)S(1)}, u32[]{:S(2)}, u32[]{:S(2)}) collective-permute-start(f32[4,128]{1,0:T(4,128)S(1)} %get-tuple-element.79), channel_id=1, source_target_pairs={{32,64},{96,128},{160,192},{224,256},{288,320},{352,384},{416,448}... | collective-permute-start | bytes 6152 | tf_op jit(solution)/shard_map/ppermute | solution.py:542
  85.6 3.1 %collective-permute-start.13 = (f32[4,128]{1,0:T(4,128)S(1)}, f32[4,128]{1,0:T(4,128)S(1)}, u32[]{:S(2)}, u32[]{:S(2)}) collective-permute-start(f32[4,128]{1,0:T(4,128)S(1)} %get-tuple-element.80), channel_id=1, source_target_pairs={{0,32},{64,96},{128,160},{192,224},{256,288},{320,352},{384,416},{... | collective-permute-start | bytes 6152 | tf_op jit(solution)/shard_map/ppermute | solution.py:555
  89.2 12.1 %collective-permute-start.14 = (f32[4,128]{1,0:T(4,128)S(1)}, f32[4,128]{1,0:T(4,128)S(1)}, u32[]{:S(2)}, u32[]{:S(2)}) collective-permute-start(f32[4,128]{1,0:T(4,128)S(1)} %get-tuple-element.83), channel_id=1, source_target_pairs={{1,2},{3,4},{5,6},{7,8},{9,10},{11,12},{13,14},{15,16},{17,18},{19... | collective-permute-start | bytes 6152 | tf_op jit(solution)/shard_map/ppermute | solution.py:552
  93.4 7.9 %collective-permute-start.15 = (f32[4,128]{1,0:T(4,128)S(1)}, f32[4,128]{1,0:T(4,128)S(1)}, u32[]{:S(2)}, u32[]{:S(2)}) collective-permute-start(f32[4,128]{1,0:T(4,128)S(1)} %get-tuple-element.84), channel_id=1, source_target_pairs={{0,1},{2,3},{4,5},{6,7},{8,9},{10,11},{12,13},{14,15},{16,17},{18,... | collective-permute-start | bytes 6152 | tf_op jit(solution)/shard_map/ppermute | solution.py:553
  95.4 5.9 %collective-permute-start.16 = (f32[4,128]{1,0:T(4,128)S(1)}, f32[4,128]{1,0:T(4,128)S(1)}, u32[]{:S(2)}, u32[]{:S(2)}) collective-permute-start(f32[4,128]{1,0:T(4,128)S(1)} %get-tuple-element.85), channel_id=1, source_target_pairs={{32,64},{96,128},{160,192},{224,256},{288,320},{352,384},{416,448}... | collective-permute-start | bytes 6152 | tf_op jit(solution)/shard_map/ppermute | solution.py:542
  98.8 3.1 %collective-permute-start.17 = (f32[4,128]{1,0:T(4,128)S(1)}, f32[4,128]{1,0:T(4,128)S(1)}, u32[]{:S(2)}, u32[]{:S(2)}) collective-permute-start(f32[4,128]{1,0:T(4,128)S(1)} %get-tuple-element.86), channel_id=1, source_target_pairs={{0,32},{64,96},{128,160},{192,224},{256,288},{320,352},{384,416},{... | collective-permute-start | bytes 6152 | tf_op jit(solution)/shard_map/ppermute | solution.py:555
  102.5 6.0 %collective-permute-start.18 = (f32[4,128]{1,0:T(4,128)S(1)}, f32[4,128]{1,0:T(4,128)S(1)}, u32[]{:S(2)}, u32[]{:S(2)}) collective-permute-start(f32[4,128]{1,0:T(4,128)S(1)} %get-tuple-element.88), channel_id=1, source_target_pairs={{32,64},{96,128},{160,192},{224,256},{288,320},{352,384},{416,448}... | collective-permute-start | bytes 6152 | tf_op jit(solution)/shard_map/ppermute | solution.py:542
  128.3 5.1 %collective-permute-start.19 = (f32[6,4,128]{2,1,0:T(4,128)S(1)}, f32[6,4,128]{2,1,0:T(4,128)S(1)}, u32[]{:S(2)}, u32[]{:S(2)}) collective-permute-start(f32[6,4,128]{2,1,0:T(4,128)S(1)} %all-gather.4), channel_id=1, source_target_pairs={{32,64},{96,128},{160,192},{224,256},{288,320},{352,384},{416,448}... | collective-permute-start | bytes 36872 | tf_op jit(solution)/shard_map/ppermute | solution.py:542

commit v6 on v5

--- a/solution.py
+++ b/solution.py
@@ -305,6 +305,8 @@
     inverse = complex_inverse((sums[0:2], sums[2:4]))
     ninv_ref[0:2] = inverse[0]
     ninv_ref[2:4] = inverse[1]
+    for ref in (m0, m1):
+        ref[4:8] = ninv_ref[...]
     for d, part in enumerate(collect((a0, a1, a2, a3), 8)):
         for k in range(2):
             row = jnp.concatenate([part[2 * k : 2 * k + 1], part[2 * k + 1 : 2 * k + 2]], axis=1)
@@ -322,47 +324,50 @@
     smooth(arrived, ohi_ref, pack_ref, first_ref, local_ref, scale_ref, right_ref, (m0, m1, m2, m3), second_ref)
 
 
-def restrict_kernel(
-    a0, a1, a2, a3, ohi_ref, oht_ref, ohh_ref, pack_ref, local_ref, right_ref,
-    far_ref, core_ref, row_ref, extra_ref,
-):
+def times_inverse(inverse, value):
+    result = complex_times((inverse[0:2], inverse[2:4]), (value[0:2], value[2:4]))
+    return jnp.concatenate(result, axis=0)
+
+
+def restrict_kernel(known, a0, a1, a2, a3, ohi_ref, oht_ref, ohh_ref, pack_ref, local_ref, right_ref, beside_ref, *refs):
+    far_ref, core_ref, row_ref, extra_ref = refs[:4]
+    even_lat, even_lon = parities()
+    if known:
+        west, east = beside_ref[0], beside_ref[1]
+    else:
+        wide, near = a0[4:8], a1[4:8]
+        west, east = jnp.where(even_lon, wide, near), jnp.where(even_lon, near, wide)
+        refs[4][0] = west
+        refs[4][1] = east
     index = index_rows(pack_ref)
     extra = interface_sum(collect((a0, a1, a2, a3)), coef_row(pack_ref), ohi_ref, index)
     keep(extra_ref, extra)
     local, right = pair(local_ref), pair(right_ref)
     rows = [lanes(right[c] - local[c] - extra[c], EB) for c in range(2)]
     own, towards = nodal(rows, ohh_ref, oht_ref, pack_ref, -1.0)
-    even_lat, _ = parities()
     far_ref[...] = jnp.where(even_lat, towards[0], towards[1])
     core_ref[...] = jnp.where(even_lat, towards[1], towards[0])
-    for k, part in enumerate((own, towards[2], towards[3])):
-        row_ref[k] = part
-
-
-def row_kernel(far_ref, core_ref, row_ref, *refs):
-    out_ref = refs[-1]
+    row_ref[0] = own
+    row_ref[1] = times_inverse(west, towards[2])
+    row_ref[2] = times_inverse(east, towards[3])
+
+
+def row_kernel(far_ref, core_ref, row_ref, ninv_ref, out_ref):
     even_lat, _ = parities()
     core = jnp.where(even_lat, core_ref[1], core_ref[0])
-    parts = [row_ref[0] + far_ref[...] + core, row_ref[1], row_ref[2]]
-    parts += [ref[...] for ref in refs[:-1]]
-    for k, part in enumerate(parts):
+    mine = times_inverse(ninv_ref[...], row_ref[0] + far_ref[...] + core)
+    for k, part in enumerate((mine, row_ref[1], row_ref[2])):
         out_ref[:, k] = jnp.broadcast_to(part[None], (out_ref.shape[0], 4, BS))
 
 
-def column_kernel(known, lon, row_ref, *refs):
-    inverse_ref, near_ref, out_ref = refs if known else (refs[2], refs[0], refs[1])
+def column_kernel(lon, row_ref, near_ref, out_ref):
     me = lax.axis_index("lon")
 
     def at(step):
         return lax.rem(me + (lon + step), lon)
 
     for k in range(5):
-        sums = row_ref[at(k - 2), 0] + row_ref[at(k - 1), 1] + row_ref[at(k - 3), 2]
-        if not known:
-            inverse_ref[k] = row_ref[at(k - 2), 3]
-        inverse = inverse_ref[k]
-        result = complex_times((inverse[0:2], inverse[2:4]), (sums[0:2], sums[2:4]))
-        near_ref[k] = jnp.concatenate(result, axis=0)
+        near_ref[k] = row_ref[at(k - 2), 0] + row_ref[at(k - 1), 1] + row_ref[at(k - 3), 2]
     for k in range(3):
         out_ref[k] = near_ref[k + 1]
 
@@ -599,7 +604,7 @@
         if step == 0:
             *sent, second, ninv, ends, oha = call(
                 smooth_first_kernel,
-                MESSAGES + [FIELD, shape(4, BS), shape(1, 8 * IFC, dtype=jnp.int32), shape(BS, 8 * IFC, dtype=BF16)],
+                [shape(8, BS)] * 2 + MESSAGES[2:] + [FIELD, shape(4, BS), shape(1, 8 * IFC, dtype=jnp.int32), shape(BS, 8 * IFC, dtype=BF16)],
                 (*arrived, own, ohi, pack, first, stiff, scale),
                 "smooth_first",
             )
@@ -613,30 +618,28 @@
             )
         arrived = exchange(sent)
         stiff = local(second)
-        far, core, row, extra = call(
-            restrict_kernel,
-            MESSAGES[:2] + [shape(3, 4, BS), FIELD],
-            (*arrived, ohi, oht, ohh, pack, stiff, source),
+        known = step > 0
+        far, core, row, extra, *found = call(
+            functools.partial(restrict_kernel, known),
+            MESSAGES[:2] + [shape(3, 4, BS), FIELD] + ([] if known else [shape(2, 4, BS)]),
+            (*arrived, ohi, oht, ohh, pack, stiff, source, sides if known else ninv),
             "restrict",
         )
-        known = step > 0
+        if not known:
+            (sides,) = found
         (row,) = call(
-            row_kernel,
-            [shape(lon, 3 if known else 4, 4, BS)],
-            (swap_far(far), on_chip(core), row) + (() if known else (ninv,)),
-            "row",
+            row_kernel, [shape(lon, 3, 4, BS)], (swap_far(far), on_chip(core), row, ninv), "row"
         )
-        near, column, *found = call(
-            functools.partial(column_kernel, known, lon),
-            [shape(5, 4, BS), shape(3, 4, BS)] + ([] if known else [shape(5, 4, BS)]),
-            (everywhere(row, "lon"),) + ((inverses,) if known else ()),
+        near, column = call(
+            functools.partial(column_kernel, lon),
+            [shape(5, 4, BS), shape(3, 4, BS)],
+            (everywhere(row, "lon"),),
             "column",
         )
         chip = on_chip(column)
         away = on_chip(swap_far(chip.reshape(6, 4, BS)))
         args = (chip, away, near, ohi, oht, ohh, pack, second, extra, ends, oha, value, inside, beside)
         if step == 0:
-            (inverses,) = found
             *sent, direction, image, first = call(
                 functools.partial(prolong_first_kernel, lat),
                 MESSAGES + [FIELD] * 3,

time: 165 us -> 164 us (level)
  no operation moved by 1% of the time
where the time goes in v6:
time: 164 us; the launch traced here: 163 us
  blocking collectives  72.6 us (44%)
  starting transfers between devices  70.3 us (43%)
  Pallas kernels  10.9 us (7%)
  waiting for transfers between devices  4.45 us (3%)
  local copies, waits for them, and re-layouts  3.44 us (2%)
    all_to_all x4, blocking collectives, everywhere(): return lax.all_to_all(row, axis, 0, 0)  56.4 us
    ppermute x8, starting transfers between devices, swap_far(): return lax.ppermute(message, 'lat', swap(lat_pairs(1)))  34.1 us
    ppermute x4, starting transfers between devices, exchange(): lax.ppermute(messages[0], 'lon', swap([(k, (k + 1) % lon) for k in range(...  20.4 us
    all_gather x6, blocking collectives, on_chip(): return lax.all_gather(message, 'lat', axis_index_groups=lat_pairs(0))  16.2 us
    pallas_call x18, Pallas kernels, call(): pl.pallas_call(body, out_shape=outs, in_specs=specs, out_specs=[pl.BlockS...  10.9 us
    ppermute x4, starting transfers between devices, exchange(): lax.ppermute(messages[1], 'lon', swap([(k, k + 1) for k in range(0, lon,...  8.08 us
    ppermute x4, starting transfers between devices, exchange(): lax.ppermute(messages[3], 'lat', swap(lat_pairs(0)))  7.68 us
    unnamed x8, local copies, waits for them, and re-layouts  3.42 us
  transfers between devices with their start and end apart: 20, of which 5 were waited for; matrix products, arithmetic and copies ran while one was open for 0% of the time, Pallas kernels for 2%

profile of v6, /device:TPU:1, one launch (start us, length us, event | category | flops | bytes accessed | tf_op | source)
XLA Modules:
  0.0 162.7 jit_solution(11567410505828315581)
XLA Ops:
  5.2 8.1 %collective-permute-start = (f32[12,128]{1,0:T(8,128)S(1)}, f32[12,128]{1,0:T(8,128)S(1)}, u32[]{:S(2)}, u32[]{:S(2)}) collective-permute-start(f32[12,128]{1,0:T(8,128)S(1)} %get-tuple-element.51), channel_id=1, source_target_pairs={{1,2},{3,4},{5,6},{7,8},{9,10},{11,12},{13,14},{15,16},{17,18},{19... | collective-permute-start | bytes 18440 | tf_op jit(solution)/shard_map/ppermute | solution.py:557
  13.4 1.9 %collective-permute-start.1 = (f32[12,128]{1,0:T(8,128)S(1)}, f32[12,128]{1,0:T(8,128)S(1)}, u32[]{:S(2)}, u32[]{:S(2)}) collective-permute-start(f32[12,128]{1,0:T(8,128)S(1)} %get-tuple-element.52), channel_id=1, source_target_pairs={{0,1},{2,3},{4,5},{6,7},{8,9},{10,11},{12,13},{14,15},{16,17},{18,... | collective-permute-start | bytes 18440 | tf_op jit(solution)/shard_map/ppermute | solution.py:558
  15.3 4.8 %collective-permute-start.2 = (f32[12,128]{1,0:T(8,128)S(1)}, f32[12,128]{1,0:T(8,128)S(1)}, u32[]{:S(2)}, u32[]{:S(2)}) collective-permute-start(f32[12,128]{1,0:T(8,128)S(1)} %get-tuple-element.53), channel_id=1, source_target_pairs={{32,64},{96,128},{160,192},{224,256},{288,320},{352,384},{416,448}... | collective-permute-start | bytes 18440 | tf_op jit(solution)/shard_map/ppermute | solution.py:547
  20.2 1.9 %collective-permute-start.3 = (f32[12,128]{1,0:T(8,128)S(1)}, f32[12,128]{1,0:T(8,128)S(1)}, u32[]{:S(2)}, u32[]{:S(2)}) collective-permute-start(f32[12,128]{1,0:T(8,128)S(1)} %get-tuple-element.54), channel_id=1, source_target_pairs={{0,32},{64,96},{128,160},{192,224},{256,288},{320,352},{384,416},{... | collective-permute-start | bytes 18440 | tf_op jit(solution)/shard_map/ppermute | solution.py:560
  25.1 4.3 %collective-permute-start.4 = (f32[8,128]{1,0:T(8,128)S(1)}, f32[8,128]{1,0:T(8,128)S(1)}, u32[]{:S(2)}, u32[]{:S(2)}) collective-permute-start(f32[8,128]{1,0:T(8,128)S(1)} %get-tuple-element.61), channel_id=1, source_target_pairs={{1,2},{3,4},{5,6},{7,8},{9,10},{11,12},{13,14},{15,16},{17,18},{19... | collective-permute-start | bytes 12296 | tf_op jit(solution)/shard_map/ppermute | solution.py:557
  29.4 1.9 %collective-permute-start.5 = (f32[8,128]{1,0:T(8,128)S(1)}, f32[8,128]{1,0:T(8,128)S(1)}, u32[]{:S(2)}, u32[]{:S(2)}) collective-permute-start(f32[8,128]{1,0:T(8,128)S(1)} %get-tuple-element.62), channel_id=1, source_target_pairs={{0,1},{2,3},{4,5},{6,7},{8,9},{10,11},{12,13},{14,15},{16,17},{18,... | collective-permute-start | bytes 12296 | tf_op jit(solution)/shard_map/ppermute | solution.py:558
  31.3 4.7 %collective-permute-start.6 = (f32[4,128]{1,0:T(4,128)S(1)}, f32[4,128]{1,0:T(4,128)S(1)}, u32[]{:S(2)}, u32[]{:S(2)}) collective-permute-start(f32[4,128]{1,0:T(4,128)S(1)} %get-tuple-element.63), channel_id=1, source_target_pairs={{32,64},{96,128},{160,192},{224,256},{288,320},{352,384},{416,448}... | collective-permute-start | bytes 6152 | tf_op jit(solution)/shard_map/ppermute | solution.py:547
  36.0 1.9 %collective-permute-start.7 = (f32[4,128]{1,0:T(4,128)S(1)}, f32[4,128]{1,0:T(4,128)S(1)}, u32[]{:S(2)}, u32[]{:S(2)}) collective-permute-start(f32[4,128]{1,0:T(4,128)S(1)} %get-tuple-element.64), channel_id=1, source_target_pairs={{0,32},{64,96},{128,160},{192,224},{256,288},{320,352},{384,416},{... | collective-permute-start | bytes 6152 | tf_op jit(solution)/shard_map/ppermute | solution.py:560
  39.8 4.1 %collective-permute-start.8 = (f32[4,128]{1,0:T(4,128)S(1)}, f32[4,128]{1,0:T(4,128)S(1)}, u32[]{:S(2)}, u32[]{:S(2)}) collective-permute-start(f32[4,128]{1,0:T(4,128)S(1)} %get-tuple-element.69), channel_id=1, source_target_pairs={{32,64},{96,128},{160,192},{224,256},{288,320},{352,384},{416,448}... | collective-permute-start | bytes 6152 | tf_op jit(solution)/shard_map/ppermute | solution.py:547
  45.7 14.7 %all_to_all.20.row_ref = f32[32,3,4,128]{3,2,1,0:T(4,128)S(1)} all-to-all(f32[32,3,4,128]{3,2,1,0:T(4,128)S(1)} %row.2), channel_id=1, replica_groups=mesh['lat'=16,'lon'=32] {'lon'}, dimensions={0} | all-to-all | bytes 393216 | tf_op jit(solution)/shard_map/all_to_all | solution.py:565
  60.4 4.5 %all-gather.1 = f32[6,4,128]{2,1,0:T(4,128)S(1)} all-gather(f32[3,4,128]{2,1,0:T(4,128)S(1)} %get-tuple-element.72), channel_id=3, replica_groups={{0,32},{64,96},{128,160},{192,224},{256,288},{320,352},{384,416},{448,4..., dimensions={0}, use_global_device_ids=true | all-gather | bytes 18432 | tf_op jit(solution)/shard_map/all_gather | solution.py:551
  64.9 5.4 %collective-permute-start.9 = (f32[6,4,128]{2,1,0:T(4,128)S(1)}, f32[6,4,128]{2,1,0:T(4,128)S(1)}, u32[]{:S(2)}, u32[]{:S(2)}) collective-permute-start(f32[6,4,128]{2,1,0:T(4,128)S(1)} %all-gather.1), channel_id=1, source_target_pairs={{32,64},{96,128},{160,192},{224,256},{288,320},{352,384},{416,448}... | collective-permute-start | bytes 36872 | tf_op jit(solution)/shard_map/ppermute | solution.py:547
  74.7 3.0 %collective-permute-start.10 = (f32[4,128]{1,0:T(4,128)S(1)}, f32[4,128]{1,0:T(4,128)S(1)}, u32[]{:S(2)}, u32[]{:S(2)}) collective-permute-start(f32[4,128]{1,0:T(4,128)S(1)} %get-tuple-element.77), channel_id=1, source_target_pairs={{1,2},{3,4},{5,6},{7,8},{9,10},{11,12},{13,14},{15,16},{17,18},{19... | collective-permute-start | bytes 6152 | tf_op jit(solution)/shard_map/ppermute | solution.py:557
  77.7 2.3 %collective-permute-start.11 = (f32[4,128]{1,0:T(4,128)S(1)}, f32[4,128]{1,0:T(4,128)S(1)}, u32[]{:S(2)}, u32[]{:S(2)}) collective-permute-start(f32[4,128]{1,0:T(4,128)S(1)} %get-tuple-element.78), channel_id=1, source_target_pairs={{0,1},{2,3},{4,5},{6,7},{8,9},{10,11},{12,13},{14,15},{16,17},{18,... | collective-permute-start | bytes 6152 | tf_op jit(solution)/shard_map/ppermute | solution.py:558
  80.0 4.2 %collective-permute-start.12 = (f32[4,128]{1,0:T(4,128)S(1)}, f32[4,128]{1,0:T(4,128)S(1)}, u32[]{:S(2)}, u32[]{:S(2)}) collective-permute-start(f32[4,128]{1,0:T(4,128)S(1)} %get-tuple-element.79), channel_id=1, source_target_pairs={{32,64},{96,128},{160,192},{224,256},{288,320},{352,384},{416,448}... | collective-permute-start | bytes 6152 | tf_op jit(solution)/shard_map/ppermute | solution.py:547
  87.8 5.0 %collective-permute-start.14 = (f32[4,128]{1,0:T(4,128)S(1)}, f32[4,128]{1,0:T(4,128)S(1)}, u32[]{:S(2)}, u32[]{:S(2)}) collective-permute-start(f32[4,128]{1,0:T(4,128)S(1)} %get-tuple-element.83), channel_id=1, source_target_pairs={{1,2},{3,4},{5,6},{7,8},{9,10},{11,12},{13,14},{15,16},{17,18},{19... | collective-permute-start | bytes 6152 | tf_op jit(solution)/shard_map/ppermute | solution.py:557
  94.7 3.4 %collective-permute-start.16 = (f32[4,128]{1,0:T(4,128)S(1)}, f32[4,128]{1,0:T(4,128)S(1)}, u32[]{:S(2)}, u32[]{:S(2)}) collective-permute-start(f32[4,128]{1,0:T(4,128)S(1)} %get-tuple-element.85), channel_id=1, source_target_pairs={{32,64},{96,128},{160,192},{224,256},{288,320},{352,384},{416,448}... | collective-permute-start | bytes 6152 | tf_op jit(solution)/shard_map/ppermute | solution.py:547
  98.2 1.9 %collective-permute-start.17 = (f32[4,128]{1,0:T(4,128)S(1)}, f32[4,128]{1,0:T(4,128)S(1)}, u32[]{:S(2)}, u32[]{:S(2)}) collective-permute-start(f32[4,128]{1,0:T(4,128)S(1)} %get-tuple-element.86), channel_id=1, source_target_pairs={{0,32},{64,96},{128,160},{192,224},{256,288},{320,352},{384,416},{... | collective-permute-start | bytes 6152 | tf_op jit(solution)/shard_map/ppermute | solution.py:560
  101.9 3.6 %collective-permute-start.18 = (f32[4,128]{1,0:T(4,128)S(1)}, f32[4,128]{1,0:T(4,128)S(1)}, u32[]{:S(2)}, u32[]{:S(2)}) collective-permute-start(f32[4,128]{1,0:T(4,128)S(1)} %get-tuple-element.89), channel_id=1, source_target_pairs={{32,64},{96,128},{160,192},{224,256},{288,320},{352,384},{416,448}... | collective-permute-start | bytes 6152 | tf_op jit(solution)/shard_map/ppermute | solution.py:547
  107.3 15.2 %all_to_all.21.row_ref = f32[32,3,4,128]{3,2,1,0:T(4,128)S(1)} all-to-all(f32[32,3,4,128]{3,2,1,0:T(4,128)S(1)} %row.3), channel_id=1, replica_groups=mesh['lat'=16,'lon'=32] {'lon'}, dimensions={0} | all-to-all | bytes 393216 | tf_op jit(solution)/shard_map/all_to_all | solution.py:565
  122.6 4.5 %all-gather.4 = f32[6,4,128]{2,1,0:T(4,128)S(1)} all-gather(f32[3,4,128]{2,1,0:T(4,128)S(1)} %get-tuple-element.92), channel_id=6, replica_groups={{0,32},{64,96},{128,160},{192,224},{256,288},{320,352},{384,416},{448,4..., dimensions={0}, use_global_device_ids=true | all-gather | bytes 18432 | tf_op jit(solution)/shard_map/all_gather | solution.py:551
  127.1 3.9 %collective-permute-start.19 = (f32[6,4,128]{2,1,0:T(4,128)S(1)}, f32[6,4,128]{2,1,0:T(4,128)S(1)}, u32[]{:S(2)}, u32[]{:S(2)}) collective-permute-start(f32[6,4,128]{2,1,0:T(4,128)S(1)} %all-gather.4), channel_id=1, source_target_pairs={{32,64},{96,128},{160,192},{224,256},{288,320},{352,384},{416,448}... | collective-permute-start | bytes 36872 | tf_op jit(solution)/shard_map/ppermute | solution.py:547
  135.3 14.2 %all_to_all.22 = f32[16,1,128]{2,1,0:T(1,128)S(1)} all-to-all(f32[16,1,128]{2,1,0:T(1,128)S(1)} %get-tuple-element.95), channel_id=1, replica_groups=mesh['lat'=16,'lon'=32] {'lat'}, dimensions={0} | all-to-all | bytes 16384 | tf_op jit(solution)/shard_map/all_to_all | solution.py:565
  149.6 12.3 %all_to_all.23.sums_ref = f32[32,1,128]{2,1,0:T(1,128)S(1)} all-to-all(f32[32,1,128]{2,1,0:T(1,128)S(1)} %broadcast_in_dim.2), channel_id=1, replica_groups=mesh['lat'=16,'lon'=32] {'lon'}, dimensions={0} | all-to-all | bytes 32768 | tf_op jit(solution)/shard_map/all_to_all | solution.py:565
  (54 shorter events, 29.8 us)
Async XLA Ops:
  2.1 0.8 copy-start
  2.9 1.2 copy-start.2
  5.2 18.9 %collective-permute-start = (f32[12,128]{1,0:T(8,128)S(1)}, f32[12,128]{1,0:T(8,128)S(1)}, u32[]{:S(2)}, u32[]{:S(2)}) collective-permute-start(f32[12,128]{1,0:T(8,128)S(1)} %get-tuple-element.51), channel_id=1, source_target_pairs={{1,2},{3,4},{5,6},{7,8},{9,10},{11,12},{13,14},{15,16},{17,18},{19... | collective-permute-start | bytes 18440 | tf_op jit(solution)/shard_map/ppermute | solution.py:557
  13.4 10.8 %collective-permute-start.1 = (f32[12,128]{1,0:T(8,128)S(1)}, f32[12,128]{1,0:T(8,128)S(1)}, u32[]{:S(2)}, u32[]{:S(2)}) collective-permute-start(f32[12,128]{1,0:T(8,128)S(1)} %get-tuple-element.52), channel_id=1, source_target_pairs={{0,1},{2,3},{4,5},{6,7},{8,9},{10,11},{12,13},{14,15},{16,17},{18,... | collective-permute-start | bytes 18440 | tf_op jit(solution)/shard_map/ppermute | solution.py:558
  15.3 8.9 %collective-permute-start.2 = (f32[12,128]{1,0:T(8,128)S(1)}, f32[12,128]{1,0:T(8,128)S(1)}, u32[]{:S(2)}, u32[]{:S(2)}) collective-permute-start(f32[12,128]{1,0:T(8,128)S(1)} %get-tuple-element.53), channel_id=1, source_target_pairs={{32,64},{96,128},{160,192},{224,256},{288,320},{352,384},{416,448}... | collective-permute-start | bytes 18440 | tf_op jit(solution)/shard_map/ppermute | solution.py:547
  20.2 4.1 %collective-permute-start.3 = (f32[12,128]{1,0:T(8,128)S(1)}, f32[12,128]{1,0:T(8,128)S(1)}, u32[]{:S(2)}, u32[]{:S(2)}) collective-permute-start(f32[12,128]{1,0:T(8,128)S(1)} %get-tuple-element.54), channel_id=1, source_target_pairs={{0,32},{64,96},{128,160},{192,224},{256,288},{320,352},{384,416},{... | collective-permute-start | bytes 18440 | tf_op jit(solution)/shard_map/ppermute | solution.py:560
  22.1 1.2 copy-start.3
  23.6 0.8 copy-start.1
  25.1 14.0 %collective-permute-start.4 = (f32[8,128]{1,0:T(8,128)S(1)}, f32[8,128]{1,0:T(8,128)S(1)}, u32[]{:S(2)}, u32[]{:S(2)}) collective-permute-start(f32[8,128]{1,0:T(8,128)S(1)} %get-tuple-element.61), channel_id=1, source_target_pairs={{1,2},{3,4},{5,6},{7,8},{9,10},{11,12},{13,14},{15,16},{17,18},{19... | collective-permute-start | bytes 12296 | tf_op jit(solution)/shard_map/ppermute | solution.py:557
  29.4 9.7 %collective-permute-start.5 = (f32[8,128]{1,0:T(8,128)S(1)}, f32[8,128]{1,0:T(8,128)S(1)}, u32[]{:S(2)}, u32[]{:S(2)}) collective-permute-start(f32[8,128]{1,0:T(8,128)S(1)} %get-tuple-element.62), channel_id=1, source_target_pairs={{0,1},{2,3},{4,5},{6,7},{8,9},{10,11},{12,13},{14,15},{16,17},{18,... | collective-permute-start | bytes 12296 | tf_op jit(solution)/shard_map/ppermute | solution.py:558
  31.3 7.1 %collective-permute-start.6 = (f32[4,128]{1,0:T(4,128)S(1)}, f32[4,128]{1,0:T(4,128)S(1)}, u32[]{:S(2)}, u32[]{:S(2)}) collective-permute-start(f32[4,128]{1,0:T(4,128)S(1)} %get-tuple-element.63), channel_id=1, source_target_pairs={{32,64},{96,128},{160,192},{224,256},{288,320},{352,384},{416,448}... | collective-permute-start | bytes 6152 | tf_op jit(solution)/shard_map/ppermute | solution.py:547
  36.0 3.1 %collective-permute-start.7 = (f32[4,128]{1,0:T(4,128)S(1)}, f32[4,128]{1,0:T(4,128)S(1)}, u32[]{:S(2)}, u32[]{:S(2)}) collective-permute-start(f32[4,128]{1,0:T(4,128)S(1)} %get-tuple-element.64), channel_id=1, source_target_pairs={{0,32},{64,96},{128,160},{192,224},{256,288},{320,352},{384,416},{... | collective-permute-start | bytes 6152 | tf_op jit(solution)/shard_map/ppermute | solution.py:560
  39.8 5.9 %collective-permute-start.8 = (f32[4,128]{1,0:T(4,128)S(1)}, f32[4,128]{1,0:T(4,128)S(1)}, u32[]{:S(2)}, u32[]{:S(2)}) collective-permute-start(f32[4,128]{1,0:T(4,128)S(1)} %get-tuple-element.69), channel_id=1, source_target_pairs={{32,64},{96,128},{160,192},{224,256},{288,320},{352,384},{416,448}... | collective-permute-start | bytes 6152 | tf_op jit(solution)/shard_map/ppermute | solution.py:547
  64.9 6.8 %collective-permute-start.9 = (f32[6,4,128]{2,1,0:T(4,128)S(1)}, f32[6,4,128]{2,1,0:T(4,128)S(1)}, u32[]{:S(2)}, u32[]{:S(2)}) collective-permute-start(f32[6,4,128]{2,1,0:T(4,128)S(1)} %all-gather.1), channel_id=1, source_target_pairs={{32,64},{96,128},{160,192},{224,256},{288,320},{352,384},{416,448}... | collective-permute-start | bytes 36872 | tf_op jit(solution)/shard_map/ppermute | solution.py:547
  74.7 12.0 %collective-permute-start.10 = (f32[4,128]{1,0:T(4,128)S(1)}, f32[4,128]{1,0:T(4,128)S(1)}, u32[]{:S(2)}, u32[]{:S(2)}) collective-permute-start(f32[4,128]{1,0:T(4,128)S(1)} %get-tuple-element.77), channel_id=1, source_target_pairs={{1,2},{3,4},{5,6},{7,8},{9,10},{11,12},{13,14},{15,16},{17,18},{19... | collective-permute-start | bytes 6152 | tf_op jit(solution)/shard_map/ppermute | solution.py:557
  77.7 9.0 %collective-permute-start.11 = (f32[4,128]{1,0:T(4,128)S(1)}, f32[4,128]{1,0:T(4,128)S(1)}, u32[]{:S(2)}, u32[]{:S(2)}) collective-permute-start(f32[4,128]{1,0:T(4,128)S(1)} %get-tuple-element.78), channel_id=1, source_target_pairs={{0,1},{2,3},{4,5},{6,7},{8,9},{10,11},{12,13},{14,15},{16,17},{18,... | collective-permute-start | bytes 6152 | tf_op jit(solution)/shard_map/ppermute | solution.py:558
  80.0 6.7 %collective-permute-start.12 = (f32[4,128]{1,0:T(4,128)S(1)}, f32[4,128]{1,0:T(4,128)S(1)}, u32[]{:S(2)}, u32[]{:S(2)}) collective-permute-start(f32[4,128]{1,0:T(4,128)S(1)} %get-tuple-element.79), channel_id=1, source_target_pairs={{32,64},{96,128},{160,192},{224,256},{288,320},{352,384},{416,448}... | collective-permute-start | bytes 6152 | tf_op jit(solution)/shard_map/ppermute | solution.py:547
  84.3 3.1 %collective-permute-start.13 = (f32[4,128]{1,0:T(4,128)S(1)}, f32[4,128]{1,0:T(4,128)S(1)}, u32[]{:S(2)}, u32[]{:S(2)}) collective-permute-start(f32[4,128]{1,0:T(4,128)S(1)} %get-tuple-element.80), channel_id=1, source_target_pairs={{0,32},{64,96},{128,160},{192,224},{256,288},{320,352},{384,416},{... | collective-permute-start | bytes 6152 | tf_op jit(solution)/shard_map/ppermute | solution.py:560
  87.8 12.8 %collective-permute-start.14 = (f32[4,128]{1,0:T(4,128)S(1)}, f32[4,128]{1,0:T(4,128)S(1)}, u32[]{:S(2)}, u32[]{:S(2)}) collective-permute-start(f32[4,128]{1,0:T(4,128)S(1)} %get-tuple-element.83), channel_id=1, source_target_pairs={{1,2},{3,4},{5,6},{7,8},{9,10},{11,12},{13,14},{15,16},{17,18},{19... | collective-permute-start | bytes 6152 | tf_op jit(solution)/shard_map/ppermute | solution.py:557
  92.8 7.8 %collective-permute-start.15 = (f32[4,128]{1,0:T(4,128)S(1)}, f32[4,128]{1,0:T(4,128)S(1)}, u32[]{:S(2)}, u32[]{:S(2)}) collective-permute-start(f32[4,128]{1,0:T(4,128)S(1)} %get-tuple-element.84), channel_id=1, source_target_pairs={{0,1},{2,3},{4,5},{6,7},{8,9},{10,11},{12,13},{14,15},{16,17},{18,... | collective-permute-start | bytes 6152 | tf_op jit(solution)/shard_map/ppermute | solution.py:558
  94.7 5.9 %collective-permute-start.16 = (f32[4,128]{1,0:T(4,128)S(1)}, f32[4,128]{1,0:T(4,128)S(1)}, u32[]{:S(2)}, u32[]{:S(2)}) collective-permute-start(f32[4,128]{1,0:T(4,128)S(1)} %get-tuple-element.85), channel_id=1, source_target_pairs={{32,64},{96,128},{160,192},{224,256},{288,320},{352,384},{416,448}... | collective-permute-start | bytes 6152 | tf_op jit(solution)/shard_map/ppermute | solution.py:547
  98.2 3.1 %collective-permute-start.17 = (f32[4,128]{1,0:T(4,128)S(1)}, f32[4,128]{1,0:T(4,128)S(1)}, u32[]{:S(2)}, u32[]{:S(2)}) collective-permute-start(f32[4,128]{1,0:T(4,128)S(1)} %get-tuple-element.86), channel_id=1, source_target_pairs={{0,32},{64,96},{128,160},{192,224},{256,288},{320,352},{384,416},{... | collective-permute-start | bytes 6152 | tf_op jit(solution)/shard_map/ppermute | solution.py:560
  101.9 5.4 %collective-permute-start.18 = (f32[4,128]{1,0:T(4,128)S(1)}, f32[4,128]{1,0:T(4,128)S(1)}, u32[]{:S(2)}, u32[]{:S(2)}) collective-permute-start(f32[4,128]{1,0:T(4,128)S(1)} %get-tuple-element.89), channel_id=1, source_target_pairs={{32,64},{96,128},{160,192},{224,256},{288,320},{352,384},{416,448}... | collective-permute-start | bytes 6152 | tf_op jit(solution)/shard_map/ppermute | solution.py:547
  127.1 5.3 %collective-permute-start.19 = (f32[6,4,128]{2,1,0:T(4,128)S(1)}, f32[6,4,128]{2,1,0:T(4,128)S(1)}, u32[]{:S(2)}, u32[]{:S(2)}) collective-permute-start(f32[6,4,128]{2,1,0:T(4,128)S(1)} %all-gather.4), channel_id=1, source_target_pairs={{32,64},{96,128},{160,192},{224,256},{288,320},{352,384},{416,448}... | collective-permute-start | bytes 36872 | tf_op jit(solution)/shard_map/ppermute | solution.py:547

commit v7 on v6

--- a/solution.py
+++ b/solution.py
@@ -295,7 +295,7 @@
 
 def smooth_first_kernel(
     a0, a1, a2, a3, own_ref, ohi_ref, pack_ref, first_ref, local_ref, scale_ref,
-    m0, m1, m2, m3, second_ref, ninv_ref, ends_ref, oha_ref,
+    m0, m1, m2, m3, second_ref, ninv_ref,
 ):
     arrived = collect((a0, a1, a2, a3))
     smooth(arrived, ohi_ref, pack_ref, first_ref, local_ref, scale_ref, pack_ref, (m0, m1, m2, m3), second_ref)
@@ -307,6 +307,9 @@
     ninv_ref[2:4] = inverse[1]
     for ref in (m0, m1):
         ref[4:8] = ninv_ref[...]
+
+
+def ends_kernel(a0, a1, a2, a3, second_ref, ends_ref, oha_ref):
     for d, part in enumerate(collect((a0, a1, a2, a3), 8)):
         for k in range(2):
             row = jnp.concatenate([part[2 * k : 2 * k + 1], part[2 * k + 1 : 2 * k + 2]], axis=1)
@@ -602,11 +605,18 @@
     for step in range(ITERS):
         stiff = local(first)
         if step == 0:
-            *sent, second, ninv, ends, oha = call(
+            *sent, second, ninv = call(
                 smooth_first_kernel,
-                [shape(8, BS)] * 2 + MESSAGES[2:] + [FIELD, shape(4, BS), shape(1, 8 * IFC, dtype=jnp.int32), shape(BS, 8 * IFC, dtype=BF16)],
+                [shape(8, BS)] * 2 + MESSAGES[2:] + [FIELD, shape(4, BS)],
                 (*arrived, own, ohi, pack, first, stiff, scale),
                 "smooth_first",
+            )
+            ends, oha = call(
+                ends_kernel,
+                [shape(1, 8 * IFC, dtype=jnp.int32), shape(BS, 8 * IFC, dtype=BF16)],
+                (*arrived, second),
+                "ends",
+                flops=10**7,
             )
             source = pack
         else:

time: 164 us -> 164 us (level)
    pallas_call x18 -> x19, Pallas kernels: 10.9 us -> 10.9 us  [call(): pl.pallas_call(body, out_shape=outs, in_specs=specs, out_specs=[pl.BlockS...]
where the time goes in v7:
time: 164 us; the launch traced here: 163 us
  blocking collectives  72.6 us (44%)
  starting transfers between devices  70.3 us (43%)
  Pallas kernels  10.9 us (7%)
  waiting for transfers between devices  4.31 us (3%)
  local copies, waits for them, and re-layouts  3.44 us (2%)
    all_to_all x4, blocking collectives, everywhere(): return lax.all_to_all(row, axis, 0, 0)  56.5 us
    ppermute x8, starting transfers between devices, swap_far(): return lax.ppermute(message, 'lat', swap(lat_pairs(1)))  34.1 us
    ppermute x4, starting transfers between devices, exchange(): lax.ppermute(messages[0], 'lon', swap([(k, (k + 1) % lon) for k in range(...  20.4 us
    all_gather x6, blocking collectives, on_chip(): return lax.all_gather(message, 'lat', axis_index_groups=lat_pairs(0))  16.2 us
    pallas_call x19, Pallas kernels, call(): pl.pallas_call(body, out_shape=outs, in_specs=specs, out_specs=[pl.BlockS...  10.9 us
    ppermute x4, starting transfers between devices, exchange(): lax.ppermute(messages[1], 'lon', swap([(k, k + 1) for k in range(0, lon,...  8.08 us
    ppermute x4, starting transfers between devices, exchange(): lax.ppermute(messages[3], 'lat', swap(lat_pairs(0)))  7.68 us
    unnamed x8, local copies, waits for them, and re-layouts  3.42 us
  transfers between devices with their start and end apart: 20, of which 5 were waited for; matrix products, arithmetic and copies ran while one was open for 0% of the time, Pallas kernels for 2%

profile of v7, /device:TPU:1, one launch (start us, length us, event | category | flops | bytes accessed | tf_op | source)
XLA Modules:
  0.0 162.5 jit_solution(9649050591366921534)
XLA Ops:
  5.2 8.1 %collective-permute-start = (f32[12,128]{1,0:T(8,128)S(1)}, f32[12,128]{1,0:T(8,128)S(1)}, u32[]{:S(2)}, u32[]{:S(2)}) collective-permute-start(f32[12,128]{1,0:T(8,128)S(1)} %get-tuple-element.51), channel_id=1, source_target_pairs={{1,2},{3,4},{5,6},{7,8},{9,10},{11,12},{13,14},{15,16},{17,18},{19... | collective-permute-start | bytes 18440 | tf_op jit(solution)/shard_map/ppermute | solution.py:560
  13.4 1.9 %collective-permute-start.1 = (f32[12,128]{1,0:T(8,128)S(1)}, f32[12,128]{1,0:T(8,128)S(1)}, u32[]{:S(2)}, u32[]{:S(2)}) collective-permute-start(f32[12,128]{1,0:T(8,128)S(1)} %get-tuple-element.52), channel_id=1, source_target_pairs={{0,1},{2,3},{4,5},{6,7},{8,9},{10,11},{12,13},{14,15},{16,17},{18,... | collective-permute-start | bytes 18440 | tf_op jit(solution)/shard_map/ppermute | solution.py:561
  15.3 4.8 %collective-permute-start.2 = (f32[12,128]{1,0:T(8,128)S(1)}, f32[12,128]{1,0:T(8,128)S(1)}, u32[]{:S(2)}, u32[]{:S(2)}) collective-permute-start(f32[12,128]{1,0:T(8,128)S(1)} %get-tuple-element.53), channel_id=1, source_target_pairs={{32,64},{96,128},{160,192},{224,256},{288,320},{352,384},{416,448}... | collective-permute-start | bytes 18440 | tf_op jit(solution)/shard_map/ppermute | solution.py:550
  20.2 1.9 %collective-permute-start.3 = (f32[12,128]{1,0:T(8,128)S(1)}, f32[12,128]{1,0:T(8,128)S(1)}, u32[]{:S(2)}, u32[]{:S(2)}) collective-permute-start(f32[12,128]{1,0:T(8,128)S(1)} %get-tuple-element.54), channel_id=1, source_target_pairs={{0,32},{64,96},{128,160},{192,224},{256,288},{320,352},{384,416},{... | collective-permute-start | bytes 18440 | tf_op jit(solution)/shard_map/ppermute | solution.py:563
  24.9 4.3 %collective-permute-start.4 = (f32[8,128]{1,0:T(8,128)S(1)}, f32[8,128]{1,0:T(8,128)S(1)}, u32[]{:S(2)}, u32[]{:S(2)}) collective-permute-start(f32[8,128]{1,0:T(8,128)S(1)} %get-tuple-element.61), channel_id=1, source_target_pairs={{1,2},{3,4},{5,6},{7,8},{9,10},{11,12},{13,14},{15,16},{17,18},{19... | collective-permute-start | bytes 12296 | tf_op jit(solution)/shard_map/ppermute | solution.py:560
  29.3 1.9 %collective-permute-start.5 = (f32[8,128]{1,0:T(8,128)S(1)}, f32[8,128]{1,0:T(8,128)S(1)}, u32[]{:S(2)}, u32[]{:S(2)}) collective-permute-start(f32[8,128]{1,0:T(8,128)S(1)} %get-tuple-element.62), channel_id=1, source_target_pairs={{0,1},{2,3},{4,5},{6,7},{8,9},{10,11},{12,13},{14,15},{16,17},{18,... | collective-permute-start | bytes 12296 | tf_op jit(solution)/shard_map/ppermute | solution.py:561
  31.2 4.7 %collective-permute-start.6 = (f32[4,128]{1,0:T(4,128)S(1)}, f32[4,128]{1,0:T(4,128)S(1)}, u32[]{:S(2)}, u32[]{:S(2)}) collective-permute-start(f32[4,128]{1,0:T(4,128)S(1)} %get-tuple-element.63), channel_id=1, source_target_pairs={{32,64},{96,128},{160,192},{224,256},{288,320},{352,384},{416,448}... | collective-permute-start | bytes 6152 | tf_op jit(solution)/shard_map/ppermute | solution.py:550
  35.9 1.9 %collective-permute-start.7 = (f32[4,128]{1,0:T(4,128)S(1)}, f32[4,128]{1,0:T(4,128)S(1)}, u32[]{:S(2)}, u32[]{:S(2)}) collective-permute-start(f32[4,128]{1,0:T(4,128)S(1)} %get-tuple-element.64), channel_id=1, source_target_pairs={{0,32},{64,96},{128,160},{192,224},{256,288},{320,352},{384,416},{... | collective-permute-start | bytes 6152 | tf_op jit(solution)/shard_map/ppermute | solution.py:563
  39.6 4.1 %collective-permute-start.8 = (f32[4,128]{1,0:T(4,128)S(1)}, f32[4,128]{1,0:T(4,128)S(1)}, u32[]{:S(2)}, u32[]{:S(2)}) collective-permute-start(f32[4,128]{1,0:T(4,128)S(1)} %get-tuple-element.69), channel_id=1, source_target_pairs={{32,64},{96,128},{160,192},{224,256},{288,320},{352,384},{416,448}... | collective-permute-start | bytes 6152 | tf_op jit(solution)/shard_map/ppermute | solution.py:550
  45.5 14.7 %all_to_all.20.row_ref = f32[32,3,4,128]{3,2,1,0:T(4,128)S(1)} all-to-all(f32[32,3,4,128]{3,2,1,0:T(4,128)S(1)} %row.2), channel_id=1, replica_groups=mesh['lat'=16,'lon'=32] {'lon'}, dimensions={0} | all-to-all | bytes 393216 | tf_op jit(solution)/shard_map/all_to_all | solution.py:568
  60.2 4.5 %all-gather.1 = f32[6,4,128]{2,1,0:T(4,128)S(1)} all-gather(f32[3,4,128]{2,1,0:T(4,128)S(1)} %get-tuple-element.72), channel_id=3, replica_groups={{0,32},{64,96},{128,160},{192,224},{256,288},{320,352},{384,416},{448,4..., dimensions={0}, use_global_device_ids=true | all-gather | bytes 18432 | tf_op jit(solution)/shard_map/all_gather | solution.py:554
  64.7 5.4 %collective-permute-start.9 = (f32[6,4,128]{2,1,0:T(4,128)S(1)}, f32[6,4,128]{2,1,0:T(4,128)S(1)}, u32[]{:S(2)}, u32[]{:S(2)}) collective-permute-start(f32[6,4,128]{2,1,0:T(4,128)S(1)} %all-gather.1), channel_id=1, source_target_pairs={{32,64},{96,128},{160,192},{224,256},{288,320},{352,384},{416,448}... | collective-permute-start | bytes 36872 | tf_op jit(solution)/shard_map/ppermute | solution.py:550
  74.6 3.0 %collective-permute-start.10 = (f32[4,128]{1,0:T(4,128)S(1)}, f32[4,128]{1,0:T(4,128)S(1)}, u32[]{:S(2)}, u32[]{:S(2)}) collective-permute-start(f32[4,128]{1,0:T(4,128)S(1)} %get-tuple-element.77), channel_id=1, source_target_pairs={{1,2},{3,4},{5,6},{7,8},{9,10},{11,12},{13,14},{15,16},{17,18},{19... | collective-permute-start | bytes 6152 | tf_op jit(solution)/shard_map/ppermute | solution.py:560
  77.5 2.3 %collective-permute-start.11 = (f32[4,128]{1,0:T(4,128)S(1)}, f32[4,128]{1,0:T(4,128)S(1)}, u32[]{:S(2)}, u32[]{:S(2)}) collective-permute-start(f32[4,128]{1,0:T(4,128)S(1)} %get-tuple-element.78), channel_id=1, source_target_pairs={{0,1},{2,3},{4,5},{6,7},{8,9},{10,11},{12,13},{14,15},{16,17},{18,... | collective-permute-start | bytes 6152 | tf_op jit(solution)/shard_map/ppermute | solution.py:561
  79.9 4.2 %collective-permute-start.12 = (f32[4,128]{1,0:T(4,128)S(1)}, f32[4,128]{1,0:T(4,128)S(1)}, u32[]{:S(2)}, u32[]{:S(2)}) collective-permute-start(f32[4,128]{1,0:T(4,128)S(1)} %get-tuple-element.79), channel_id=1, source_target_pairs={{32,64},{96,128},{160,192},{224,256},{288,320},{352,384},{416,448}... | collective-permute-start | bytes 6152 | tf_op jit(solution)/shard_map/ppermute | solution.py:550
  84.1 1.9 %collective-permute-start.13 = (f32[4,128]{1,0:T(4,128)S(1)}, f32[4,128]{1,0:T(4,128)S(1)}, u32[]{:S(2)}, u32[]{:S(2)}) collective-permute-start(f32[4,128]{1,0:T(4,128)S(1)} %get-tuple-element.80), channel_id=1, source_target_pairs={{0,32},{64,96},{128,160},{192,224},{256,288},{320,352},{384,416},{... | collective-permute-start | bytes 6152 | tf_op jit(solution)/shard_map/ppermute | solution.py:563
  87.7 5.0 %collective-permute-start.14 = (f32[4,128]{1,0:T(4,128)S(1)}, f32[4,128]{1,0:T(4,128)S(1)}, u32[]{:S(2)}, u32[]{:S(2)}) collective-permute-start(f32[4,128]{1,0:T(4,128)S(1)} %get-tuple-element.83), channel_id=1, source_target_pairs={{1,2},{3,4},{5,6},{7,8},{9,10},{11,12},{13,14},{15,16},{17,18},{19... | collective-permute-start | bytes 6152 | tf_op jit(solution)/shard_map/ppermute | solution.py:560
  94.6 3.4 %collective-permute-start.16 = (f32[4,128]{1,0:T(4,128)S(1)}, f32[4,128]{1,0:T(4,128)S(1)}, u32[]{:S(2)}, u32[]{:S(2)}) collective-permute-start(f32[4,128]{1,0:T(4,128)S(1)} %get-tuple-element.85), channel_id=1, source_target_pairs={{32,64},{96,128},{160,192},{224,256},{288,320},{352,384},{416,448}... | collective-permute-start | bytes 6152 | tf_op jit(solution)/shard_map/ppermute | solution.py:550
  101.7 3.6 %collective-permute-start.18 = (f32[4,128]{1,0:T(4,128)S(1)}, f32[4,128]{1,0:T(4,128)S(1)}, u32[]{:S(2)}, u32[]{:S(2)}) collective-permute-start(f32[4,128]{1,0:T(4,128)S(1)} %get-tuple-element.89), channel_id=1, source_target_pairs={{32,64},{96,128},{160,192},{224,256},{288,320},{352,384},{416,448}... | collective-permute-start | bytes 6152 | tf_op jit(solution)/shard_map/ppermute | solution.py:550
  107.2 15.2 %all_to_all.21.row_ref = f32[32,3,4,128]{3,2,1,0:T(4,128)S(1)} all-to-all(f32[32,3,4,128]{3,2,1,0:T(4,128)S(1)} %row.3), channel_id=1, replica_groups=mesh['lat'=16,'lon'=32] {'lon'}, dimensions={0} | all-to-all | bytes 393216 | tf_op jit(solution)/shard_map/all_to_all | solution.py:568
  122.4 4.5 %all-gather.4 = f32[6,4,128]{2,1,0:T(4,128)S(1)} all-gather(f32[3,4,128]{2,1,0:T(4,128)S(1)} %get-tuple-element.92), channel_id=6, replica_groups={{0,32},{64,96},{128,160},{192,224},{256,288},{320,352},{384,416},{448,4..., dimensions={0}, use_global_device_ids=true | all-gather | bytes 18432 | tf_op jit(solution)/shard_map/all_gather | solution.py:554
  126.9 3.9 %collective-permute-start.19 = (f32[6,4,128]{2,1,0:T(4,128)S(1)}, f32[6,4,128]{2,1,0:T(4,128)S(1)}, u32[]{:S(2)}, u32[]{:S(2)}) collective-permute-start(f32[6,4,128]{2,1,0:T(4,128)S(1)} %all-gather.4), channel_id=1, source_target_pairs={{32,64},{96,128},{160,192},{224,256},{288,320},{352,384},{416,448}... | collective-permute-start | bytes 36872 | tf_op jit(solution)/shard_map/ppermute | solution.py:550
  135.2 14.2 %all_to_all.22 = f32[16,1,128]{2,1,0:T(1,128)S(1)} all-to-all(f32[16,1,128]{2,1,0:T(1,128)S(1)} %get-tuple-element.95), channel_id=1, replica_groups=mesh['lat'=16,'lon'=32] {'lat'}, dimensions={0} | all-to-all | bytes 16384 | tf_op jit(solution)/shard_map/all_to_all | solution.py:568
  149.4 12.3 %all_to_all.23.sums_ref = f32[32,1,128]{2,1,0:T(1,128)S(1)} all-to-all(f32[32,1,128]{2,1,0:T(1,128)S(1)} %broadcast_in_dim.2), channel_id=1, replica_groups=mesh['lat'=16,'lon'=32] {'lon'}, dimensions={0} | all-to-all | bytes 32768 | tf_op jit(solution)/shard_map/all_to_all | solution.py:568
  (55 shorter events, 29.7 us)
Async XLA Ops:
  2.1 0.8 copy-start
  2.9 1.2 copy-start.2
  5.2 18.9 %collective-permute-start = (f32[12,128]{1,0:T(8,128)S(1)}, f32[12,128]{1,0:T(8,128)S(1)}, u32[]{:S(2)}, u32[]{:S(2)}) collective-permute-start(f32[12,128]{1,0:T(8,128)S(1)} %get-tuple-element.51), channel_id=1, source_target_pairs={{1,2},{3,4},{5,6},{7,8},{9,10},{11,12},{13,14},{15,16},{17,18},{19... | collective-permute-start | bytes 18440 | tf_op jit(solution)/shard_map/ppermute | solution.py:560
  13.4 10.8 %collective-permute-start.1 = (f32[12,128]{1,0:T(8,128)S(1)}, f32[12,128]{1,0:T(8,128)S(1)}, u32[]{:S(2)}, u32[]{:S(2)}) collective-permute-start(f32[12,128]{1,0:T(8,128)S(1)} %get-tuple-element.52), channel_id=1, source_target_pairs={{0,1},{2,3},{4,5},{6,7},{8,9},{10,11},{12,13},{14,15},{16,17},{18,... | collective-permute-start | bytes 18440 | tf_op jit(solution)/shard_map/ppermute | solution.py:561
  15.3 8.9 %collective-permute-start.2 = (f32[12,128]{1,0:T(8,128)S(1)}, f32[12,128]{1,0:T(8,128)S(1)}, u32[]{:S(2)}, u32[]{:S(2)}) collective-permute-start(f32[12,128]{1,0:T(8,128)S(1)} %get-tuple-element.53), channel_id=1, source_target_pairs={{32,64},{96,128},{160,192},{224,256},{288,320},{352,384},{416,448}... | collective-permute-start | bytes 18440 | tf_op jit(solution)/shard_map/ppermute | solution.py:550
  20.2 4.1 %collective-permute-start.3 = (f32[12,128]{1,0:T(8,128)S(1)}, f32[12,128]{1,0:T(8,128)S(1)}, u32[]{:S(2)}, u32[]{:S(2)}) collective-permute-start(f32[12,128]{1,0:T(8,128)S(1)} %get-tuple-element.54), channel_id=1, source_target_pairs={{0,32},{64,96},{128,160},{192,224},{256,288},{320,352},{384,416},{... | collective-permute-start | bytes 18440 | tf_op jit(solution)/shard_map/ppermute | solution.py:563
  22.1 1.2 copy-start.3
  23.6 0.8 copy-start.1
  24.9 14.0 %collective-permute-start.4 = (f32[8,128]{1,0:T(8,128)S(1)}, f32[8,128]{1,0:T(8,128)S(1)}, u32[]{:S(2)}, u32[]{:S(2)}) collective-permute-start(f32[8,128]{1,0:T(8,128)S(1)} %get-tuple-element.61), channel_id=1, source_target_pairs={{1,2},{3,4},{5,6},{7,8},{9,10},{11,12},{13,14},{15,16},{17,18},{19... | collective-permute-start | bytes 12296 | tf_op jit(solution)/shard_map/ppermute | solution.py:560
  29.3 9.7 %collective-permute-start.5 = (f32[8,128]{1,0:T(8,128)S(1)}, f32[8,128]{1,0:T(8,128)S(1)}, u32[]{:S(2)}, u32[]{:S(2)}) collective-permute-start(f32[8,128]{1,0:T(8,128)S(1)} %get-tuple-element.62), channel_id=1, source_target_pairs={{0,1},{2,3},{4,5},{6,7},{8,9},{10,11},{12,13},{14,15},{16,17},{18,... | collective-permute-start | bytes 12296 | tf_op jit(solution)/shard_map/ppermute | solution.py:561
  31.2 7.1 %collective-permute-start.6 = (f32[4,128]{1,0:T(4,128)S(1)}, f32[4,128]{1,0:T(4,128)S(1)}, u32[]{:S(2)}, u32[]{:S(2)}) collective-permute-start(f32[4,128]{1,0:T(4,128)S(1)} %get-tuple-element.63), channel_id=1, source_target_pairs={{32,64},{96,128},{160,192},{224,256},{288,320},{352,384},{416,448}... | collective-permute-start | bytes 6152 | tf_op jit(solution)/shard_map/ppermute | solution.py:550
  35.9 3.1 %collective-permute-start.7 = (f32[4,128]{1,0:T(4,128)S(1)}, f32[4,128]{1,0:T(4,128)S(1)}, u32[]{:S(2)}, u32[]{:S(2)}) collective-permute-start(f32[4,128]{1,0:T(4,128)S(1)} %get-tuple-element.64), channel_id=1, source_target_pairs={{0,32},{64,96},{128,160},{192,224},{256,288},{320,352},{384,416},{... | collective-permute-start | bytes 6152 | tf_op jit(solution)/shard_map/ppermute | solution.py:563
  39.6 5.9 %collective-permute-start.8 = (f32[4,128]{1,0:T(4,128)S(1)}, f32[4,128]{1,0:T(4,128)S(1)}, u32[]{:S(2)}, u32[]{:S(2)}) collective-permute-start(f32[4,128]{1,0:T(4,128)S(1)} %get-tuple-element.69), channel_id=1, source_target_pairs={{32,64},{96,128},{160,192},{224,256},{288,320},{352,384},{416,448}... | collective-permute-start | bytes 6152 | tf_op jit(solution)/shard_map/ppermute | solution.py:550
  64.7 6.8 %collective-permute-start.9 = (f32[6,4,128]{2,1,0:T(4,128)S(1)}, f32[6,4,128]{2,1,0:T(4,128)S(1)}, u32[]{:S(2)}, u32[]{:S(2)}) collective-permute-start(f32[6,4,128]{2,1,0:T(4,128)S(1)} %all-gather.1), channel_id=1, source_target_pairs={{32,64},{96,128},{160,192},{224,256},{288,320},{352,384},{416,448}... | collective-permute-start | bytes 36872 | tf_op jit(solution)/shard_map/ppermute | solution.py:550
  74.6 12.0 %collective-permute-start.10 = (f32[4,128]{1,0:T(4,128)S(1)}, f32[4,128]{1,0:T(4,128)S(1)}, u32[]{:S(2)}, u32[]{:S(2)}) collective-permute-start(f32[4,128]{1,0:T(4,128)S(1)} %get-tuple-element.77), channel_id=1, source_target_pairs={{1,2},{3,4},{5,6},{7,8},{9,10},{11,12},{13,14},{15,16},{17,18},{19... | collective-permute-start | bytes 6152 | tf_op jit(solution)/shard_map/ppermute | solution.py:560
  77.5 9.0 %collective-permute-start.11 = (f32[4,128]{1,0:T(4,128)S(1)}, f32[4,128]{1,0:T(4,128)S(1)}, u32[]{:S(2)}, u32[]{:S(2)}) collective-permute-start(f32[4,128]{1,0:T(4,128)S(1)} %get-tuple-element.78), channel_id=1, source_target_pairs={{0,1},{2,3},{4,5},{6,7},{8,9},{10,11},{12,13},{14,15},{16,17},{18,... | collective-permute-start | bytes 6152 | tf_op jit(solution)/shard_map/ppermute | solution.py:561
  79.9 6.7 %collective-permute-start.12 = (f32[4,128]{1,0:T(4,128)S(1)}, f32[4,128]{1,0:T(4,128)S(1)}, u32[]{:S(2)}, u32[]{:S(2)}) collective-permute-start(f32[4,128]{1,0:T(4,128)S(1)} %get-tuple-element.79), channel_id=1, source_target_pairs={{32,64},{96,128},{160,192},{224,256},{288,320},{352,384},{416,448}... | collective-permute-start | bytes 6152 | tf_op jit(solution)/shard_map/ppermute | solution.py:550
  84.1 3.1 %collective-permute-start.13 = (f32[4,128]{1,0:T(4,128)S(1)}, f32[4,128]{1,0:T(4,128)S(1)}, u32[]{:S(2)}, u32[]{:S(2)}) collective-permute-start(f32[4,128]{1,0:T(4,128)S(1)} %get-tuple-element.80), channel_id=1, source_target_pairs={{0,32},{64,96},{128,160},{192,224},{256,288},{320,352},{384,416},{... | collective-permute-start | bytes 6152 | tf_op jit(solution)/shard_map/ppermute | solution.py:563
  87.7 12.8 %collective-permute-start.14 = (f32[4,128]{1,0:T(4,128)S(1)}, f32[4,128]{1,0:T(4,128)S(1)}, u32[]{:S(2)}, u32[]{:S(2)}) collective-permute-start(f32[4,128]{1,0:T(4,128)S(1)} %get-tuple-element.83), channel_id=1, source_target_pairs={{1,2},{3,4},{5,6},{7,8},{9,10},{11,12},{13,14},{15,16},{17,18},{19... | collective-permute-start | bytes 6152 | tf_op jit(solution)/shard_map/ppermute | solution.py:560
  92.6 7.8 %collective-permute-start.15 = (f32[4,128]{1,0:T(4,128)S(1)}, f32[4,128]{1,0:T(4,128)S(1)}, u32[]{:S(2)}, u32[]{:S(2)}) collective-permute-start(f32[4,128]{1,0:T(4,128)S(1)} %get-tuple-element.84), channel_id=1, source_target_pairs={{0,1},{2,3},{4,5},{6,7},{8,9},{10,11},{12,13},{14,15},{16,17},{18,... | collective-permute-start | bytes 6152 | tf_op jit(solution)/shard_map/ppermute | solution.py:561
  94.6 5.9 %collective-permute-start.16 = (f32[4,128]{1,0:T(4,128)S(1)}, f32[4,128]{1,0:T(4,128)S(1)}, u32[]{:S(2)}, u32[]{:S(2)}) collective-permute-start(f32[4,128]{1,0:T(4,128)S(1)} %get-tuple-element.85), channel_id=1, source_target_pairs={{32,64},{96,128},{160,192},{224,256},{288,320},{352,384},{416,448}... | collective-permute-start | bytes 6152 | tf_op jit(solution)/shard_map/ppermute | solution.py:550
  98.0 3.1 %collective-permute-start.17 = (f32[4,128]{1,0:T(4,128)S(1)}, f32[4,128]{1,0:T(4,128)S(1)}, u32[]{:S(2)}, u32[]{:S(2)}) collective-permute-start(f32[4,128]{1,0:T(4,128)S(1)} %get-tuple-element.86), channel_id=1, source_target_pairs={{0,32},{64,96},{128,160},{192,224},{256,288},{320,352},{384,416},{... | collective-permute-start | bytes 6152 | tf_op jit(solution)/shard_map/ppermute | solution.py:563
  101.7 5.4 %collective-permute-start.18 = (f32[4,128]{1,0:T(4,128)S(1)}, f32[4,128]{1,0:T(4,128)S(1)}, u32[]{:S(2)}, u32[]{:S(2)}) collective-permute-start(f32[4,128]{1,0:T(4,128)S(1)} %get-tuple-element.89), channel_id=1, source_target_pairs={{32,64},{96,128},{160,192},{224,256},{288,320},{352,384},{416,448}... | collective-permute-start | bytes 6152 | tf_op jit(solution)/shard_map/ppermute | solution.py:550
  126.9 5.3 %collective-permute-start.19 = (f32[6,4,128]{2,1,0:T(4,128)S(1)}, f32[6,4,128]{2,1,0:T(4,128)S(1)}, u32[]{:S(2)}, u32[]{:S(2)}) collective-permute-start(f32[6,4,128]{2,1,0:T(4,128)S(1)} %all-gather.4), channel_id=1, source_target_pairs={{32,64},{96,128},{160,192},{224,256},{288,320},{352,384},{416,448}... | collective-permute-start | bytes 36872 | tf_op jit(solution)/shard_map/ppermute | solution.py:550

commit v8 on v7

--- a/solution.py
+++ b/solution.py
@@ -333,6 +333,7 @@
 
 
 def restrict_kernel(known, a0, a1, a2, a3, ohi_ref, oht_ref, ohh_ref, pack_ref, local_ref, right_ref, beside_ref, *refs):
+    refs = refs if known else refs[1:]
     far_ref, core_ref, row_ref, extra_ref = refs[:4]
     even_lat, even_lon = parities()
     if known:
@@ -632,7 +633,7 @@
         far, core, row, extra, *found = call(
             functools.partial(restrict_kernel, known),
             MESSAGES[:2] + [shape(3, 4, BS), FIELD] + ([] if known else [shape(2, 4, BS)]),
-            (*arrived, ohi, oht, ohh, pack, stiff, source, sides if known else ninv),
+            (*arrived, ohi, oht, ohh, pack, stiff, source) + ((sides,) if known else (ninv, ends)),
             "restrict",
         )
         if not known:

time: 164 us -> 164 us (level)
  no operation moved by 1% of the time
where the time goes in v8:
time: 164 us; the launch traced here: 163 us
  blocking collectives  72.6 us (44%)
  starting transfers between devices  70.3 us (43%)
  Pallas kernels  10.9 us (7%)
  waiting for transfers between devices  4.31 us (3%)
  local copies, waits for them, and re-layouts  3.44 us (2%)
    all_to_all x4, blocking collectives, everywhere(): return lax.all_to_all(row, axis, 0, 0)  56.4 us
    ppermute x8, starting transfers between devices, swap_far(): return lax.ppermute(message, 'lat', swap(lat_pairs(1)))  34.2 us
    ppermute x4, starting transfers between devices, exchange(): lax.ppermute(messages[0], 'lon', swap([(k, (k + 1) % lon) for k in range(...  20.3 us
    all_gather x6, blocking collectives, on_chip(): return lax.all_gather(message, 'lat', axis_index_groups=lat_pairs(0))  16.2 us
    pallas_call x19, Pallas kernels, call(): pl.pallas_call(body, out_shape=outs, in_specs=specs, out_specs=[pl.BlockS...  10.9 us
    ppermute x4, starting transfers between devices, exchange(): lax.ppermute(messages[1], 'lon', swap([(k, k + 1) for k in range(0, lon,...  8.09 us
    ppermute x4, starting transfers between devices, exchange(): lax.ppermute(messages[3], 'lat', swap(lat_pairs(0)))  7.68 us
    unnamed x8, local copies, waits for them, and re-layouts  3.42 us
  transfers between devices with their start and end apart: 20, of which 5 were waited for; matrix products, arithmetic and copies ran while one was open for 0% of the time, Pallas kernels for 2%

profile of v8, /device:TPU:1, one launch (start us, length us, event | category | flops | bytes accessed | tf_op | source)
XLA Modules:
  0.0 162.6 jit_solution(4803816942945733623)
XLA Ops:
  5.2 8.1 %collective-permute-start = (f32[12,128]{1,0:T(8,128)S(1)}, f32[12,128]{1,0:T(8,128)S(1)}, u32[]{:S(2)}, u32[]{:S(2)}) collective-permute-start(f32[12,128]{1,0:T(8,128)S(1)} %get-tuple-element.51), channel_id=1, source_target_pairs={{1,2},{3,4},{5,6},{7,8},{9,10},{11,12},{13,14},{15,16},{17,18},{19... | collective-permute-start | bytes 18440 | tf_op jit(solution)/shard_map/ppermute | solution.py:561
  13.4 1.9 %collective-permute-start.1 = (f32[12,128]{1,0:T(8,128)S(1)}, f32[12,128]{1,0:T(8,128)S(1)}, u32[]{:S(2)}, u32[]{:S(2)}) collective-permute-start(f32[12,128]{1,0:T(8,128)S(1)} %get-tuple-element.52), channel_id=1, source_target_pairs={{0,1},{2,3},{4,5},{6,7},{8,9},{10,11},{12,13},{14,15},{16,17},{18,... | collective-permute-start | bytes 18440 | tf_op jit(solution)/shard_map/ppermute | solution.py:562
  15.3 4.8 %collective-permute-start.2 = (f32[12,128]{1,0:T(8,128)S(1)}, f32[12,128]{1,0:T(8,128)S(1)}, u32[]{:S(2)}, u32[]{:S(2)}) collective-permute-start(f32[12,128]{1,0:T(8,128)S(1)} %get-tuple-element.53), channel_id=1, source_target_pairs={{32,64},{96,128},{160,192},{224,256},{288,320},{352,384},{416,448}... | collective-permute-start | bytes 18440 | tf_op jit(solution)/shard_map/ppermute | solution.py:551
  20.2 1.9 %collective-permute-start.3 = (f32[12,128]{1,0:T(8,128)S(1)}, f32[12,128]{1,0:T(8,128)S(1)}, u32[]{:S(2)}, u32[]{:S(2)}) collective-permute-start(f32[12,128]{1,0:T(8,128)S(1)} %get-tuple-element.54), channel_id=1, source_target_pairs={{0,32},{64,96},{128,160},{192,224},{256,288},{320,352},{384,416},{... | collective-permute-start | bytes 18440 | tf_op jit(solution)/shard_map/ppermute | solution.py:564
  24.9 4.3 %collective-permute-start.4 = (f32[8,128]{1,0:T(8,128)S(1)}, f32[8,128]{1,0:T(8,128)S(1)}, u32[]{:S(2)}, u32[]{:S(2)}) collective-permute-start(f32[8,128]{1,0:T(8,128)S(1)} %get-tuple-element.61), channel_id=1, source_target_pairs={{1,2},{3,4},{5,6},{7,8},{9,10},{11,12},{13,14},{15,16},{17,18},{19... | collective-permute-start | bytes 12296 | tf_op jit(solution)/shard_map/ppermute | solution.py:561
  29.3 1.9 %collective-permute-start.5 = (f32[8,128]{1,0:T(8,128)S(1)}, f32[8,128]{1,0:T(8,128)S(1)}, u32[]{:S(2)}, u32[]{:S(2)}) collective-permute-start(f32[8,128]{1,0:T(8,128)S(1)} %get-tuple-element.62), channel_id=1, source_target_pairs={{0,1},{2,3},{4,5},{6,7},{8,9},{10,11},{12,13},{14,15},{16,17},{18,... | collective-permute-start | bytes 12296 | tf_op jit(solution)/shard_map/ppermute | solution.py:562
  31.2 4.7 %collective-permute-start.6 = (f32[4,128]{1,0:T(4,128)S(1)}, f32[4,128]{1,0:T(4,128)S(1)}, u32[]{:S(2)}, u32[]{:S(2)}) collective-permute-start(f32[4,128]{1,0:T(4,128)S(1)} %get-tuple-element.63), channel_id=1, source_target_pairs={{32,64},{96,128},{160,192},{224,256},{288,320},{352,384},{416,448}... | collective-permute-start | bytes 6152 | tf_op jit(solution)/shard_map/ppermute | solution.py:551
  35.9 1.9 %collective-permute-start.7 = (f32[4,128]{1,0:T(4,128)S(1)}, f32[4,128]{1,0:T(4,128)S(1)}, u32[]{:S(2)}, u32[]{:S(2)}) collective-permute-start(f32[4,128]{1,0:T(4,128)S(1)} %get-tuple-element.64), channel_id=1, source_target_pairs={{0,32},{64,96},{128,160},{192,224},{256,288},{320,352},{384,416},{... | collective-permute-start | bytes 6152 | tf_op jit(solution)/shard_map/ppermute | solution.py:564
  39.6 4.1 %collective-permute-start.8 = (f32[4,128]{1,0:T(4,128)S(1)}, f32[4,128]{1,0:T(4,128)S(1)}, u32[]{:S(2)}, u32[]{:S(2)}) collective-permute-start(f32[4,128]{1,0:T(4,128)S(1)} %get-tuple-element.70), channel_id=1, source_target_pairs={{32,64},{96,128},{160,192},{224,256},{288,320},{352,384},{416,448}... | collective-permute-start | bytes 6152 | tf_op jit(solution)/shard_map/ppermute | solution.py:551
  45.5 14.7 %all_to_all.20.row_ref = f32[32,3,4,128]{3,2,1,0:T(4,128)S(1)} all-to-all(f32[32,3,4,128]{3,2,1,0:T(4,128)S(1)} %row.2), channel_id=1, replica_groups=mesh['lat'=16,'lon'=32] {'lon'}, dimensions={0} | all-to-all | bytes 393216 | tf_op jit(solution)/shard_map/all_to_all | solution.py:569
  60.2 4.5 %all-gather.1 = f32[6,4,128]{2,1,0:T(4,128)S(1)} all-gather(f32[3,4,128]{2,1,0:T(4,128)S(1)} %get-tuple-element.73), channel_id=3, replica_groups={{0,32},{64,96},{128,160},{192,224},{256,288},{320,352},{384,416},{448,4..., dimensions={0}, use_global_device_ids=true | all-gather | bytes 18432 | tf_op jit(solution)/shard_map/all_gather | solution.py:555
  64.7 5.4 %collective-permute-start.9 = (f32[6,4,128]{2,1,0:T(4,128)S(1)}, f32[6,4,128]{2,1,0:T(4,128)S(1)}, u32[]{:S(2)}, u32[]{:S(2)}) collective-permute-start(f32[6,4,128]{2,1,0:T(4,128)S(1)} %all-gather.1), channel_id=1, source_target_pairs={{32,64},{96,128},{160,192},{224,256},{288,320},{352,384},{416,448}... | collective-permute-start | bytes 36872 | tf_op jit(solution)/shard_map/ppermute | solution.py:551
  74.6 2.9 %collective-permute-start.10 = (f32[4,128]{1,0:T(4,128)S(1)}, f32[4,128]{1,0:T(4,128)S(1)}, u32[]{:S(2)}, u32[]{:S(2)}) collective-permute-start(f32[4,128]{1,0:T(4,128)S(1)} %get-tuple-element.77), channel_id=1, source_target_pairs={{1,2},{3,4},{5,6},{7,8},{9,10},{11,12},{13,14},{15,16},{17,18},{19... | collective-permute-start | bytes 6152 | tf_op jit(solution)/shard_map/ppermute | solution.py:561
  77.5 2.3 %collective-permute-start.11 = (f32[4,128]{1,0:T(4,128)S(1)}, f32[4,128]{1,0:T(4,128)S(1)}, u32[]{:S(2)}, u32[]{:S(2)}) collective-permute-start(f32[4,128]{1,0:T(4,128)S(1)} %get-tuple-element.78), channel_id=1, source_target_pairs={{0,1},{2,3},{4,5},{6,7},{8,9},{10,11},{12,13},{14,15},{16,17},{18,... | collective-permute-start | bytes 6152 | tf_op jit(solution)/shard_map/ppermute | solution.py:562
  79.9 4.2 %collective-permute-start.12 = (f32[4,128]{1,0:T(4,128)S(1)}, f32[4,128]{1,0:T(4,128)S(1)}, u32[]{:S(2)}, u32[]{:S(2)}) collective-permute-start(f32[4,128]{1,0:T(4,128)S(1)} %get-tuple-element.79), channel_id=1, source_target_pairs={{32,64},{96,128},{160,192},{224,256},{288,320},{352,384},{416,448}... | collective-permute-start | bytes 6152 | tf_op jit(solution)/shard_map/ppermute | solution.py:551
  84.1 1.9 %collective-permute-start.13 = (f32[4,128]{1,0:T(4,128)S(1)}, f32[4,128]{1,0:T(4,128)S(1)}, u32[]{:S(2)}, u32[]{:S(2)}) collective-permute-start(f32[4,128]{1,0:T(4,128)S(1)} %get-tuple-element.80), channel_id=1, source_target_pairs={{0,32},{64,96},{128,160},{192,224},{256,288},{320,352},{384,416},{... | collective-permute-start | bytes 6152 | tf_op jit(solution)/shard_map/ppermute | solution.py:564
  87.7 5.0 %collective-permute-start.14 = (f32[4,128]{1,0:T(4,128)S(1)}, f32[4,128]{1,0:T(4,128)S(1)}, u32[]{:S(2)}, u32[]{:S(2)}) collective-permute-start(f32[4,128]{1,0:T(4,128)S(1)} %get-tuple-element.83), channel_id=1, source_target_pairs={{1,2},{3,4},{5,6},{7,8},{9,10},{11,12},{13,14},{15,16},{17,18},{19... | collective-permute-start | bytes 6152 | tf_op jit(solution)/shard_map/ppermute | solution.py:561
  94.6 3.4 %collective-permute-start.16 = (f32[4,128]{1,0:T(4,128)S(1)}, f32[4,128]{1,0:T(4,128)S(1)}, u32[]{:S(2)}, u32[]{:S(2)}) collective-permute-start(f32[4,128]{1,0:T(4,128)S(1)} %get-tuple-element.85), channel_id=1, source_target_pairs={{32,64},{96,128},{160,192},{224,256},{288,320},{352,384},{416,448}... | collective-permute-start | bytes 6152 | tf_op jit(solution)/shard_map/ppermute | solution.py:551
  101.7 3.6 %collective-permute-start.18 = (f32[4,128]{1,0:T(4,128)S(1)}, f32[4,128]{1,0:T(4,128)S(1)}, u32[]{:S(2)}, u32[]{:S(2)}) collective-permute-start(f32[4,128]{1,0:T(4,128)S(1)} %get-tuple-element.89), channel_id=1, source_target_pairs={{32,64},{96,128},{160,192},{224,256},{288,320},{352,384},{416,448}... | collective-permute-start | bytes 6152 | tf_op jit(solution)/shard_map/ppermute | solution.py:551
  107.2 15.2 %all_to_all.21.row_ref = f32[32,3,4,128]{3,2,1,0:T(4,128)S(1)} all-to-all(f32[32,3,4,128]{3,2,1,0:T(4,128)S(1)} %row.3), channel_id=1, replica_groups=mesh['lat'=16,'lon'=32] {'lon'}, dimensions={0} | all-to-all | bytes 393216 | tf_op jit(solution)/shard_map/all_to_all | solution.py:569
  122.4 4.5 %all-gather.4 = f32[6,4,128]{2,1,0:T(4,128)S(1)} all-gather(f32[3,4,128]{2,1,0:T(4,128)S(1)} %get-tuple-element.92), channel_id=6, replica_groups={{0,32},{64,96},{128,160},{192,224},{256,288},{320,352},{384,416},{448,4..., dimensions={0}, use_global_device_ids=true | all-gather | bytes 18432 | tf_op jit(solution)/shard_map/all_gather | solution.py:555
  126.9 3.9 %collective-permute-start.19 = (f32[6,4,128]{2,1,0:T(4,128)S(1)}, f32[6,4,128]{2,1,0:T(4,128)S(1)}, u32[]{:S(2)}, u32[]{:S(2)}) collective-permute-start(f32[6,4,128]{2,1,0:T(4,128)S(1)} %all-gather.4), channel_id=1, source_target_pairs={{32,64},{96,128},{160,192},{224,256},{288,320},{352,384},{416,448}... | collective-permute-start | bytes 36872 | tf_op jit(solution)/shard_map/ppermute | solution.py:551
  135.2 14.2 %all_to_all.22 = f32[16,1,128]{2,1,0:T(1,128)S(1)} all-to-all(f32[16,1,128]{2,1,0:T(1,128)S(1)} %get-tuple-element.95), channel_id=1, replica_groups=mesh['lat'=16,'lon'=32] {'lat'}, dimensions={0} | all-to-all | bytes 16384 | tf_op jit(solution)/shard_map/all_to_all | solution.py:569
  149.4 12.3 %all_to_all.23.sums_ref = f32[32,1,128]{2,1,0:T(1,128)S(1)} all-to-all(f32[32,1,128]{2,1,0:T(1,128)S(1)} %broadcast_in_dim.2), channel_id=1, replica_groups=mesh['lat'=16,'lon'=32] {'lon'}, dimensions={0} | all-to-all | bytes 32768 | tf_op jit(solution)/shard_map/all_to_all | solution.py:569
  (55 shorter events, 29.7 us)
Async XLA Ops:
  2.1 0.8 copy-start
  2.9 1.2 copy-start.2
  5.2 18.9 %collective-permute-start = (f32[12,128]{1,0:T(8,128)S(1)}, f32[12,128]{1,0:T(8,128)S(1)}, u32[]{:S(2)}, u32[]{:S(2)}) collective-permute-start(f32[12,128]{1,0:T(8,128)S(1)} %get-tuple-element.51), channel_id=1, source_target_pairs={{1,2},{3,4},{5,6},{7,8},{9,10},{11,12},{13,14},{15,16},{17,18},{19... | collective-permute-start | bytes 18440 | tf_op jit(solution)/shard_map/ppermute | solution.py:561
  13.4 10.8 %collective-permute-start.1 = (f32[12,128]{1,0:T(8,128)S(1)}, f32[12,128]{1,0:T(8,128)S(1)}, u32[]{:S(2)}, u32[]{:S(2)}) collective-permute-start(f32[12,128]{1,0:T(8,128)S(1)} %get-tuple-element.52), channel_id=1, source_target_pairs={{0,1},{2,3},{4,5},{6,7},{8,9},{10,11},{12,13},{14,15},{16,17},{18,... | collective-permute-start | bytes 18440 | tf_op jit(solution)/shard_map/ppermute | solution.py:562
  15.3 8.9 %collective-permute-start.2 = (f32[12,128]{1,0:T(8,128)S(1)}, f32[12,128]{1,0:T(8,128)S(1)}, u32[]{:S(2)}, u32[]{:S(2)}) collective-permute-start(f32[12,128]{1,0:T(8,128)S(1)} %get-tuple-element.53), channel_id=1, source_target_pairs={{32,64},{96,128},{160,192},{224,256},{288,320},{352,384},{416,448}... | collective-permute-start | bytes 18440 | tf_op jit(solution)/shard_map/ppermute | solution.py:551
  20.2 4.1 %collective-permute-start.3 = (f32[12,128]{1,0:T(8,128)S(1)}, f32[12,128]{1,0:T(8,128)S(1)}, u32[]{:S(2)}, u32[]{:S(2)}) collective-permute-start(f32[12,128]{1,0:T(8,128)S(1)} %get-tuple-element.54), channel_id=1, source_target_pairs={{0,32},{64,96},{128,160},{192,224},{256,288},{320,352},{384,416},{... | collective-permute-start | bytes 18440 | tf_op jit(solution)/shard_map/ppermute | solution.py:564
  22.1 1.2 copy-start.3
  23.6 0.8 copy-start.1
  24.9 14.0 %collective-permute-start.4 = (f32[8,128]{1,0:T(8,128)S(1)}, f32[8,128]{1,0:T(8,128)S(1)}, u32[]{:S(2)}, u32[]{:S(2)}) collective-permute-start(f32[8,128]{1,0:T(8,128)S(1)} %get-tuple-element.61), channel_id=1, source_target_pairs={{1,2},{3,4},{5,6},{7,8},{9,10},{11,12},{13,14},{15,16},{17,18},{19... | collective-permute-start | bytes 12296 | tf_op jit(solution)/shard_map/ppermute | solution.py:561
  29.3 9.7 %collective-permute-start.5 = (f32[8,128]{1,0:T(8,128)S(1)}, f32[8,128]{1,0:T(8,128)S(1)}, u32[]{:S(2)}, u32[]{:S(2)}) collective-permute-start(f32[8,128]{1,0:T(8,128)S(1)} %get-tuple-element.62), channel_id=1, source_target_pairs={{0,1},{2,3},{4,5},{6,7},{8,9},{10,11},{12,13},{14,15},{16,17},{18,... | collective-permute-start | bytes 12296 | tf_op jit(solution)/shard_map/ppermute | solution.py:562
  31.2 7.3 %collective-permute-start.6 = (f32[4,128]{1,0:T(4,128)S(1)}, f32[4,128]{1,0:T(4,128)S(1)}, u32[]{:S(2)}, u32[]{:S(2)}) collective-permute-start(f32[4,128]{1,0:T(4,128)S(1)} %get-tuple-element.63), channel_id=1, source_target_pairs={{32,64},{96,128},{160,192},{224,256},{288,320},{352,384},{416,448}... | collective-permute-start | bytes 6152 | tf_op jit(solution)/shard_map/ppermute | solution.py:551
  35.9 3.1 %collective-permute-start.7 = (f32[4,128]{1,0:T(4,128)S(1)}, f32[4,128]{1,0:T(4,128)S(1)}, u32[]{:S(2)}, u32[]{:S(2)}) collective-permute-start(f32[4,128]{1,0:T(4,128)S(1)} %get-tuple-element.64), channel_id=1, source_target_pairs={{0,32},{64,96},{128,160},{192,224},{256,288},{320,352},{384,416},{... | collective-permute-start | bytes 6152 | tf_op jit(solution)/shard_map/ppermute | solution.py:564
  39.6 5.9 %collective-permute-start.8 = (f32[4,128]{1,0:T(4,128)S(1)}, f32[4,128]{1,0:T(4,128)S(1)}, u32[]{:S(2)}, u32[]{:S(2)}) collective-permute-start(f32[4,128]{1,0:T(4,128)S(1)} %get-tuple-element.70), channel_id=1, source_target_pairs={{32,64},{96,128},{160,192},{224,256},{288,320},{352,384},{416,448}... | collective-permute-start | bytes 6152 | tf_op jit(solution)/shard_map/ppermute | solution.py:551
  64.7 6.8 %collective-permute-start.9 = (f32[6,4,128]{2,1,0:T(4,128)S(1)}, f32[6,4,128]{2,1,0:T(4,128)S(1)}, u32[]{:S(2)}, u32[]{:S(2)}) collective-permute-start(f32[6,4,128]{2,1,0:T(4,128)S(1)} %all-gather.1), channel_id=1, source_target_pairs={{32,64},{96,128},{160,192},{224,256},{288,320},{352,384},{416,448}... | collective-permute-start | bytes 36872 | tf_op jit(solution)/shard_map/ppermute | solution.py:551
  74.6 12.0 %collective-permute-start.10 = (f32[4,128]{1,0:T(4,128)S(1)}, f32[4,128]{1,0:T(4,128)S(1)}, u32[]{:S(2)}, u32[]{:S(2)}) collective-permute-start(f32[4,128]{1,0:T(4,128)S(1)} %get-tuple-element.77), channel_id=1, source_target_pairs={{1,2},{3,4},{5,6},{7,8},{9,10},{11,12},{13,14},{15,16},{17,18},{19... | collective-permute-start | bytes 6152 | tf_op jit(solution)/shard_map/ppermute | solution.py:561
  77.5 9.0 %collective-permute-start.11 = (f32[4,128]{1,0:T(4,128)S(1)}, f32[4,128]{1,0:T(4,128)S(1)}, u32[]{:S(2)}, u32[]{:S(2)}) collective-permute-start(f32[4,128]{1,0:T(4,128)S(1)} %get-tuple-element.78), channel_id=1, source_target_pairs={{0,1},{2,3},{4,5},{6,7},{8,9},{10,11},{12,13},{14,15},{16,17},{18,... | collective-permute-start | bytes 6152 | tf_op jit(solution)/shard_map/ppermute | solution.py:562
  79.9 6.7 %collective-permute-start.12 = (f32[4,128]{1,0:T(4,128)S(1)}, f32[4,128]{1,0:T(4,128)S(1)}, u32[]{:S(2)}, u32[]{:S(2)}) collective-permute-start(f32[4,128]{1,0:T(4,128)S(1)} %get-tuple-element.79), channel_id=1, source_target_pairs={{32,64},{96,128},{160,192},{224,256},{288,320},{352,384},{416,448}... | collective-permute-start | bytes 6152 | tf_op jit(solution)/shard_map/ppermute | solution.py:551
  84.1 3.1 %collective-permute-start.13 = (f32[4,128]{1,0:T(4,128)S(1)}, f32[4,128]{1,0:T(4,128)S(1)}, u32[]{:S(2)}, u32[]{:S(2)}) collective-permute-start(f32[4,128]{1,0:T(4,128)S(1)} %get-tuple-element.80), channel_id=1, source_target_pairs={{0,32},{64,96},{128,160},{192,224},{256,288},{320,352},{384,416},{... | collective-permute-start | bytes 6152 | tf_op jit(solution)/shard_map/ppermute | solution.py:564
  87.7 12.8 %collective-permute-start.14 = (f32[4,128]{1,0:T(4,128)S(1)}, f32[4,128]{1,0:T(4,128)S(1)}, u32[]{:S(2)}, u32[]{:S(2)}) collective-permute-start(f32[4,128]{1,0:T(4,128)S(1)} %get-tuple-element.83), channel_id=1, source_target_pairs={{1,2},{3,4},{5,6},{7,8},{9,10},{11,12},{13,14},{15,16},{17,18},{19... | collective-permute-start | bytes 6152 | tf_op jit(solution)/shard_map/ppermute | solution.py:561
  92.6 7.9 %collective-permute-start.15 = (f32[4,128]{1,0:T(4,128)S(1)}, f32[4,128]{1,0:T(4,128)S(1)}, u32[]{:S(2)}, u32[]{:S(2)}) collective-permute-start(f32[4,128]{1,0:T(4,128)S(1)} %get-tuple-element.84), channel_id=1, source_target_pairs={{0,1},{2,3},{4,5},{6,7},{8,9},{10,11},{12,13},{14,15},{16,17},{18,... | collective-permute-start | bytes 6152 | tf_op jit(solution)/shard_map/ppermute | solution.py:562
  94.6 5.9 %collective-permute-start.16 = (f32[4,128]{1,0:T(4,128)S(1)}, f32[4,128]{1,0:T(4,128)S(1)}, u32[]{:S(2)}, u32[]{:S(2)}) collective-permute-start(f32[4,128]{1,0:T(4,128)S(1)} %get-tuple-element.85), channel_id=1, source_target_pairs={{32,64},{96,128},{160,192},{224,256},{288,320},{352,384},{416,448}... | collective-permute-start | bytes 6152 | tf_op jit(solution)/shard_map/ppermute | solution.py:551
  98.0 3.1 %collective-permute-start.17 = (f32[4,128]{1,0:T(4,128)S(1)}, f32[4,128]{1,0:T(4,128)S(1)}, u32[]{:S(2)}, u32[]{:S(2)}) collective-permute-start(f32[4,128]{1,0:T(4,128)S(1)} %get-tuple-element.86), channel_id=1, source_target_pairs={{0,32},{64,96},{128,160},{192,224},{256,288},{320,352},{384,416},{... | collective-permute-start | bytes 6152 | tf_op jit(solution)/shard_map/ppermute | solution.py:564
  101.7 5.4 %collective-permute-start.18 = (f32[4,128]{1,0:T(4,128)S(1)}, f32[4,128]{1,0:T(4,128)S(1)}, u32[]{:S(2)}, u32[]{:S(2)}) collective-permute-start(f32[4,128]{1,0:T(4,128)S(1)} %get-tuple-element.89), channel_id=1, source_target_pairs={{32,64},{96,128},{160,192},{224,256},{288,320},{352,384},{416,448}... | collective-permute-start | bytes 6152 | tf_op jit(solution)/shard_map/ppermute | solution.py:551
  126.9 5.3 %collective-permute-start.19 = (f32[6,4,128]{2,1,0:T(4,128)S(1)}, f32[6,4,128]{2,1,0:T(4,128)S(1)}, u32[]{:S(2)}, u32[]{:S(2)}) collective-permute-start(f32[6,4,128]{2,1,0:T(4,128)S(1)} %all-gather.4), channel_id=1, source_target_pairs={{32,64},{96,128},{160,192},{224,256},{288,320},{352,384},{416,448}... | collective-permute-start | bytes 36872 | tf_op jit(solution)/shard_map/ppermute | solution.py:551
